TPU v7x, 32 devices: a whole 2x2x4 slice. The times are simulated.
32 devices in a mesh: rows: 8 (over y, x, core), depth: 4 (over z).
Axes of the slice: x: 2, y: 2, z: 4, core: 2. Of those that a mesh axis runs over, the one named last changes fastest.
Arguments:
- field: float32 [64, 64, 1024], P('rows', 'depth'), may hold values from 0 to 1
- diffusivity: bfloat16 [64, 64, 1024], P('rows', 'depth'), may hold values from 0.019897461 to 0.119628906
- velocity: bfloat16 [3, 64, 64, 1024], P(None, 'rows', 'depth'), may hold values from -1 to 1
Outputs:
- front: float32 [64, 64, 1024], P('rows', 'depth')
- picture: float32 [4, 64, 1024], P(None, 'rows', 'depth')
All inputs are finite; a program needn't handle non-finite values.
Results may differ from a plain program's by a relative error of at most 0.0003.
Values sent between devices are 32-bit elements; how exact they have to be, the bound alone decides.
No kernel may reach another device: no remote copies, remote signals or barrier semaphores. Data moves between devices by JAX's collectives and lax.ppermute only.
A program may use at most 64 MiB of HBM per device.

v0:
```python
import jax
import jax.numpy as jnp
from jax import lax
from jax.sharding import PartitionSpec as P

time_step = 0.2
growth_rate = 1.0
opacity_total = 3.0


def extended_2(block, sides, width):
    for axis, dim in sides:
        count = lax.axis_size(axis)
        forward = [(i, i + 1) for i in range(count - 1)]
        backward = [(target, source) for source, target in forward]
        low = lax.ppermute(
            lax.slice_in_dim(block, block.shape[dim] - width, None, axis=dim), axis, forward
        )
        high = lax.ppermute(lax.slice_in_dim(block, 0, width, axis=dim), axis, backward)
        block = jnp.concatenate([low, block, high], axis=dim)
    return block


def swapped(value, axis, apart):
    return lax.ppermute(value, axis, [(i, i ^ 1 << apart) for i in range(lax.axis_size(axis))])


def upwind(speed, center, behind, ahead):
    return jnp.maximum(speed, 0.0) * (center - behind) + jnp.minimum(speed, 0.0) * (ahead - center)


def evolve(extended, diffusivity, velocity):
    padded = jnp.pad(extended, ((0, 0), (0, 0), (1, 1)))
    center = padded[1:-1, 1:-1, 1:-1]
    row_after = padded[2:, 1:-1, 1:-1]
    row_before = padded[:-2, 1:-1, 1:-1]
    deep_after = padded[1:-1, 2:, 1:-1]
    deep_before = padded[1:-1, :-2, 1:-1]
    col_after = padded[1:-1, 1:-1, 2:]
    col_before = padded[1:-1, 1:-1, :-2]
    laplace = (
        row_after + row_before + deep_after + deep_before + col_after + col_before - 6.0 * center
    )
    transport = upwind(velocity[0], center, row_before, row_after)
    transport = transport + upwind(velocity[1], center, deep_before, deep_after)
    transport = transport + upwind(velocity[2], center, col_before, col_after)
    return center + time_step * (
        diffusivity * laplace - transport + growth_rate * center * (1.0 - center)
    )


def render(extended, opacity):
    padded = jnp.pad(extended, ((0, 0), (0, 0), (1, 1)))
    center = padded[1:-1, 1:-1, 1:-1]
    grad_row = (padded[2:, 1:-1, 1:-1] - padded[:-2, 1:-1, 1:-1]) * 0.5
    grad_deep = (padded[1:-1, 2:, 1:-1] - padded[1:-1, :-2, 1:-1]) * 0.5
    grad_col = (padded[1:-1, 1:-1, 2:] - padded[1:-1, 1:-1, :-2]) * 0.5
    lighting = 0.48 * grad_row + 0.64 * grad_deep + 0.6 * grad_col
    magnitude = grad_row * grad_row + grad_deep * grad_deep + grad_col * grad_col + 0.1
    shade = 0.35 + 0.65 * lighting * lighting / magnitude
    optical = opacity * center
    through = jnp.cumsum(optical, axis=1)
    weight = jnp.exp(optical - through) * (1.0 - jnp.exp(-optical)) * shade
    red = jnp.sum(weight * center, axis=1)
    green = jnp.sum(weight * center * center, axis=1)
    blue = jnp.sum(weight * (1.0 - center), axis=1)
    remain = jnp.exp(-through[:, -1])
    return jnp.stack([red, green, blue, remain])


def over(nearer, farther):
    return jnp.concatenate(
        [nearer[:3] + nearer[3:] * farther[:3], nearer[3:] * farther[3:]], axis=0
    )


def shards(field, diffusivity, velocity):
    coef_diff = diffusivity.astype(jnp.float32)
    coef_vel = velocity.astype(jnp.float32)

    def advance(current):
        extended = extended_2(current, (("rows", 0), ("depth", 1)), 1)
        return evolve(extended, coef_diff, coef_vel)

    front = advance(advance(field))
    outlined = extended_2(front, (("rows", 0), ("depth", 1)), 1)
    groups = lax.axis_size("depth")
    depth_total = front.shape[1] * groups
    segment = render(outlined, opacity_total / depth_total)
    row_count = front.shape[0]
    col_width = front.shape[2] // groups
    levels = groups.bit_length() - 1
    position = lax.axis_index("depth")
    partial_value = segment.reshape((4, row_count) + (2,) * levels + (col_width,))
    for bit_index in range(levels):
        split_axis = 2 + (levels - 1 - bit_index)
        my_bit = position // 2**bit_index % 2
        keep_half = lax.dynamic_index_in_dim(partial_value, my_bit, split_axis, keepdims=False)
        give_half = lax.dynamic_index_in_dim(partial_value, 1 - my_bit, split_axis, keepdims=False)
        got_half = swapped(give_half, "depth", bit_index)
        nearer = jnp.where(my_bit == 0, keep_half, got_half)
        farther = jnp.where(my_bit == 0, got_half, keep_half)
        partial_value = over(nearer, farther)
    return (front, partial_value)


def solution(mesh):
    return jax.shard_map(
        shards,
        mesh=mesh,
        in_specs=(
            P("rows", "depth", None),
            P("rows", "depth", None),
            P(None, "rows", "depth", None),
        ),
        out_specs=(P("rows", "depth", None), P(None, "rows", "depth")),
        check_vma=False,
    )
```

profile of v0, /device:TPU:4, one launch (start us, length us, event | category | flops | bytes accessed | tf_op | source)
XLA Modules:
  0.0 73.9 jit_solution(15302056917452210463)
XLA Ops:
  1.7 2.8 %collective-permute-start = (f32[1,16,1024]{2,0,1:T(1,128)S(1)}, f32[1,16,1024]{2,0,1:T(1,128)S(1)}, u32[]{:S(2)}, u32[]{:S(2)}) collective-permute-start(f32[1,16,1024]{2,0,1:T(1,128)S(1)} %copy.24), channel_id=1, source_target_pairs={{4,0},{8,4},{12,8},{16,12},{20,16},{24,20},{28,24},{5,1},{9,5},{13... | collective-permute-start | bytes 196616 | tf_op jit(solution)/shard_map/ppermute | solution.py:19
  4.5 1.9 %collective-permute-start.1 = (f32[1,16,1024]{2,0,1:T(1,128)S(1)}, f32[1,16,1024]{2,0,1:T(1,128)S(1)}, u32[]{:S(2)}, u32[]{:S(2)}) collective-permute-start(f32[1,16,1024]{2,0,1:T(1,128)S(1)} %copy.26), channel_id=1, source_target_pairs={{0,4},{4,8},{8,12},{12,16},{16,20},{20,24},{24,28},{1,5},{5,9},{9,... | collective-permute-start | bytes 196616 | tf_op jit(solution)/shard_map/ppermute | solution.py:16
  6.5 1.4 %copy.39 = f32[8,16,1024]{2,0,1:T(8,128)S(1)} copy(f32[8,16,1024]{2,1,0:T(8,128)} %param.3) | data formatting | bytes 1048576 | tf_op args[0]
  7.8 3.2 %collective-permute-done.1 = f32[1,16,1024]{2,0,1:T(1,128)S(1)} collective-permute-done((f32[1,16,1024]{2,0,1:T(1,128)S(1)}, f32[1,16,1024]{2,0,1:T(1,128)S(1)}, u32[]{:S(2)}, u32[]{:S(2)}) %collective-permute-start.1) | collective-permute-done | bytes 65568 | tf_op jit(solution)/shard_map/ppermute | solution.py:16
  11.1 1.3 %collective-permute-start.2 = (f32[10,1,1024]{2,0,1:T(8,128)S(1)}, f32[10,1,1024]{2,0,1:T(8,128)S(1)}, u32[]{:S(2)}, u32[]{:S(2)}) collective-permute-start(f32[10,1,1024]{2,0,1:T(8,128)S(1)} %get-tuple-element.14), channel_id=1, source_target_pairs={{1,0},{2,1},{3,2},{5,4},{6,5},{7,6},{9,8},{10,9},{11,10},{13,12},{... | collective-permute-start | bytes 122888 | tf_op jit(solution)/shard_map/ppermute | solution.py:19
  12.4 4.5 %collective-permute-start.3 = (f32[10,1,1024]{2,0,1:T(8,128)S(1)}, f32[10,1,1024]{2,0,1:T(8,128)S(1)}, u32[]{:S(2)}, u32[]{:S(2)}) collective-permute-start(f32[10,1,1024]{2,0,1:T(8,128)S(1)} %get-tuple-element.13), channel_id=1, source_target_pairs={{0,1},{1,2},{2,3},{4,5},{5,6},{6,7},{8,9},{9,10},{10,11},{12,13},{... | collective-permute-start | bytes 122888 | tf_op jit(solution)/shard_map/ppermute | solution.py:16
  17.4 1.4 %collective-permute-done.3 = f32[10,1,1024]{2,0,1:T(8,128)S(1)} collective-permute-done((f32[10,1,1024]{2,0,1:T(8,128)S(1)}, f32[10,1,1024]{2,0,1:T(8,128)S(1)}, u32[]{:S(2)}, u32[]{:S(2)}) %collective-permute-start.3) | collective-permute-done | bytes 40992 | tf_op jit(solution)/shard_map/ppermute | solution.py:16
  20.7 1.9 %collective-permute-start.4 = (f32[1,16,1024]{2,0,1:T(1,128)S(1)}, f32[1,16,1024]{2,0,1:T(1,128)S(1)}, u32[]{:S(2)}, u32[]{:S(2)}) collective-permute-start(f32[1,16,1024]{2,0,1:T(1,128)S(1)} %get-tuple-element.17), channel_id=1, source_target_pairs={{4,0},{8,4},{12,8},{16,12},{20,16},{24,20},{28,24},{5,1},{9,5},{13... | collective-permute-start | bytes 196616 | tf_op jit(solution)/shard_map/ppermute | solution.py:19
  22.6 2.4 %collective-permute-start.5 = (f32[1,16,1024]{2,0,1:T(1,128)S(1)}, f32[1,16,1024]{2,0,1:T(1,128)S(1)}, u32[]{:S(2)}, u32[]{:S(2)}) collective-permute-start(f32[1,16,1024]{2,0,1:T(1,128)S(1)} %get-tuple-element.18), channel_id=1, source_target_pairs={{0,4},{4,8},{8,12},{12,16},{16,20},{20,24},{24,28},{1,5},{5,9},{9,... | collective-permute-start | bytes 196616 | tf_op jit(solution)/shard_map/ppermute | solution.py:16
  25.0 4.1 %collective-permute-done.5 = f32[1,16,1024]{2,0,1:T(1,128)S(1)} collective-permute-done((f32[1,16,1024]{2,0,1:T(1,128)S(1)}, f32[1,16,1024]{2,0,1:T(1,128)S(1)}, u32[]{:S(2)}, u32[]{:S(2)}) %collective-permute-start.5) | collective-permute-done | bytes 65568 | tf_op jit(solution)/shard_map/ppermute | solution.py:16
  29.1 1.3 %collective-permute-start.6 = (f32[10,1,1024]{2,0,1:T(8,128)S(1)}, f32[10,1,1024]{2,0,1:T(8,128)S(1)}, u32[]{:S(2)}, u32[]{:S(2)}) collective-permute-start(f32[10,1,1024]{2,0,1:T(8,128)S(1)} %get-tuple-element.12), channel_id=1, source_target_pairs={{1,0},{2,1},{3,2},{5,4},{6,5},{7,6},{9,8},{10,9},{11,10},{13,12},{... | collective-permute-start | bytes 122888 | tf_op jit(solution)/shard_map/ppermute | solution.py:19
  30.4 4.9 %collective-permute-start.7 = (f32[10,1,1024]{2,0,1:T(8,128)S(1)}, f32[10,1,1024]{2,0,1:T(8,128)S(1)}, u32[]{:S(2)}, u32[]{:S(2)}) collective-permute-start(f32[10,1,1024]{2,0,1:T(8,128)S(1)} %get-tuple-element.11), channel_id=1, source_target_pairs={{0,1},{1,2},{2,3},{4,5},{5,6},{6,7},{8,9},{9,10},{10,11},{12,13},{... | collective-permute-start | bytes 122888 | tf_op jit(solution)/shard_map/ppermute | solution.py:16
  35.6 1.6 %collective-permute-done.7 = f32[10,1,1024]{2,0,1:T(8,128)S(1)} collective-permute-done((f32[10,1,1024]{2,0,1:T(8,128)S(1)}, f32[10,1,1024]{2,0,1:T(8,128)S(1)}, u32[]{:S(2)}, u32[]{:S(2)}) %collective-permute-start.7) | collective-permute-done | bytes 40992 | tf_op jit(solution)/shard_map/ppermute | solution.py:16
  39.1 1.9 %collective-permute-start.8 = (f32[1,16,1024]{2,0,1:T(1,128)S(1)}, f32[1,16,1024]{2,0,1:T(1,128)S(1)}, u32[]{:S(2)}, u32[]{:S(2)}) collective-permute-start(f32[1,16,1024]{2,0,1:T(1,128)S(1)} %get-tuple-element.16), channel_id=1, source_target_pairs={{4,0},{8,4},{12,8},{16,12},{20,16},{24,20},{28,24},{5,1},{9,5},{13... | collective-permute-start | bytes 196616 | tf_op jit(solution)/shard_map/ppermute | solution.py:19
  41.0 2.4 %collective-permute-start.9 = (f32[1,16,1024]{2,0,1:T(1,128)S(1)}, f32[1,16,1024]{2,0,1:T(1,128)S(1)}, u32[]{:S(2)}, u32[]{:S(2)}) collective-permute-start(f32[1,16,1024]{2,0,1:T(1,128)S(1)} %get-tuple-element.15), channel_id=1, source_target_pairs={{0,4},{4,8},{8,12},{12,16},{16,20},{20,24},{24,28},{1,5},{5,9},{9,... | collective-permute-start | bytes 196616 | tf_op jit(solution)/shard_map/ppermute | solution.py:16
  43.4 4.1 %collective-permute-done.9 = f32[1,16,1024]{2,0,1:T(1,128)S(1)} collective-permute-done((f32[1,16,1024]{2,0,1:T(1,128)S(1)}, f32[1,16,1024]{2,0,1:T(1,128)S(1)}, u32[]{:S(2)}, u32[]{:S(2)}) %collective-permute-start.9) | collective-permute-done | bytes 65568 | tf_op jit(solution)/shard_map/ppermute | solution.py:16
  47.5 1.3 %collective-permute-start.10 = (f32[10,1,1024]{2,0,1:T(8,128)S(1)}, f32[10,1,1024]{2,0,1:T(8,128)S(1)}, u32[]{:S(2)}, u32[]{:S(2)}) collective-permute-start(f32[10,1,1024]{2,0,1:T(8,128)S(1)} %get-tuple-element.10), channel_id=1, source_target_pairs={{1,0},{2,1},{3,2},{5,4},{6,5},{7,6},{9,8},{10,9},{11,10},{13,12},{... | collective-permute-start | bytes 122888 | tf_op jit(solution)/shard_map/ppermute | solution.py:19
  48.8 4.9 %collective-permute-start.11 = (f32[10,1,1024]{2,0,1:T(8,128)S(1)}, f32[10,1,1024]{2,0,1:T(8,128)S(1)}, u32[]{:S(2)}, u32[]{:S(2)}) collective-permute-start(f32[10,1,1024]{2,0,1:T(8,128)S(1)} %get-tuple-element.9), channel_id=1, source_target_pairs={{0,1},{1,2},{2,3},{4,5},{5,6},{6,7},{8,9},{9,10},{10,11},{12,13},{... | collective-permute-start | bytes 122888 | tf_op jit(solution)/shard_map/ppermute | solution.py:16
  54.0 1.6 %collective-permute-done.11 = f32[10,1,1024]{2,0,1:T(8,128)S(1)} collective-permute-done((f32[10,1,1024]{2,0,1:T(8,128)S(1)}, f32[10,1,1024]{2,0,1:T(8,128)S(1)}, u32[]{:S(2)}, u32[]{:S(2)}) %collective-permute-start.11) | collective-permute-done | bytes 40992 | tf_op jit(solution)/shard_map/ppermute | solution.py:16
  56.3 6.6 %multiply_reduce_fusion.2 = (f32[8,1024]{1,0:T(8,128)S(1)}, f32[8,1024]{1,0:T(8,128)S(1)}, f32[8,1024]{1,0:T(8,128)S(1)}, f32[8,16,1024]{2,0,1:T(8,128)S(1)}) fusion(f32[8,16,1024]{2,0,1:T(8,128)S(1)} %fusion.8, f32[10,18,1026]{2,0,1:T(8,128)S(1)} %select_maximum_fusion, f32[1,16,1024]{2,0,1:T(1,128)S(1)} %collective-permute-done.8, ...), kind=kOutput, calls=%fused_computation.107 | output fusion | flops 7577600 | bytes 2981888 | tf_op jit(solution)/shard_map/jit(cumsum)/reduce_window_sum | solution.py:62
  63.0 2.4 %collective-permute-start.12 = (f32[4,8,2,256]{3,1,2,0:T(8,128)S(1)}, f32[4,8,2,256]{3,1,2,0:T(8,128)S(1)}, u32[]{:S(2)}, u32[]{:S(2)}) collective-permute-start(f32[4,8,2,256]{3,1,2,0:T(8,128)S(1)} %dynamic-slice_bitcast_fusion), channel_id=1, source_target_pairs={{0,1},{1,0},{2,3},{3,2},{4,5},{5,4},{6,7},{7,6},{8,9},{9,8},{10,11... | collective-permute-start | bytes 196616 | tf_op jit(solution)/shard_map/ppermute | solution.py:25
  65.5 2.6 %collective-permute-done.12 = f32[4,8,2,256]{3,1,2,0:T(8,128)S(1)} collective-permute-done((f32[4,8,2,256]{3,1,2,0:T(8,128)S(1)}, f32[4,8,2,256]{3,1,2,0:T(8,128)S(1)}, u32[]{:S(2)}, u32[]{:S(2)}) %collective-permute-start.12) | collective-permute-done | bytes 65568 | tf_op jit(solution)/shard_map/ppermute | solution.py:25
  68.1 3.2 %collective-permute-start.13 = (f32[4,8,256]{2,1,0:T(8,128)S(1)}, f32[4,8,256]{2,1,0:T(8,128)S(1)}, u32[]{:S(2)}, u32[]{:S(2)}) collective-permute-start(f32[4,8,256]{2,1,0:T(8,128)S(1)} %fusion.49), channel_id=1, source_target_pairs={{0,2},{1,3},{2,0},{3,1},{4,6},{5,7},{6,4},{7,5},{8,10},{9,11},{10,... | collective-permute-start | bytes 98312 | tf_op jit(solution)/shard_map/ppermute | solution.py:25
  71.3 1.1 %copy.40 = f32[8,16,1024]{2,1,0:T(8,128)} copy(f32[8,16,1024]{2,0,1:T(8,128)S(1)} %fusion.8) | data formatting | bytes 1048576
  (36 shorter events, 8.2 us)
Async XLA Ops:
  0.6 16.3 %copy-start.1 = (bf16[3,8,16,1024]{3,2,1,0:T(8,128)(2,1)S(1)}, bf16[3,8,16,1024]{3,2,1,0:T(8,128)(2,1)}, u32[]{:S(2)}) copy-start(bf16[3,8,16,1024]{3,2,1,0:T(8,128)(2,1)} %param.5) | copy-start | bytes 2359300
  1.7 6.2 %collective-permute-start = (f32[1,16,1024]{2,0,1:T(1,128)S(1)}, f32[1,16,1024]{2,0,1:T(1,128)S(1)}, u32[]{:S(2)}, u32[]{:S(2)}) collective-permute-start(f32[1,16,1024]{2,0,1:T(1,128)S(1)} %copy.24), channel_id=1, source_target_pairs={{4,0},{8,4},{12,8},{16,12},{20,16},{24,20},{28,24},{5,1},{9,5},{13... | collective-permute-start | bytes 196616 | tf_op jit(solution)/shard_map/ppermute | solution.py:19
  4.5 6.5 %collective-permute-start.1 = (f32[1,16,1024]{2,0,1:T(1,128)S(1)}, f32[1,16,1024]{2,0,1:T(1,128)S(1)}, u32[]{:S(2)}, u32[]{:S(2)}) collective-permute-start(f32[1,16,1024]{2,0,1:T(1,128)S(1)} %copy.26), channel_id=1, source_target_pairs={{0,4},{4,8},{8,12},{12,16},{16,20},{20,24},{24,28},{1,5},{5,9},{9,... | collective-permute-start | bytes 196616 | tf_op jit(solution)/shard_map/ppermute | solution.py:16
  11.1 6.4 %collective-permute-start.2 = (f32[10,1,1024]{2,0,1:T(8,128)S(1)}, f32[10,1,1024]{2,0,1:T(8,128)S(1)}, u32[]{:S(2)}, u32[]{:S(2)}) collective-permute-start(f32[10,1,1024]{2,0,1:T(8,128)S(1)} %get-tuple-element.14), channel_id=1, source_target_pairs={{1,0},{2,1},{3,2},{5,4},{6,5},{7,6},{9,8},{10,9},{11,10},{13,12},{... | collective-permute-start | bytes 122888 | tf_op jit(solution)/shard_map/ppermute | solution.py:19
  12.4 6.4 %collective-permute-start.3 = (f32[10,1,1024]{2,0,1:T(8,128)S(1)}, f32[10,1,1024]{2,0,1:T(8,128)S(1)}, u32[]{:S(2)}, u32[]{:S(2)}) collective-permute-start(f32[10,1,1024]{2,0,1:T(8,128)S(1)} %get-tuple-element.13), channel_id=1, source_target_pairs={{0,1},{1,2},{2,3},{4,5},{5,6},{6,7},{8,9},{9,10},{10,11},{12,13},{... | collective-permute-start | bytes 122888 | tf_op jit(solution)/shard_map/ppermute | solution.py:16
  17.4 2.1 %copy-start = (bf16[8,16,1024]{2,1,0:T(8,128)(2,1)S(1)}, bf16[8,16,1024]{2,1,0:T(8,128)(2,1)}, u32[]{:S(2)}) copy-start(bf16[8,16,1024]{2,1,0:T(8,128)(2,1)} %param.4) | copy-start | bytes 786436
  20.7 4.3 %collective-permute-start.4 = (f32[1,16,1024]{2,0,1:T(1,128)S(1)}, f32[1,16,1024]{2,0,1:T(1,128)S(1)}, u32[]{:S(2)}, u32[]{:S(2)}) collective-permute-start(f32[1,16,1024]{2,0,1:T(1,128)S(1)} %get-tuple-element.17), channel_id=1, source_target_pairs={{4,0},{8,4},{12,8},{16,12},{20,16},{24,20},{28,24},{5,1},{9,5},{13... | collective-permute-start | bytes 196616 | tf_op jit(solution)/shard_map/ppermute | solution.py:19
  22.6 6.5 %collective-permute-start.5 = (f32[1,16,1024]{2,0,1:T(1,128)S(1)}, f32[1,16,1024]{2,0,1:T(1,128)S(1)}, u32[]{:S(2)}, u32[]{:S(2)}) collective-permute-start(f32[1,16,1024]{2,0,1:T(1,128)S(1)} %get-tuple-element.18), channel_id=1, source_target_pairs={{0,4},{4,8},{8,12},{12,16},{16,20},{20,24},{24,28},{1,5},{5,9},{9,... | collective-permute-start | bytes 196616 | tf_op jit(solution)/shard_map/ppermute | solution.py:16
  29.1 6.5 %collective-permute-start.6 = (f32[10,1,1024]{2,0,1:T(8,128)S(1)}, f32[10,1,1024]{2,0,1:T(8,128)S(1)}, u32[]{:S(2)}, u32[]{:S(2)}) collective-permute-start(f32[10,1,1024]{2,0,1:T(8,128)S(1)} %get-tuple-element.12), channel_id=1, source_target_pairs={{1,0},{2,1},{3,2},{5,4},{6,5},{7,6},{9,8},{10,9},{11,10},{13,12},{... | collective-permute-start | bytes 122888 | tf_op jit(solution)/shard_map/ppermute | solution.py:19
  30.4 6.8 %collective-permute-start.7 = (f32[10,1,1024]{2,0,1:T(8,128)S(1)}, f32[10,1,1024]{2,0,1:T(8,128)S(1)}, u32[]{:S(2)}, u32[]{:S(2)}) collective-permute-start(f32[10,1,1024]{2,0,1:T(8,128)S(1)} %get-tuple-element.11), channel_id=1, source_target_pairs={{0,1},{1,2},{2,3},{4,5},{5,6},{6,7},{8,9},{9,10},{10,11},{12,13},{... | collective-permute-start | bytes 122888 | tf_op jit(solution)/shard_map/ppermute | solution.py:16
  39.1 4.3 %collective-permute-start.8 = (f32[1,16,1024]{2,0,1:T(1,128)S(1)}, f32[1,16,1024]{2,0,1:T(1,128)S(1)}, u32[]{:S(2)}, u32[]{:S(2)}) collective-permute-start(f32[1,16,1024]{2,0,1:T(1,128)S(1)} %get-tuple-element.16), channel_id=1, source_target_pairs={{4,0},{8,4},{12,8},{16,12},{20,16},{24,20},{28,24},{5,1},{9,5},{13... | collective-permute-start | bytes 196616 | tf_op jit(solution)/shard_map/ppermute | solution.py:19
  41.0 6.5 %collective-permute-start.9 = (f32[1,16,1024]{2,0,1:T(1,128)S(1)}, f32[1,16,1024]{2,0,1:T(1,128)S(1)}, u32[]{:S(2)}, u32[]{:S(2)}) collective-permute-start(f32[1,16,1024]{2,0,1:T(1,128)S(1)} %get-tuple-element.15), channel_id=1, source_target_pairs={{0,4},{4,8},{8,12},{12,16},{16,20},{20,24},{24,28},{1,5},{5,9},{9,... | collective-permute-start | bytes 196616 | tf_op jit(solution)/shard_map/ppermute | solution.py:16
  47.5 6.5 %collective-permute-start.10 = (f32[10,1,1024]{2,0,1:T(8,128)S(1)}, f32[10,1,1024]{2,0,1:T(8,128)S(1)}, u32[]{:S(2)}, u32[]{:S(2)}) collective-permute-start(f32[10,1,1024]{2,0,1:T(8,128)S(1)} %get-tuple-element.10), channel_id=1, source_target_pairs={{1,0},{2,1},{3,2},{5,4},{6,5},{7,6},{9,8},{10,9},{11,10},{13,12},{... | collective-permute-start | bytes 122888 | tf_op jit(solution)/shard_map/ppermute | solution.py:19
  48.8 6.8 %collective-permute-start.11 = (f32[10,1,1024]{2,0,1:T(8,128)S(1)}, f32[10,1,1024]{2,0,1:T(8,128)S(1)}, u32[]{:S(2)}, u32[]{:S(2)}) collective-permute-start(f32[10,1,1024]{2,0,1:T(8,128)S(1)} %get-tuple-element.9), channel_id=1, source_target_pairs={{0,1},{1,2},{2,3},{4,5},{5,6},{6,7},{8,9},{9,10},{10,11},{12,13},{... | collective-permute-start | bytes 122888 | tf_op jit(solution)/shard_map/ppermute | solution.py:16
  63.0 5.0 %collective-permute-start.12 = (f32[4,8,2,256]{3,1,2,0:T(8,128)S(1)}, f32[4,8,2,256]{3,1,2,0:T(8,128)S(1)}, u32[]{:S(2)}, u32[]{:S(2)}) collective-permute-start(f32[4,8,2,256]{3,1,2,0:T(8,128)S(1)} %dynamic-slice_bitcast_fusion), channel_id=1, source_target_pairs={{0,1},{1,0},{2,3},{3,2},{4,5},{5,4},{6,7},{7,6},{8,9},{9,8},{10,11... | collective-permute-start | bytes 196616 | tf_op jit(solution)/shard_map/ppermute | solution.py:25
  68.1 5.1 %collective-permute-start.13 = (f32[4,8,256]{2,1,0:T(8,128)S(1)}, f32[4,8,256]{2,1,0:T(8,128)S(1)}, u32[]{:S(2)}, u32[]{:S(2)}) collective-permute-start(f32[4,8,256]{2,1,0:T(8,128)S(1)} %fusion.49), channel_id=1, source_target_pairs={{0,2},{1,3},{2,0},{3,1},{4,6},{5,7},{6,4},{7,5},{8,10},{9,11},{10,... | collective-permute-start | bytes 98312 | tf_op jit(solution)/shard_map/ppermute | solution.py:25
where the time goes:
time: 75.1 us; the launch traced here: 73.9 us
  starting transfers between devices  37.2 us (50%)
  waiting for transfers between devices  19.8 us (26%)
  other arithmetic  12.2 us (16%)
  local copies, waits for them, and re-layouts  3.73 us (5%)
  between operations  0.96 us (1%)
    ppermute x6, starting transfers between devices, extended_2(): lax.ppermute(lax.slice_in_dim(block, block.shape[dim] - width, None, axis...  21.1 us
    ppermute x6, waiting for transfers between devices, extended_2(): lax.ppermute(lax.slice_in_dim(block, block.shape[dim] - width, None, axis...  15.9 us
    ppermute x6, starting transfers between devices, extended_2(): lax.ppermute(lax.slice_in_dim(block, 0, width, axis=dim), axis, backward)  10.5 us
    another operation x1, other arithmetic, render(): through = jnp.cumsum(optical, axis=1)  6.65 us
    ppermute x2, starting transfers between devices, swapped(): lax.ppermute(value, axis, [(i, i ^ 1 << apart) for i in range(lax.axis_si...  5.61 us
    ppermute x2, waiting for transfers between devices, swapped(): lax.ppermute(value, axis, [(i, i ^ 1 << apart) for i in range(lax.axis_si...  3.39 us
    unnamed x6, local copies, waits for them, and re-layouts  2.46 us
    concatenate x6, other arithmetic, extended_2(): block = jnp.concatenate([low, block, high], axis=dim)  2.24 us
  transfers between devices with their start and end apart: 14, of which 10 were waited for; matrix products, arithmetic and copies ran while one was open for 4% of the time, Pallas kernels for 0%

commit v1 on v0

v1 whole, which is shorter than its diff:
```python
import jax
import jax.numpy as jnp
from jax import lax
from jax.experimental import pallas as pl
from jax.experimental.pallas import tpu as pltpu
from jax.sharding import PartitionSpec as P

time_step = 0.2
growth_rate = 1.0
opacity_total = 3.0

lanes = 128
margin = 8


def pairs(count, first):
    forward = [(i, i + 1) for i in range(first, count - 1, 2)]
    return forward + [(target, source) for source, target in forward]


def swap_pairs(value, axis, first):
    return lax.ppermute(value, axis, pairs(lax.axis_size(axis), first))


def stencil(u, low, high, coef):
    diff = coef[0]
    change = growth_rate * u * (1.0 - u)
    for before, after, speed in zip(low, high, coef[1:]):
        change = change + (diff + jnp.maximum(speed, 0.0)) * (before - u)
        change = change + (diff - jnp.minimum(speed, 0.0)) * (after - u)
    return u + time_step * change


def beside(chunks):
    lane = lax.broadcasted_iota(jnp.int32, chunks[0].shape, 1)
    right = [pltpu.roll(x, 1, 1) for x in chunks]
    left = [pltpu.roll(x, lanes - 1, 1) for x in chunks]
    zero = jnp.zeros_like(chunks[0])
    count = len(chunks)
    before = [jnp.where(lane == 0, right[c - 1] if c else zero, right[c]) for c in range(count)]
    after = [
        jnp.where(lane == lanes - 1, left[c + 1] if c + 1 < count else zero, left[c])
        for c in range(count)
    ]
    return before, after


def cols(c):
    return slice(c * lanes, (c + 1) * lanes)


def pack_kernel(field, diff, vel, even_d, odd_d, even_r, odd_r, flat, coefs):
    rows, depth, width = field.shape
    count = width // lanes
    depth_odd = lax.axis_index("depth") % 2 == 1
    rows_odd = lax.axis_index("rows") % 2 == 1

    def coef_row(r, c):
        return [diff[r, :, cols(c)].astype(jnp.float32)] + [
            vel[i, r, :, cols(c)].astype(jnp.float32) for i in range(3)
        ]

    for c in range(count):
        for r in range(rows):
            place = pl.ds(r * depth, depth)
            flat[c, place, :] = field[r, :, cols(c)]
            for i, value in enumerate(coef_row(r, c)):
                coefs[i, c, place, :] = value
        first = [field[0, :, cols(c)], field[1, :, cols(c)]] + coef_row(0, c)
        last = [field[rows - 1, :, cols(c)], field[rows - 2, :, cols(c)]] + coef_row(rows - 1, c)
        for i in range(6):
            even_r[i, :, cols(c)] = jnp.where(rows_odd, first[i], last[i])
            odd_r[i, :, cols(c)] = jnp.where(rows_odd, last[i], first[i])

    row = lax.broadcasted_iota(jnp.int32, (rows, lanes), 0)
    sides = []
    for near, step in ((0, 1), (depth - 1, -1)):

        def slab(ref, d):
            return [ref[c, pl.ds(d, rows, stride=depth), :] for c in range(count)]

        u0, u1, u2 = (slab(flat, near + step * j) for j in range(3))
        near_coef = [slab(coefs.at[i], near) for i in range(4)]
        next_coef = [slab(coefs.at[i], near + step) for i in range(4)]
        before, after = beside(u1)
        side = []
        for c in range(count):
            above = jnp.where(row == 0, 0.0, pltpu.roll(u1[c], 1, 0))
            below = jnp.where(row == rows - 1, 0.0, pltpu.roll(u1[c], rows - 1, 0))
            deep = (u0[c], u2[c]) if step > 0 else (u2[c], u0[c])
            coef = [next_coef[i][c] for i in range(4)]
            middle = stencil(
                u1[c], (above, deep[0], before[c]), (below, deep[1], after[c]), coef
            )
            outer = jnp.where(row == 0, jnp.maximum(coef[1], 0.0), -jnp.minimum(coef[1], 0.0))
            weight = time_step * (coef[0] + outer)
            side.append([u0[c], u1[c]] + [near_coef[i][c] for i in range(4)] + [middle, weight])
        sides.append(side)
    low, high = sides
    for c in range(count):
        for i in range(8):
            even_d[i, :, cols(c)] = jnp.where(depth_odd, low[c][i], high[c][i])
            odd_d[i, :, cols(c)] = jnp.where(depth_odd, high[c][i], low[c][i])


def arrived(even, odd, is_odd, index):
    a, b = even[index], odd[index]
    return jnp.where(is_odd, a, b), jnp.where(is_odd, b, a)


def corner_kernel(field, diff, vel, even_d, odd_d, even_2, odd_2, ext):
    rows, depth, width = field.shape
    count = width // lanes
    depth_odd = lax.axis_index("depth") % 2 == 1
    rows_odd = lax.axis_index("rows") % 2 == 1
    sides = []
    for edge, inner in ((0, 1), (rows - 1, rows - 2)):
        far = 2 * inner - edge
        u = [field[inner, :, cols(c)] for c in range(count)]
        before, after = beside(u)
        side = []
        for c in range(count):
            low, high = arrived(even_d, odd_d, depth_odd, (0, pl.ds(inner, 1), cols(c)))
            ext[c, margin - 1 : margin, :] = low
            ext[c, margin : margin + depth, :] = u[c]
            ext[c, margin + depth : margin + depth + 1, :] = high
            shallow = ext[c, pl.ds(margin - 1, depth), :]
            deep = ext[c, pl.ds(margin + 1, depth), :]
            outer, further = field[edge, :, cols(c)], field[far, :, cols(c)]
            above, below = (outer, further) if edge < inner else (further, outer)
            coef = [diff[inner, :, cols(c)].astype(jnp.float32)] + [
                vel[i, inner, :, cols(c)].astype(jnp.float32) for i in range(3)
            ]
            side.append(stencil(u[c], (above, shallow, before[c]), (below, deep, after[c]), coef))
        sides.append(side)
    first, last = sides
    for c in range(count):
        even_2[:depth, cols(c)] = jnp.where(rows_odd, first[c], last[c])
        odd_2[:depth, cols(c)] = jnp.where(rows_odd, last[c], first[c])
    for j, (item, second) in enumerate(
        ((0, False), (1, False), (0, True), (2, False), (3, False), (4, False), (5, False))
    ):
        at_first = 1 if second else 0
        at_last = rows - 1 - at_first
        for c in range(count):
            f_low, f_high = arrived(even_d, odd_d, depth_odd, (item, pl.ds(at_first, 1), cols(c)))
            l_low, l_high = arrived(even_d, odd_d, depth_odd, (item, pl.ds(at_last, 1), cols(c)))
            for k, f_val, l_val in ((0, f_low, l_low), (1, f_high, l_high)):
                place = depth + 8 * k + j
                even_2[place : place + 1, cols(c)] = jnp.where(rows_odd, f_val, l_val)
                odd_2[place : place + 1, cols(c)] = jnp.where(rows_odd, l_val, f_val)


def main_kernel(
    opacity, field, diff, vel, even_d, odd_d, even_r, odd_r, even_2, odd_2,
    front, partial, first, second, third, slabs,
):
    rows, depth, width = field.shape
    count = width // lanes
    pitch = depth + 2 * margin
    depth_odd = lax.axis_index("depth") % 2 == 1
    rows_odd = lax.axis_index("rows") % 2 == 1
    every = range(count)

    def at(r, d):
        return (r + 2) * pitch + margin + d

    def line(ref, r, d=0):
        return [ref[c, pl.ds(at(r, d), depth), :] for c in every]

    def slab(ref, r, d, length):
        return [ref[c, pl.ds(at(r, d), length, stride=pitch), :] for c in every]

    for c in every:
        for r in range(rows):
            first[c, pl.ds(at(r, 0), depth), :] = field[r, :, cols(c)]
        for j in range(2):
            low, high = arrived(even_r, odd_r, rows_odd, (j, slice(None), cols(c)))
            first[c, pl.ds(at(-1 - j, 0), depth), :] = low
            first[c, pl.ds(at(rows + j, 0), depth), :] = high
            low, high = arrived(even_d, odd_d, depth_odd, (j, slice(None), cols(c)))
            first[c, pl.ds(at(0, -1 - j), rows, stride=pitch), :] = low
            first[c, pl.ds(at(0, depth + j), rows, stride=pitch), :] = high
        for j, r, d in ((0, 1, 1), (1, 1, 2), (2, 2, 1)):
            for k, deep in ((0, -d), (1, depth - 1 + d)):
                place = depth + 8 * k + j
                low, high = arrived(even_2, odd_2, rows_odd, (slice(place, place + 1), cols(c)))
                first[c, pl.ds(at(-r, deep), 1), :] = low
                first[c, pl.ds(at(rows - 1 + r, deep), 1), :] = high
        for i in range(4):
            both = arrived(even_d, odd_d, depth_odd, (2 + i, slice(None), cols(c)))
            for k in range(2):
                slabs[k, i, c, 1 : rows + 1, :] = both[k]
                place = depth + 8 * k + 3 + i
                low, high = arrived(even_2, odd_2, rows_odd, (slice(place, place + 1), cols(c)))
                slabs[k, i, c, 0:1, :] = low
                slabs[k, i, c, rows + 1 : rows + 2, :] = high
        low, high = arrived(even_2, odd_2, rows_odd, (slice(0, depth), cols(c)))
        second[c, pl.ds(at(-2, 0), depth), :] = low
        second[c, pl.ds(at(rows + 1, 0), depth), :] = high

    row = lax.broadcasted_iota(jnp.int32, (rows, lanes), 0)
    for k, d in ((0, -2), (1, depth + 1)):
        above, below = slab(first, -1, d, rows), slab(first, 1, d, rows)
        for c in every:
            partly = arrived(even_d, odd_d, depth_odd, (6, slice(None), cols(c)))[k]
            weight = arrived(even_d, odd_d, depth_odd, (7, slice(None), cols(c)))[k]
            extra = jnp.where(row == 0, above[c], jnp.where(row == rows - 1, below[c], 0.0))
            second[c, pl.ds(at(0, d), rows, stride=pitch), :] = partly + weight * extra

    def section_line(source, r, coef):
        u = line(source, r)
        before, after = beside(u)
        low = (line(source, r - 1), line(source, r, -1), before)
        high = (line(source, r + 1), line(source, r, 1), after)
        return [
            stencil(u[c], [x[c] for x in low], [x[c] for x in high], coef(c)) for c in every
        ]

    def section_slab(source, r, d, length, coef):
        u = slab(source, r, d, length)
        before, after = beside(u)
        low = (slab(source, r - 1, d, length), slab(source, r, d - 1, length), before)
        high = (slab(source, r + 1, d, length), slab(source, r, d + 1, length), after)
        return [
            stencil(u[c], [x[c] for x in low], [x[c] for x in high], coef(c)) for c in every
        ]

    def own_coef(r):
        return lambda c: [diff[r, :, cols(c)].astype(jnp.float32)] + [
            vel[i, r, :, cols(c)].astype(jnp.float32) for i in range(3)
        ]

    def beyond_coef(k):
        return lambda c: [
            arrived(even_r, odd_r, rows_odd, (2 + i, slice(None), cols(c)))[k] for i in range(4)
        ]

    def slab_coef(k, start, length):
        return lambda c: [slabs[k, i, c, start : start + length, :] for i in range(4)]

    def own_middle(r, carry):
        for c, value in enumerate(section_line(first, r, own_coef(r))):
            second[c, pl.ds(at(r, 0), depth), :] = value
        return carry

    lax.fori_loop(0, rows, own_middle, 0)
    for k, r in ((0, -1), (1, rows)):
        for c, value in enumerate(section_line(first, r, beyond_coef(k))):
            second[c, pl.ds(at(r, 0), depth), :] = value
    for k, d in ((0, -1), (1, depth)):
        values = section_slab(first, -1, d, rows + 2, slab_coef(k, 0, rows + 2))
        for c, value in enumerate(values):
            second[c, pl.ds(at(-1, d), rows + 2, stride=pitch), :] = value

    def own_front(r, carry):
        for c, value in enumerate(section_line(second, r, own_coef(r))):
            third[c, pl.ds(at(r, 0), depth), :] = value
            front[r, :, cols(c)] = value
        return carry

    lax.fori_loop(0, rows, own_front, 0)
    for k, r in ((0, -1), (1, rows)):
        for c, value in enumerate(section_line(second, r, beyond_coef(k))):
            third[c, pl.ds(at(r, 0), depth), :] = value
    for k, d in ((0, -1), (1, depth)):
        values = section_slab(second, 0, d, rows, slab_coef(k, 1, rows))
        for c, value in enumerate(values):
            third[c, pl.ds(at(0, d), rows, stride=pitch), :] = value

    def shine(d, carry):
        center = slab(third, 0, d, rows)
        before, after = beside(center)
        above, below = slab(third, -1, d, rows), slab(third, 1, d, rows)
        shallow, deep = slab(third, 0, d - 1, rows), slab(third, 0, d + 1, rows)
        result = []
        for c in every:
            through, total, red, green = carry[c]
            u = center[c]
            grad_row = below[c] - above[c]
            grad_deep = deep[c] - shallow[c]
            grad_col = after[c] - before[c]
            lighting = 0.48 * grad_row + 0.64 * grad_deep + 0.6 * grad_col
            magnitude = grad_row * grad_row + grad_deep * grad_deep + grad_col * grad_col + 0.4
            shade = 0.35 + 0.65 * lighting * lighting / magnitude
            passed = jnp.exp(-opacity * u)
            weight = through * (1.0 - passed) * shade
            colored = weight * u
            result.append((through * passed, total + weight, red + colored, green + colored * u))
        return tuple(result)

    zero, one = jnp.zeros((rows, lanes), jnp.float32), jnp.ones((rows, lanes), jnp.float32)
    carry = tuple((one, zero, zero, zero) for _ in every)
    for d in range(depth):
        carry = shine(d, carry)
    for c, (through, total, red, green) in enumerate(carry):
        partial[0, :, cols(c)] = red
        partial[1, :, cols(c)] = green
        partial[2, :, cols(c)] = total - red
        partial[3, :, cols(c)] = through


def vmem(shape):
    return pltpu.VMEM(shape, jnp.float32)


def here(value):
    return pltpu.with_memory_space_constraint(value, pltpu.VMEM)


def shards(field, diffusivity, velocity):
    rows, depth, width = field.shape
    count = width // lanes
    pitch = depth + 2 * margin
    groups = lax.axis_size("depth")
    params = pltpu.CompilerParams(vmem_limit_bytes=24 * 2**20)

    even_d, odd_d, even_r, odd_r = pl.pallas_call(
        pack_kernel,
        out_shape=[vmem((8, rows, width))] * 2 + [vmem((6, depth, width))] * 2,
        scratch_shapes=[
            pltpu.VMEM((count, rows * depth, lanes), jnp.float32),
            pltpu.VMEM((4, count, rows * depth, lanes), jnp.float32),
        ],
        compiler_params=params,
        name="pack",
    )(field, diffusivity, velocity)
    even_d = here(swap_pairs(even_d, "depth", 0))
    odd_d = here(swap_pairs(odd_d, "depth", 1))
    even_r = here(swap_pairs(even_r, "rows", 0))
    odd_r = here(swap_pairs(odd_r, "rows", 1))
    own = (here(field), here(diffusivity), here(velocity))
    even_2, odd_2 = pl.pallas_call(
        corner_kernel,
        out_shape=[vmem((depth + 16, width))] * 2,
        scratch_shapes=[pltpu.VMEM((count, pitch, lanes), jnp.float32)],
        compiler_params=params,
        name="corner",
    )(*own, even_d, odd_d)
    even_2 = here(swap_pairs(even_2, "rows", 0))
    odd_2 = here(swap_pairs(odd_2, "rows", 1))
    opacity = opacity_total / (depth * groups)
    front, partial = pl.pallas_call(
        lambda *refs: main_kernel(opacity, *refs),
        out_shape=[jax.ShapeDtypeStruct(field.shape, jnp.float32), vmem((4, rows, width))],
        scratch_shapes=[pltpu.VMEM((count, (rows + 4) * pitch, lanes), jnp.float32)] * 3
        + [pltpu.VMEM((2, 4, count, rows + 8, lanes), jnp.float32)],
        compiler_params=params,
        name="main",
    )(*own, even_d, odd_d, even_r, odd_r, even_2, odd_2)

    position = lax.axis_index("depth")
    split = partial.reshape(4, rows, groups, width // groups)
    parts = []
    for apart in range(groups):
        part = lax.dynamic_index_in_dim(split, position ^ apart, 2, keepdims=False)
        if apart:
            part = lax.ppermute(part, "depth", [(i, i ^ apart) for i in range(groups)])
        parts.append(part)
    parts = jnp.stack(parts)
    picture = None
    for s in range(groups):
        segment = lax.dynamic_index_in_dim(parts, position ^ s, 0, keepdims=False)
        if picture is None:
            colors, through = segment[:3], segment[3:]
            picture = (colors, through)
        else:
            colors = colors + through * segment[:3]
            through = through * segment[3:]
    return front, jnp.concatenate([colors, through], axis=0)


def solution(mesh):
    return jax.shard_map(
        shards,
        mesh=mesh,
        in_specs=(
            P("rows", "depth", None),
            P("rows", "depth", None),
            P(None, "rows", "depth", None),
        ),
        out_specs=(P("rows", "depth", None), P(None, "rows", "depth")),
        check_vma=False,
    )
```

time: 75.1 us -> 40.4 us (0.54); the launches traced: 73.9 us -> 40.1 us
  starting transfers between devices: 37.2 us -> 16.2 us
  other arithmetic: 12.2 us -> 0.68 us
  waiting for transfers between devices: 19.8 us -> 12.1 us
  Pallas kernels: 0 us -> 7.17 us
    ppermute x14 -> x9, starting transfers between devices: 37.2 us -> 16.2 us  [the longest x6 9.29 us: swap_pairs(): return lax.ppermute(value, axis, pairs(lax.axis_size(axis), first))]
    ppermute x14 -> x9, waiting for transfers between devices: 19.8 us -> 12.1 us  [the longest x6 8.84 us: swap_pairs(): return lax.ppermute(value, axis, pairs(lax.axis_size(axis), first))]
    pallas_call x0 -> x3, Pallas kernels: none -> 7.17 us  [the longest x1 5.11 us: shards(): pl.pallas_call(lambda *refs: main_kernel(opacity, *refs), out_shape=[jax....]
    another operation x2 -> x1, other arithmetic: 6.66 us -> 0.01 us  [shards(): parts = jnp.stack(parts)]
    concatenate x7 -> x1, other arithmetic: 2.86 us -> 0.62 us  [shards(): return (front, jnp.concatenate([colors, through], axis=0))]
    add x4 -> x1, other arithmetic: 2.11 us -> 0.02 us  [shards(): colors = colors + through * segment[:3]]
    slice x5 -> x0, local copies, waits for them, and re-layouts: 1.26 us -> none  [the longest x3 1.11 us: extended_2(): lax.slice_in_dim(block, 0, width, axis=dim)]
    unnamed x6 -> x12, local copies, waits for them, and re-layouts: 2.46 us -> 3.14 us
  transfers between devices with their start and end apart: 14 -> 9, of which waited for: 10 -> 4; matrix products, arithmetic and copies ran while one was open for 4% -> 0% of each run, Pallas kernels for 0% -> 2%
where the time goes in v1:
time: 40.4 us; the launch traced here: 40.1 us
  starting transfers between devices  16.2 us (40%)
  waiting for transfers between devices  12.1 us (30%)
  Pallas kernels  7.17 us (18%)
  local copies, waits for them, and re-layouts  3.15 us (8%)
  between operations  0.78 us (2%)
  other arithmetic  0.68 us (2%)
    ppermute x6, starting transfers between devices, swap_pairs(): return lax.ppermute(value, axis, pairs(lax.axis_size(axis), first))  9.29 us
    ppermute x6, waiting for transfers between devices, swap_pairs(): return lax.ppermute(value, axis, pairs(lax.axis_size(axis), first))  8.84 us
    ppermute x3, starting transfers between devices, shards(): part = lax.ppermute(part, 'depth', [(i, i ^ apart) for i in range(groups)])  6.89 us
    pallas_call x1, Pallas kernels, shards(): pl.pallas_call(lambda *refs: main_kernel(opacity, *refs), out_shape=[jax....  5.11 us
    ppermute x3, waiting for transfers between devices, shards(): part = lax.ppermute(part, 'depth', [(i, i ^ apart) for i in range(groups)])  3.27 us
    unnamed x12, local copies, waits for them, and re-layouts  3.14 us
    pallas_call x1, Pallas kernels, shards(): pl.pallas_call(pack_kernel, out_shape=[vmem((8, rows, width))] * 2 + [vme...  1.09 us
    pallas_call x1, Pallas kernels, shards(): pl.pallas_call(corner_kernel, out_shape=[vmem((depth + 16, width))] * 2,...  0.97 us
  transfers between devices with their start and end apart: 9, of which 4 were waited for; matrix products, arithmetic and copies ran while one was open for 0% of the time, Pallas kernels for 2%

profile of v1, /device:TPU:4, one launch (start us, length us, event | category | flops | bytes accessed | tf_op | source)
XLA Modules:
  0.0 40.1 jit_solution(8138883265647015694)
XLA Ops:
  0.6 0.0 copy-start
  0.6 1.1 %copy-done = bf16[3,8,16,1024]{3,2,1,0:T(8,128)(2,1)S(1)} copy-done((bf16[3,8,16,1024]{3,2,1,0:T(8,128)(2,1)S(1)}, bf16[3,8,16,1024]{3,2,1,0:T(8,128)(2,1)}, u32[]{:S(2)}) %copy-start) | copy-done | bytes 786456
  1.8 1.0 %copy-done.2 = f32[8,16,1024]{2,1,0:T(8,128)S(1)} copy-done((f32[8,16,1024]{2,1,0:T(8,128)S(1)}, f32[8,16,1024]{2,1,0:T(8,128)}, u32[]{:S(2)}) %copy-start.2) | copy-done | bytes 524312
  2.8 0.9 %copy-done.4 = bf16[8,16,1024]{2,1,0:T(8,128)(2,1)S(1)} copy-done((bf16[8,16,1024]{2,1,0:T(8,128)(2,1)S(1)}, bf16[8,16,1024]{2,1,0:T(8,128)(2,1)}, u32[]{:S(2)}) %copy-start.4) | copy-done | bytes 262168
  3.8 1.1 %pack.1 = (f32[8,8,1024]{2,1,0:T(8,128)S(1)}, f32[8,8,1024]{2,1,0:T(8,128)S(1)}, f32[6,16,1024]{2,1,0:T(8,128)}, f32[6,16,1024]{2,1,0:T(8,128)S(1)}) custom-call(f32[8,16,1024]{2,1,0:T(8,128)S(1)} %copy-done.2, bf16[8,16,1024]{2,1,0:T(8,128)(2,1)S(1)} %copy-done.4, bf16[3,8,16,1024]{3,2,1,0:T(8,128)(2,1)S(1)} %copy-done), custom_call_target="tpu_custom_call" | custom-call | tf_op jit(solution)/shard_map/pack/pallas_call | solution.py:318
  4.8 1.6 %collective-permute-start = (f32[8,8,1024]{2,1,0:T(8,128)S(1)}, f32[8,8,1024]{2,1,0:T(8,128)S(1)}, u32[]{:S(2)}, u32[]{:S(2)}) collective-permute-start(f32[8,8,1024]{2,1,0:T(8,128)S(1)} %get-tuple-element.10), channel_id=1, source_target_pairs={{0,1},{2,3},{1,0},{3,2},{4,5},{6,7},{5,4},{7,6},{8,9},{10,11},{9,8... | collective-permute-start | bytes 786440 | tf_op jit(solution)/shard_map/ppermute | solution.py:22
  6.4 0.7 %collective-permute-start.1 = (f32[8,8,1024]{2,1,0:T(8,128)S(1)}, f32[8,8,1024]{2,1,0:T(8,128)S(1)}, u32[]{:S(2)}, u32[]{:S(2)}) collective-permute-start(f32[8,8,1024]{2,1,0:T(8,128)S(1)} %get-tuple-element.11), channel_id=1, source_target_pairs={{1,2},{2,1},{5,6},{6,5},{9,10},{10,9},{13,14},{14,13},{17,18},{18,... | collective-permute-start | bytes 786440 | tf_op jit(solution)/shard_map/ppermute | solution.py:22
  7.1 0.1 collective-permute-start.2
  7.2 0.0 copy-start.1
  7.2 0.0 copy-start.3
  7.2 0.0 copy-start.5
  7.2 3.5 %collective-permute-start.3 = (f32[6,16,1024]{2,1,0:T(8,128)S(1)}, f32[6,16,1024]{2,1,0:T(8,128)S(1)}, u32[]{:S(2)}, u32[]{:S(2)}) collective-permute-start(f32[6,16,1024]{2,1,0:T(8,128)S(1)} %get-tuple-element.13), channel_id=1, source_target_pairs={{4,8},{12,16},{20,24},{8,4},{16,12},{24,20},{5,9},{13,17},{21,25},... | collective-permute-start | bytes 1179656 | tf_op jit(solution)/shard_map/ppermute | solution.py:22
  10.8 2.1 %collective-permute-done.even_d.refs_3_ = f32[8,8,1024]{2,1,0:T(8,128)S(1)} collective-permute-done((f32[8,8,1024]{2,1,0:T(8,128)S(1)}, f32[8,8,1024]{2,1,0:T(8,128)S(1)}, u32[]{:S(2)}, u32[]{:S(2)}) %collective-permute-start) | collective-permute-done | bytes 262176 | tf_op jit(solution)/shard_map/ppermute | solution.py:22
  12.9 1.0 %corner.1 = (f32[32,1024]{1,0:T(8,128)}, f32[32,1024]{1,0:T(8,128)}) custom-call(f32[8,16,1024]{2,1,0:T(8,128)S(1)} %copy-done.2, bf16[8,16,1024]{2,1,0:T(8,128)(2,1)S(1)} %copy-done.4, bf16[3,8,16,1024]{3,2,1,0:T(8,128)(2,1)S(1)} %copy-done, f32[8,8,1024]{2,1,0:T(8,128)S(1)} %collective-permute-done.even_d.refs_3_, ...), custom_call_target="tpu_custom_call" | custom-call | tf_op jit(solution)/shard_map/corner/pallas_call | solution.py:333
  13.9 0.0 collective-permute-start.4
  13.9 3.4 %collective-permute-start.5 = (f32[32,1024]{1,0:T(8,128)}, f32[32,1024]{1,0:T(8,128)S(1)}, u32[]{:S(2)}, u32[]{:S(2)}) collective-permute-start(f32[32,1024]{1,0:T(8,128)} %get-tuple-element.15), channel_id=1, source_target_pairs={{4,8},{12,16},{20,24},{8,4},{16,12},{24,20},{5,9},{13,17},{21,25},... | collective-permute-start | bytes 393224 | tf_op jit(solution)/shard_map/ppermute | solution.py:22
  17.3 0.0 collective-permute-done.4.refs_7_
  17.4 6.7 %collective-permute-done.5.refs_8_ = f32[32,1024]{1,0:T(8,128)S(1)} collective-permute-done((f32[32,1024]{1,0:T(8,128)}, f32[32,1024]{1,0:T(8,128)S(1)}, u32[]{:S(2)}, u32[]{:S(2)}) %collective-permute-start.5) | collective-permute-done | bytes 131104 | tf_op jit(solution)/shard_map/ppermute | solution.py:22
  24.1 5.1 %main.1 = (f32[8,16,1024]{2,1,0:T(8,128)}, f32[4,8,1024]{2,1,0:T(8,128)S(1)}) custom-call(f32[8,16,1024]{2,1,0:T(8,128)S(1)} %copy-done.3, bf16[8,16,1024]{2,1,0:T(8,128)(2,1)S(1)} %copy-done.5, bf16[3,8,16,1024]{3,2,1,0:T(8,128)(2,1)S(1)} %copy-done.1, f32[8,8,1024]{2,1,0:T(8,128)S(1)} %collective-permute-done.even_d.refs_3_, ...), custom_call_target="tpu_custom_call" | custom-call | tf_op jit(solution)/shard_map/main/pallas_call | solution.py:343
  29.2 4.4 %collective-permute-start.6 = (f32[4,8,256]{2,1,0:T(8,128)S(1)}, f32[4,8,256]{2,1,0:T(8,128)S(1)}, u32[]{:S(2)}, u32[]{:S(2)}) collective-permute-start(f32[4,8,256]{2,1,0:T(8,128)S(1)} %get-tuple-element.24), channel_id=1, source_target_pairs={{0,1},{1,0},{2,3},{3,2},{4,5},{5,4},{6,7},{7,6},{8,9},{9,8},{10,11... | collective-permute-start | bytes 98312 | tf_op jit(solution)/shard_map/ppermute | solution.py:358
  33.6 2.4 %collective-permute-start.8 = (f32[4,8,256]{2,1,0:T(8,128)S(1)}, f32[4,8,256]{2,1,0:T(8,128)S(1)}, u32[]{:S(2)}, u32[]{:S(2)}) collective-permute-start(f32[4,8,256]{2,1,0:T(8,128)S(1)} %get-tuple-element.22), channel_id=1, source_target_pairs={{0,3},{1,2},{2,1},{3,0},{4,7},{5,6},{6,5},{7,4},{8,11},{9,10},{10,... | collective-permute-start | bytes 98312 | tf_op jit(solution)/shard_map/ppermute | solution.py:358
  36.1 2.4 %collective-permute-done.7 = f32[4,8,256]{2,1,0:T(8,128)S(1)} collective-permute-done((f32[4,8,256]{2,1,0:T(8,128)S(1)}, f32[4,8,256]{2,1,0:T(8,128)S(1)}, u32[]{:S(2)}, u32[]{:S(2)}) %collective-permute-start.7) | collective-permute-done | bytes 32800 | tf_op jit(solution)/shard_map/ppermute | solution.py:358
  38.5 0.9 %collective-permute-done.8 = f32[4,8,256]{2,1,0:T(8,128)S(1)} collective-permute-done((f32[4,8,256]{2,1,0:T(8,128)S(1)}, f32[4,8,256]{2,1,0:T(8,128)S(1)}, u32[]{:S(2)}, u32[]{:S(2)}) %collective-permute-start.8) | collective-permute-done | bytes 32800 | tf_op jit(solution)/shard_map/ppermute | solution.py:358
  39.5 0.6 %pad_maximum_fusion.1 = f32[4,8,256]{2,1,0:T(8,128)} fusion(f32[1,8,256]{2,1,0:T(8,128)S(1)} %fusion.6, f32[3,8,256]{2,1,0:T(8,128)S(1)} %fusion.1), kind=kLoop, calls=%fused_computation.1 | loop fusion | flops 8192 | bytes 65536 | tf_op jit(solution)/shard_map/concatenate | solution.py:370
  (15 shorter events, 0.1 us)
Async XLA Ops:
  0.6 1.1 %copy-start = (bf16[3,8,16,1024]{3,2,1,0:T(8,128)(2,1)S(1)}, bf16[3,8,16,1024]{3,2,1,0:T(8,128)(2,1)}, u32[]{:S(2)}) copy-start(bf16[3,8,16,1024]{3,2,1,0:T(8,128)(2,1)} %refs_2_.1) | copy-start | bytes 2359300
  1.8 1.0 %copy-start.2 = (f32[8,16,1024]{2,1,0:T(8,128)S(1)}, f32[8,16,1024]{2,1,0:T(8,128)}, u32[]{:S(2)}) copy-start(f32[8,16,1024]{2,1,0:T(8,128)} %refs_0_.1) | copy-start | bytes 1572868
  2.8 0.9 %copy-start.4 = (bf16[8,16,1024]{2,1,0:T(8,128)(2,1)S(1)}, bf16[8,16,1024]{2,1,0:T(8,128)(2,1)}, u32[]{:S(2)}) copy-start(bf16[8,16,1024]{2,1,0:T(8,128)(2,1)} %refs_1_.1) | copy-start | bytes 786436
  4.8 8.0 %collective-permute-start = (f32[8,8,1024]{2,1,0:T(8,128)S(1)}, f32[8,8,1024]{2,1,0:T(8,128)S(1)}, u32[]{:S(2)}, u32[]{:S(2)}) collective-permute-start(f32[8,8,1024]{2,1,0:T(8,128)S(1)} %get-tuple-element.10), channel_id=1, source_target_pairs={{0,1},{2,3},{1,0},{3,2},{4,5},{6,7},{5,4},{7,6},{8,9},{10,11},{9,8... | collective-permute-start | bytes 786440 | tf_op jit(solution)/shard_map/ppermute | solution.py:22
  6.4 6.5 %collective-permute-start.1 = (f32[8,8,1024]{2,1,0:T(8,128)S(1)}, f32[8,8,1024]{2,1,0:T(8,128)S(1)}, u32[]{:S(2)}, u32[]{:S(2)}) collective-permute-start(f32[8,8,1024]{2,1,0:T(8,128)S(1)} %get-tuple-element.11), channel_id=1, source_target_pairs={{1,2},{2,1},{5,6},{6,5},{9,10},{10,9},{13,14},{14,13},{17,18},{18,... | collective-permute-start | bytes 786440 | tf_op jit(solution)/shard_map/ppermute | solution.py:22
  7.1 16.9 %collective-permute-start.2 = (f32[6,16,1024]{2,1,0:T(8,128)}, f32[6,16,1024]{2,1,0:T(8,128)S(1)}, u32[]{:S(2)}, u32[]{:S(2)}) collective-permute-start(f32[6,16,1024]{2,1,0:T(8,128)} %get-tuple-element.12), channel_id=1, source_target_pairs={{0,4},{8,12},{16,20},{24,28},{4,0},{12,8},{20,16},{28,24},{1,5},{9... | collective-permute-start | bytes 1179656 | tf_op jit(solution)/shard_map/ppermute | solution.py:22
  7.2 16.9 %copy-start.1 = (bf16[3,8,16,1024]{3,2,1,0:T(8,128)(2,1)S(1)}, bf16[3,8,16,1024]{3,2,1,0:T(8,128)(2,1)}, u32[]{:S(2)}) copy-start(bf16[3,8,16,1024]{3,2,1,0:T(8,128)(2,1)} %refs_2_.1) | copy-start | bytes 2359300
  7.2 16.9 %copy-start.3 = (f32[8,16,1024]{2,1,0:T(8,128)S(1)}, f32[8,16,1024]{2,1,0:T(8,128)}, u32[]{:S(2)}) copy-start(f32[8,16,1024]{2,1,0:T(8,128)} %refs_0_.1) | copy-start | bytes 1572868
  7.2 16.9 %copy-start.5 = (bf16[8,16,1024]{2,1,0:T(8,128)(2,1)S(1)}, bf16[8,16,1024]{2,1,0:T(8,128)(2,1)}, u32[]{:S(2)}) copy-start(bf16[8,16,1024]{2,1,0:T(8,128)(2,1)} %refs_1_.1) | copy-start | bytes 786436
  7.2 16.8 %collective-permute-start.3 = (f32[6,16,1024]{2,1,0:T(8,128)S(1)}, f32[6,16,1024]{2,1,0:T(8,128)S(1)}, u32[]{:S(2)}, u32[]{:S(2)}) collective-permute-start(f32[6,16,1024]{2,1,0:T(8,128)S(1)} %get-tuple-element.13), channel_id=1, source_target_pairs={{4,8},{12,16},{20,24},{8,4},{16,12},{24,20},{5,9},{13,17},{21,25},... | collective-permute-start | bytes 1179656 | tf_op jit(solution)/shard_map/ppermute | solution.py:22
  13.9 3.5 %collective-permute-start.4 = (f32[32,1024]{1,0:T(8,128)}, f32[32,1024]{1,0:T(8,128)S(1)}, u32[]{:S(2)}, u32[]{:S(2)}) collective-permute-start(f32[32,1024]{1,0:T(8,128)} %get-tuple-element.14), channel_id=1, source_target_pairs={{0,4},{8,12},{16,20},{24,28},{4,0},{12,8},{20,16},{28,24},{1,5},{9... | collective-permute-start | bytes 393224 | tf_op jit(solution)/shard_map/ppermute | solution.py:22
  13.9 10.2 %collective-permute-start.5 = (f32[32,1024]{1,0:T(8,128)}, f32[32,1024]{1,0:T(8,128)S(1)}, u32[]{:S(2)}, u32[]{:S(2)}) collective-permute-start(f32[32,1024]{1,0:T(8,128)} %get-tuple-element.15), channel_id=1, source_target_pairs={{4,8},{12,16},{20,24},{8,4},{16,12},{24,20},{5,9},{13,17},{21,25},... | collective-permute-start | bytes 393224 | tf_op jit(solution)/shard_map/ppermute | solution.py:22
  29.2 6.9 %collective-permute-start.6 = (f32[4,8,256]{2,1,0:T(8,128)S(1)}, f32[4,8,256]{2,1,0:T(8,128)S(1)}, u32[]{:S(2)}, u32[]{:S(2)}) collective-permute-start(f32[4,8,256]{2,1,0:T(8,128)S(1)} %get-tuple-element.24), channel_id=1, source_target_pairs={{0,1},{1,0},{2,3},{3,2},{4,5},{5,4},{6,7},{7,6},{8,9},{9,8},{10,11... | collective-permute-start | bytes 98312 | tf_op jit(solution)/shard_map/ppermute | solution.py:358
  33.6 4.8 %collective-permute-start.7 = (f32[4,8,256]{2,1,0:T(8,128)S(1)}, f32[4,8,256]{2,1,0:T(8,128)S(1)}, u32[]{:S(2)}, u32[]{:S(2)}) collective-permute-start(f32[4,8,256]{2,1,0:T(8,128)S(1)} %get-tuple-element.23), channel_id=1, source_target_pairs={{0,2},{1,3},{2,0},{3,1},{4,6},{5,7},{6,4},{7,5},{8,10},{9,11},{10,... | collective-permute-start | bytes 98312 | tf_op jit(solution)/shard_map/ppermute | solution.py:358
  33.6 5.7 %collective-permute-start.8 = (f32[4,8,256]{2,1,0:T(8,128)S(1)}, f32[4,8,256]{2,1,0:T(8,128)S(1)}, u32[]{:S(2)}, u32[]{:S(2)}) collective-permute-start(f32[4,8,256]{2,1,0:T(8,128)S(1)} %get-tuple-element.22), channel_id=1, source_target_pairs={{0,3},{1,2},{2,1},{3,0},{4,7},{5,6},{6,5},{7,4},{8,11},{9,10},{10,... | collective-permute-start | bytes 98312 | tf_op jit(solution)/shard_map/ppermute | solution.py:358

commit v2 on v1

v2 whole, which is shorter than its diff:
```python
import jax
import jax.numpy as jnp
from jax import lax
from jax.experimental import pallas as pl
from jax.experimental.pallas import tpu as pltpu
from jax.sharding import PartitionSpec as P

time_step = 0.2
growth_rate = 1.0
opacity_total = 3.0

lanes = 128
margin = 8


def pairs(count, first):
    forward = [(i, i + 1) for i in range(first, count - 1, 2)]
    return forward + [(target, source) for source, target in forward]


def swap_pairs(value, axis, first):
    return lax.ppermute(value, axis, pairs(lax.axis_size(axis), first))


def stencil(u, low, high, coef):
    diff = coef[0]
    change = growth_rate * u * (1.0 - u)
    for before, after, speed in zip(low, high, coef[1:]):
        change = change + (diff + jnp.maximum(speed, 0.0)) * (before - u)
        change = change + (diff - jnp.minimum(speed, 0.0)) * (after - u)
    return u + time_step * change


def beside(chunks):
    lane = lax.broadcasted_iota(jnp.int32, chunks[0].shape, 1)
    right = [pltpu.roll(x, 1, 1) for x in chunks]
    left = [pltpu.roll(x, lanes - 1, 1) for x in chunks]
    zero = jnp.zeros_like(chunks[0])
    count = len(chunks)
    before = [jnp.where(lane == 0, right[c - 1] if c else zero, right[c]) for c in range(count)]
    after = [
        jnp.where(lane == lanes - 1, left[c + 1] if c + 1 < count else zero, left[c])
        for c in range(count)
    ]
    return before, after


def cols(c):
    return slice(c * lanes, (c + 1) * lanes)


def coef_of(diff, vel, r, c):
    return [diff[r, :, cols(c)].astype(jnp.float32)] + [
        vel[i, r, :, cols(c)].astype(jnp.float32) for i in range(3)
    ]


def weight_low(diff, speed):
    return time_step * (diff + jnp.maximum(speed, 0.0))


def weight_high(diff, speed):
    return time_step * (diff - jnp.minimum(speed, 0.0))


def pack_kernel(
    field_far, diff_far, vel_far, field, diff, vel, even_d, odd_d, even_r, odd_r, flat, coefs, sems
):
    loads = [
        pltpu.make_async_copy(source, target, sems.at[i])
        for i, (source, target) in enumerate(
            ((field_far, field), (diff_far, diff), (vel_far, vel))
        )
    ]
    for load in loads:
        load.start()
    for load in loads:
        load.wait()
    rows, depth, width = field.shape
    count = width // lanes
    depth_odd = lax.axis_index("depth") % 2 == 1
    rows_odd = lax.axis_index("rows") % 2 == 1

    for c in range(count):
        for r in range(rows):
            place = pl.ds(r * depth, depth)
            coef = coef_of(diff, vel, r, c)
            flat[c, place, :] = field[r, :, cols(c)]
            for i in range(4):
                coefs[i, c, place, :] = coef[i]
            if r == 0:
                first = (field[r, :, cols(c)], weight_low(coef[0], coef[1]))
            if r == rows - 1:
                last = (field[r, :, cols(c)], weight_high(coef[0], coef[1]))
        for i in range(2):
            even_r[i, :, cols(c)] = jnp.where(rows_odd, first[i], last[i])
            odd_r[i, :, cols(c)] = jnp.where(rows_odd, last[i], first[i])

    row = lax.broadcasted_iota(jnp.int32, (rows, lanes), 0)
    sides = []
    for near, step in ((0, 1), (depth - 1, -1)):

        def slab(ref, d):
            return [ref[c, pl.ds(d, rows, stride=depth), :] for c in range(count)]

        u0, u1, u2 = (slab(flat, near + step * j) for j in range(3))
        near_coef = [slab(coefs.at[i], near) for i in range(4)]
        next_coef = [slab(coefs.at[i], near + step) for i in range(4)]
        before, after = beside(u1)
        side = []
        for c in range(count):
            above = jnp.where(row == 0, 0.0, pltpu.roll(u1[c], 1, 0))
            below = jnp.where(row == rows - 1, 0.0, pltpu.roll(u1[c], rows - 1, 0))
            deep = (u0[c], u2[c]) if step > 0 else (u2[c], u0[c])
            coef = [next_coef[i][c] for i in range(4)]
            middle = stencil(
                u1[c], (above, deep[0], before[c]), (below, deep[1], after[c]), coef
            )
            weight = jnp.where(
                row == 0, weight_low(coef[0], coef[1]), weight_high(coef[0], coef[1])
            )
            side.append([u0[c], u1[c]] + [near_coef[i][c] for i in range(4)] + [middle, weight])
        sides.append(side)
    low, high = sides
    for c in range(count):
        for i in range(8):
            even_d[i, :, cols(c)] = jnp.where(depth_odd, low[c][i], high[c][i])
            odd_d[i, :, cols(c)] = jnp.where(depth_odd, high[c][i], low[c][i])


def arrived(even, odd, is_odd, index):
    a, b = even[index], odd[index]
    return jnp.where(is_odd, a, b), jnp.where(is_odd, b, a)


def edge_kernel(
    field, diff, vel, even_d, odd_d, even_r, odd_r, even_2, odd_2, middles, ext, edge
):
    rows, depth, width = field.shape
    every = range(width // lanes)
    depth_odd = lax.axis_index("depth") % 2 == 1
    rows_odd = lax.axis_index("rows") % 2 == 1
    own = pl.ds(margin, depth)
    shallow, deep = pl.ds(margin - 1, depth), pl.ds(margin + 1, depth)
    beyond = [arrived(even_r, odd_r, rows_odd, (0, slice(None), cols(c))) for c in every]
    lines = (0, 1, rows - 2, rows - 1)
    values = {r: [field[r, :, cols(c)] for c in every] for r in lines + (2, rows - 3)}
    values[-1] = [x[0] for x in beyond]
    values[rows] = [x[1] for x in beyond]
    coefs = {r: [coef_of(diff, vel, r, c) for c in every] for r in lines}
    for j, r in enumerate(lines):
        u = values[r]
        before, after = beside(u)
        for c in every:
            low, high = arrived(even_d, odd_d, depth_odd, (0, pl.ds(r, 1), cols(c)))
            ext[j, c, margin - 1 : margin, :] = low
            ext[j, c, own, :] = u[c]
            ext[j, c, margin + depth : margin + depth + 1, :] = high
        for c in every:
            middles[j, :, cols(c)] = stencil(
                u[c],
                (values[r - 1][c], ext[j, c, shallow, :], before[c]),
                (values[r + 1][c], ext[j, c, deep, :], after[c]),
                coefs[r][c],
            )
    zero = jnp.zeros((1, lanes), jnp.float32)
    none = jnp.zeros((depth, lanes), jnp.float32)
    sides = []
    for j, inner, r in ((0, 1, 0), (3, 2, rows - 1)):
        u = [middles[j, :, cols(c)] for c in every]
        before, after = beside(u)
        side = []
        for c in every:
            edge[j // 3, c, margin - 1 : margin, :] = zero
            edge[j // 3, c, own, :] = u[c]
            edge[j // 3, c, margin + depth : margin + depth + 1, :] = zero
        for c in every:
            next_row = middles[inner, :, cols(c)]
            above, below = (none, next_row) if r == 0 else (next_row, none)
            coef = coefs[r][c]
            partly = stencil(
                u[c],
                (above, edge[j // 3, c, shallow, :], before[c]),
                (below, edge[j // 3, c, deep, :], after[c]),
                coef,
            )
            side.append(
                (u[c], partly, weight_low(coef[0], coef[2]), weight_high(coef[0], coef[2]))
            )
        sides.append(side)
    first, last = sides
    for c in every:
        for i in range(2):
            place = pl.ds(i * depth, depth)
            even_2[place, cols(c)] = jnp.where(rows_odd, first[c][i], last[c][i])
            odd_2[place, cols(c)] = jnp.where(rows_odd, last[c][i], first[c][i])
        for k, d in ((0, 0), (1, depth - 1)):
            place = 2 * depth + 8 * k + 7
            f_val, l_val = first[c][2 + k][d : d + 1], last[c][2 + k][d : d + 1]
            even_2[place : place + 1, cols(c)] = jnp.where(rows_odd, f_val, l_val)
            odd_2[place : place + 1, cols(c)] = jnp.where(rows_odd, l_val, f_val)
    for j, (item, f_row) in enumerate(
        ((0, 0), (1, 0), (0, 1), (2, 0), (3, 0), (4, 0), (5, 0))
    ):
        l_row = rows - 1 - f_row
        for c in every:
            f_both = arrived(even_d, odd_d, depth_odd, (item, pl.ds(f_row, 1), cols(c)))
            l_both = arrived(even_d, odd_d, depth_odd, (item, pl.ds(l_row, 1), cols(c)))
            for k in range(2):
                place = 2 * depth + 8 * k + j
                even_2[place : place + 1, cols(c)] = jnp.where(rows_odd, f_both[k], l_both[k])
                odd_2[place : place + 1, cols(c)] = jnp.where(rows_odd, l_both[k], f_both[k])


class Block:
    def __init__(self, rows, depth, width):
        self.rows, self.depth, self.every = rows, depth, range(width // lanes)
        self.pitch = depth + 2 * margin

    def at(self, r, d):
        return (r + 2) * self.pitch + margin + d

    def along(self, r, d=0):
        return pl.ds(self.at(r, d), self.depth)

    def across(self, r, d, length):
        return pl.ds(self.at(r, d), length, stride=self.pitch)

    def line(self, ref, r, d=0):
        return [ref[c, self.along(r, d), :] for c in self.every]

    def slab(self, ref, r, d, length):
        return [ref[c, self.across(r, d, length), :] for c in self.every]

    def put(self, ref, place, values):
        for c in self.every:
            ref[c, place, :] = values[c]

    def section_line(self, ref, r, coef):
        u = self.line(ref, r)
        before, after = beside(u)
        low = (self.line(ref, r - 1), self.line(ref, r, -1), before)
        high = (self.line(ref, r + 1), self.line(ref, r, 1), after)
        return [
            stencil(u[c], [x[c] for x in low], [x[c] for x in high], coef(c)) for c in self.every
        ]

    def section_slab(self, ref, r, d, length, coef):
        u = self.slab(ref, r, d, length)
        before, after = beside(u)
        low = (self.slab(ref, r - 1, d, length), self.slab(ref, r, d - 1, length), before)
        high = (self.slab(ref, r + 1, d, length), self.slab(ref, r, d + 1, length), after)
        return [
            stencil(u[c], [x[c] for x in low], [x[c] for x in high], coef(c)) for c in self.every
        ]


def inner_kernel(
    field, diff, vel, even_d, odd_d, even_r, odd_r, middles, first, second, third, slabs, front
):
    rows, depth, width = field.shape
    block = Block(rows, depth, width)
    depth_odd = lax.axis_index("depth") % 2 == 1
    rows_odd = lax.axis_index("rows") % 2 == 1
    for c in block.every:
        for r in range(rows):
            first[c, block.along(r), :] = field[r, :, cols(c)]
        low, high = arrived(even_r, odd_r, rows_odd, (0, slice(None), cols(c)))
        first[c, block.along(-1), :] = low
        first[c, block.along(rows), :] = high
        for j in range(2):
            low, high = arrived(even_d, odd_d, depth_odd, (j, slice(None), cols(c)))
            first[c, block.across(0, -1 - j, rows), :] = low
            first[c, block.across(0, depth + j, rows), :] = high
        for i in range(4):
            both = arrived(even_d, odd_d, depth_odd, (2 + i, slice(None), cols(c)))
            for k in range(2):
                slabs[k, i, c, 1 : rows + 1, :] = both[k]
        for j, r in enumerate((0, 1, rows - 2, rows - 1)):
            second[c, block.along(r), :] = middles[j, :, cols(c)]

    def own_middle(r, carry):
        values = block.section_line(first, r, lambda c: coef_of(diff, vel, r, c))
        block.put(second, block.along(r), values)
        return carry

    lax.fori_loop(2, rows - 2, own_middle, 0)
    for k, d in ((0, -1), (1, depth)):
        values = block.section_slab(
            first, 1, d, rows - 2, lambda c: [slabs[k, i, c, 2:rows, :] for i in range(4)]
        )
        block.put(second, block.across(1, d, rows - 2), values)

    def own_front(r, carry):
        values = block.section_line(second, r, lambda c: coef_of(diff, vel, r, c))
        block.put(third, block.along(r), values)
        for c in block.every:
            front[r, :, cols(c)] = values[c]
        return carry

    lax.fori_loop(1, rows - 1, own_front, 0)


def rim_kernel(
    opacity, diff, vel, even_d, odd_d, even_r, odd_r, even_2, odd_2, *refs
):
    first, second, third, slabs, front, front_far, partial, sem = refs[5:]
    rows, depth, width = front.shape
    block = Block(rows, depth, width)
    every = block.every
    depth_odd = lax.axis_index("depth") % 2 == 1
    rows_odd = lax.axis_index("rows") % 2 == 1
    row = lax.broadcasted_iota(jnp.int32, (rows, lanes), 0)

    def corner(k, j, c):
        place = 2 * depth + 8 * k + j
        return arrived(even_2, odd_2, rows_odd, (slice(place, place + 1), cols(c)))

    for c in every:
        for k, step in ((0, -1), (1, 1)):
            near = -1 if k == 0 else depth
            for j, r, d in ((0, 1, near), (1, 1, near + step), (2, 2, near)):
                low, high = corner(k, j, c)
                first[c, pl.ds(block.at(-r, d), 1), :] = low
                first[c, pl.ds(block.at(rows - 1 + r, d), 1), :] = high
            for i in range(4):
                low, high = corner(k, 3 + i, c)
                slabs[k, i, c, 0:1, :] = low
                slabs[k, i, c, rows + 1 : rows + 2, :] = high
        low, high = arrived(even_2, odd_2, rows_odd, (slice(0, depth), cols(c)))
        second[c, block.along(-1), :] = low
        second[c, block.along(rows), :] = high
    for k, d in ((0, -2), (1, depth + 1)):
        above, below = block.slab(first, -1, d, rows), block.slab(first, 1, d, rows)
        for c in every:
            partly = arrived(even_d, odd_d, depth_odd, (6, slice(None), cols(c)))[k]
            weight = arrived(even_d, odd_d, depth_odd, (7, slice(None), cols(c)))[k]
            extra = jnp.where(row == 0, above[c], jnp.where(row == rows - 1, below[c], 0.0))
            second[c, block.across(0, d, rows), :] = partly + weight * extra
    for k, d in ((0, -1), (1, depth)):
        values = block.section_slab(
            first, -1, d, rows + 2, lambda c: [slabs[k, i, c, 0 : rows + 2, :] for i in range(4)]
        )
        block.put(second, block.across(-1, d, rows + 2), values)

    for r in (0, rows - 1):
        values = block.section_line(second, r, lambda c: coef_of(diff, vel, r, c))
        block.put(third, block.along(r), values)
        for c in every:
            front[r, :, cols(c)] = values[c]
    save = pltpu.make_async_copy(front, front_far, sem)
    save.start()
    for k, r, inner in ((0, -1, 0), (1, rows, rows - 1)):
        for c in every:
            partly = arrived(even_2, odd_2, rows_odd, (slice(depth, 2 * depth), cols(c)))[k]
            weight = arrived(even_r, odd_r, rows_odd, (1, slice(None), cols(c)))[k]
            third[c, block.along(r), :] = partly + weight * second[c, block.along(inner), :]
            for side, d, past in ((0, 0, -1), (1, depth - 1, depth)):
                place = pl.ds(block.at(r, d), 1)
                more = corner(side, 7, c)[k] * second[c, pl.ds(block.at(r, past), 1), :]
                third[c, place, :] = third[c, place, :] + more
    for k, d in ((0, -1), (1, depth)):
        values = block.section_slab(
            second, 0, d, rows, lambda c: [slabs[k, i, c, 1 : rows + 1, :] for i in range(4)]
        )
        block.put(third, block.across(0, d, rows), values)

    def shine(d, carry):
        center = block.slab(third, 0, d, rows)
        before, after = beside(center)
        above, below = block.slab(third, -1, d, rows), block.slab(third, 1, d, rows)
        shallow, deep = block.slab(third, 0, d - 1, rows), block.slab(third, 0, d + 1, rows)
        result = []
        for c in every:
            through, total, red, green = carry[c]
            u = center[c]
            grad_row = below[c] - above[c]
            grad_deep = deep[c] - shallow[c]
            grad_col = after[c] - before[c]
            lighting = 0.48 * grad_row + 0.64 * grad_deep + 0.6 * grad_col
            magnitude = grad_row * grad_row + grad_deep * grad_deep + grad_col * grad_col + 0.4
            shade = 0.35 + 0.65 * lighting * lighting / magnitude
            passed = jnp.exp(-opacity * u)
            weight = through * (1.0 - passed) * shade
            colored = weight * u
            result.append((through * passed, total + weight, red + colored, green + colored * u))
        return tuple(result)

    zero, one = jnp.zeros((rows, lanes), jnp.float32), jnp.ones((rows, lanes), jnp.float32)
    carry = tuple((one, zero, zero, zero) for _ in every)
    for d in range(depth):
        carry = shine(d, carry)
    for c, (through, total, red, green) in enumerate(carry):
        partial[0, :, cols(c)] = red
        partial[1, :, cols(c)] = green
        partial[2, :, cols(c)] = total - red
        partial[3, :, cols(c)] = through
    save.wait()


def vmem(shape):
    return pltpu.VMEM(shape, jnp.float32)


def here(value):
    return pltpu.with_memory_space_constraint(value, pltpu.VMEM)


def far(value):
    return pltpu.with_memory_space_constraint(value, pltpu.HBM)


def shards(field, diffusivity, velocity):
    rows, depth, width = field.shape
    count = width // lanes
    block = Block(rows, depth, width)
    groups = lax.axis_size("depth")
    params = pltpu.CompilerParams(vmem_limit_bytes=24 * 2**20)
    in_hbm = pl.BlockSpec(memory_space=pltpu.HBM)

    own_types = [pltpu.VMEM(x.shape, x.dtype) for x in (field, diffusivity, velocity)]
    *own, even_d, odd_d, even_r, odd_r = pl.pallas_call(
        pack_kernel,
        in_specs=[in_hbm] * 3,
        out_shape=own_types + [vmem((8, rows, width))] * 2 + [vmem((2, depth, width))] * 2,
        scratch_shapes=[
            vmem((count, rows * depth, lanes)),
            vmem((4, count, rows * depth, lanes)),
            pltpu.SemaphoreType.DMA((3,)),
        ],
        compiler_params=params,
        name="pack",
    )(far(field), far(diffusivity), far(velocity))
    odd_r = here(swap_pairs(odd_r, "rows", 1))
    even_d = here(swap_pairs(even_d, "depth", 0))
    odd_d = here(swap_pairs(odd_d, "depth", 1))
    even_r = here(swap_pairs(even_r, "rows", 0))
    own = [here(x) for x in own]
    even_2, odd_2, middles = pl.pallas_call(
        edge_kernel,
        out_shape=[vmem((2 * depth + 16, width))] * 2 + [vmem((4, depth, width))],
        scratch_shapes=[
            vmem((4, count, block.pitch, lanes)),
            vmem((2, count, block.pitch, lanes)),
        ],
        compiler_params=params,
        name="edge",
    )(*own, even_d, odd_d, even_r, odd_r)
    even_2 = here(swap_pairs(even_2, "rows", 0))
    odd_2 = here(swap_pairs(odd_2, "rows", 1))
    held = [vmem((count, (rows + 4) * block.pitch, lanes))] * 3
    held += [vmem((2, 4, count, rows + 8, lanes)), vmem(field.shape)]
    state = pl.pallas_call(
        inner_kernel,
        out_shape=held,
        compiler_params=params,
        cost_estimate=pl.CostEstimate(
            flops=80 * field.size, bytes_accessed=8 * field.size, transcendentals=0
        ),
        name="inner",
    )(*own, even_d, odd_d, even_r, odd_r, here(middles))
    opacity = opacity_total / (depth * groups)
    *_, front, partial = pl.pallas_call(
        lambda *refs: rim_kernel(opacity, *refs),
        out_shape=held + [jax.ShapeDtypeStruct(field.shape, jnp.float32), vmem((4, rows, width))],
        out_specs=[pl.BlockSpec(memory_space=pltpu.VMEM)] * 5
        + [in_hbm, pl.BlockSpec(memory_space=pltpu.VMEM)],
        scratch_shapes=[pltpu.SemaphoreType.DMA],
        input_output_aliases={8 + i: i for i in range(5)},
        compiler_params=params,
        name="rim",
    )(*own[1:], even_d, odd_d, even_r, odd_r, even_2, odd_2, *[here(x) for x in state])

    position = lax.axis_index("depth")
    split = partial.reshape(4, rows, groups, width // groups)
    parts = []
    for apart in range(groups):
        part = lax.dynamic_index_in_dim(split, position ^ apart, 2, keepdims=False)
        if apart:
            part = lax.ppermute(part, "depth", [(i, i ^ apart) for i in range(groups)])
        parts.append(part)
    parts = jnp.stack(parts)
    picture = None
    for s in range(groups):
        segment = lax.dynamic_index_in_dim(parts, position ^ s, 0, keepdims=False)
        if picture is None:
            colors, through = segment[:3], segment[3:]
            picture = (colors, through)
        else:
            colors = colors + through * segment[:3]
            through = through * segment[3:]
    return front, jnp.concatenate([colors, through], axis=0)


def solution(mesh):
    return jax.shard_map(
        shards,
        mesh=mesh,
        in_specs=(
            P("rows", "depth", None),
            P("rows", "depth", None),
            P(None, "rows", "depth", None),
        ),
        out_specs=(P("rows", "depth", None), P(None, "rows", "depth")),
        check_vma=False,
    )
```

time: 40.4 us -> 37 us (0.916)
  local copies, waits for them, and re-layouts: 3.15 us -> 0.02 us
  waiting for transfers between devices: 12.1 us -> 12.7 us
    unnamed x12 -> x0, local copies, waits for them, and re-layouts: 3.14 us -> none
    ppermute x6, waiting for transfers between devices: 8.84 us -> 9.44 us  [swap_pairs(): return lax.ppermute(value, axis, pairs(lax.axis_size(axis), first))]
    pallas_call x3 -> x4, Pallas kernels: 7.17 us -> 6.79 us  [the longest x1 2.59 us: shards(): pl.pallas_call(lambda *refs: rim_kernel(opacity, *refs), out_shape=held +...]
  transfers between devices with their start and end apart: 9 -> 9, of which waited for: 4 -> 4; matrix products, arithmetic and copies ran while one was open for 0% -> 0% of each run, Pallas kernels for 2% -> 4%
where the time goes in v2:
time: 37 us; the launch traced here: 36.9 us
  starting transfers between devices  15.9 us (43%)
  waiting for transfers between devices  12.7 us (34%)
  Pallas kernels  6.79 us (18%)
  between operations  0.78 us (2%)
  other arithmetic  0.68 us (2%)
    ppermute x6, waiting for transfers between devices, swap_pairs(): return lax.ppermute(value, axis, pairs(lax.axis_size(axis), first))  9.44 us
    ppermute x6, starting transfers between devices, swap_pairs(): return lax.ppermute(value, axis, pairs(lax.axis_size(axis), first))  9 us
    ppermute x3, starting transfers between devices, shards(): part = lax.ppermute(part, 'depth', [(i, i ^ apart) for i in range(groups)])  6.89 us
    ppermute x3, waiting for transfers between devices, shards(): part = lax.ppermute(part, 'depth', [(i, i ^ apart) for i in range(groups)])  3.27 us
    pallas_call x1, Pallas kernels, shards(): pl.pallas_call(lambda *refs: rim_kernel(opacity, *refs), out_shape=held +...  2.59 us
    pallas_call x1, Pallas kernels, shards(): pl.pallas_call(pack_kernel, in_specs=[in_hbm] * 3, out_shape=own_types +...  2.03 us
    pallas_call x1, Pallas kernels, shards(): pl.pallas_call(inner_kernel, out_shape=held, compiler_params=params, cost...  1.49 us
  transfers between devices with their start and end apart: 9, of which 4 were waited for; matrix products, arithmetic and copies ran while one was open for 0% of the time, Pallas kernels for 4%

profile of v2, /device:TPU:4, one launch (start us, length us, event | category | flops | bytes accessed | tf_op | source)
XLA Modules:
  0.0 36.9 jit_solution(11826455295721109037)
XLA Ops:
  0.6 2.0 %pack.1 = (f32[8,16,1024]{2,1,0:T(8,128)S(1)}, bf16[8,16,1024]{2,1,0:T(8,128)(2,1)S(1)}, bf16[3,8,16,1024]{3,2,1,0:T(8,128)(2,1)S(1)}, f32[8,8,1024]{2,1,0:T(8,1...) custom-call(f32[8,16,1024]{2,1,0:T(8,128)} %field_far.1, ...), custom_call_target="tpu_custom_call" | custom-call | tf_op jit(solution)/shard_map/pack/pallas_call | solution.py:422
  2.7 1.6 %collective-permute-start = (f32[8,8,1024]{2,1,0:T(8,128)S(1)}, f32[8,8,1024]{2,1,0:T(8,128)S(1)}, u32[]{:S(2)}, u32[]{:S(2)}) collective-permute-start(f32[8,8,1024]{2,1,0:T(8,128)S(1)} %get-tuple-element.21), channel_id=1, source_target_pairs={{0,1},{2,3},{1,0},{3,2},{4,5},{6,7},{5,4},{7,6},{8,9},{10,11},{9,8... | collective-permute-start | bytes 786440 | tf_op jit(solution)/shard_map/ppermute | solution.py:22
  4.3 0.7 %collective-permute-start.1 = (f32[8,8,1024]{2,1,0:T(8,128)S(1)}, f32[8,8,1024]{2,1,0:T(8,128)S(1)}, u32[]{:S(2)}, u32[]{:S(2)}) collective-permute-start(f32[8,8,1024]{2,1,0:T(8,128)S(1)} %get-tuple-element.22), channel_id=1, source_target_pairs={{1,2},{2,1},{5,6},{6,5},{9,10},{10,9},{13,14},{14,13},{17,18},{18,... | collective-permute-start | bytes 786440 | tf_op jit(solution)/shard_map/ppermute | solution.py:22
  5.0 0.1 collective-permute-start.2
  5.1 3.4 %collective-permute-start.3 = (f32[2,16,1024]{2,1,0:T(8,128)S(1)}, f32[2,16,1024]{2,1,0:T(8,128)S(1)}, u32[]{:S(2)}, u32[]{:S(2)}) collective-permute-start(f32[2,16,1024]{2,1,0:T(8,128)S(1)} %get-tuple-element.24), channel_id=1, source_target_pairs={{4,8},{12,16},{20,24},{8,4},{16,12},{24,20},{5,9},{13,17},{21,25},... | collective-permute-start | bytes 393224 | tf_op jit(solution)/shard_map/ppermute | solution.py:22
  8.5 0.0 collective-permute-done.2.even_r.refs_4_
  8.5 4.8 %collective-permute-done.3.odd_r.refs_5_ = f32[2,16,1024]{2,1,0:T(8,128)S(1)} collective-permute-done((f32[2,16,1024]{2,1,0:T(8,128)S(1)}, f32[2,16,1024]{2,1,0:T(8,128)S(1)}, u32[]{:S(2)}, u32[]{:S(2)}) %collective-permute-start.3) | collective-permute-done | bytes 131104 | tf_op jit(solution)/shard_map/ppermute | solution.py:22
  13.4 0.0 collective-permute-done.even_d.refs_2_
  13.4 0.0 collective-permute-done.1.odd_d.refs_3_
  13.4 0.7 %edge.1 = (f32[48,1024]{1,0:T(8,128)S(1)}, f32[48,1024]{1,0:T(8,128)S(1)}, f32[4,16,1024]{2,1,0:T(8,128)S(1)}) custom-call(f32[8,16,1024]{2,1,0:T(8,128)S(1)} %get-tuple-element.25.field, bf16[8,16,1024]{2,1,0:T(8,128)(2,1)S(1)} %get-tuple-element.19.diff.refs_0_, bf16[3,8,16,1024]{3,2,1,0:T(8,128)(2,1)S(1)} %get-tuple-element.20.vel.refs_1_, ...), custom_call_target="tpu_custom_call" | custom-call | tf_op jit(solution)/shard_map/edge/pallas_call | solution.py:439
  14.0 0.1 collective-permute-start.4
  14.1 3.1 %collective-permute-start.5 = (f32[48,1024]{1,0:T(8,128)S(1)}, f32[48,1024]{1,0:T(8,128)S(1)}, u32[]{:S(2)}, u32[]{:S(2)}) collective-permute-start(f32[48,1024]{1,0:T(8,128)S(1)} %get-tuple-element.27), channel_id=1, source_target_pairs={{4,8},{12,16},{20,24},{8,4},{16,12},{24,20},{5,9},{13,17},{21,25},... | collective-permute-start | bytes 589832 | tf_op jit(solution)/shard_map/ppermute | solution.py:22
  17.3 1.5 %inner.1 = (f32[8,384,128]{2,1,0:T(8,128)S(1)}, f32[8,384,128]{2,1,0:T(8,128)S(1)}, f32[8,384,128]{2,1,0:T(8,128)S(1)}, f32[2,4,8,16,128]{4,3,2,1,0:T(8,128)S(1)}, f32[8,16,1024]{2,1,0:T(8,128)S(1)}) custom-call(f32[8,16,1024]{2,1,0:T(8,128)S(1)} %get-tuple-element.25.field, bf16[8,16,1024]{2,1,0:T(8,128)(2,1)S(1)} %get-tuple-element.19.diff.refs_0_, ...), custom_call_target="tpu_custom_call" | custom-call | flops 10485760 | bytes 1048576 | tf_op jit(solution)/shard_map/inner/pallas_call | solution.py:453
  18.8 0.0 collective-permute-done.4.refs_6_
  18.8 4.6 %collective-permute-done.5.refs_7_ = f32[48,1024]{1,0:T(8,128)S(1)} collective-permute-done((f32[48,1024]{1,0:T(8,128)S(1)}, f32[48,1024]{1,0:T(8,128)S(1)}, u32[]{:S(2)}, u32[]{:S(2)}) %collective-permute-start.5) | collective-permute-done | bytes 196640 | tf_op jit(solution)/shard_map/ppermute | solution.py:22
  23.4 2.6 %rim.1 = (f32[8,384,128]{2,1,0:T(8,128)S(1)}, f32[8,384,128]{2,1,0:T(8,128)S(1)}, f32[8,384,128]{2,1,0:T(8,128)S(1)}, f32[2,4,8,16,128]{4,3,2,1,0:T(8,128)S(1)},...) custom-call(bf16[8,16,1024]{2,1,0:T(8,128)(2,1)S(1)} %get-tuple-elem, ...), custom_call_target="tpu_custom_call", output_to_operand_aliasing={{0}: (8, {}), {1}: (9, {}), {2}: (10, {}), {3}: (11, {}), {... | custom-call | tf_op jit(solution)/shard_map/rim/pallas_call | solution.py:463
  26.0 4.4 %collective-permute-start.6 = (f32[4,8,256]{2,1,0:T(8,128)S(1)}, f32[4,8,256]{2,1,0:T(8,128)S(1)}, u32[]{:S(2)}, u32[]{:S(2)}) collective-permute-start(f32[4,8,256]{2,1,0:T(8,128)S(1)} %get-tuple-element.42), channel_id=1, source_target_pairs={{0,1},{1,0},{2,3},{3,2},{4,5},{5,4},{6,7},{7,6},{8,9},{9,8},{10,11... | collective-permute-start | bytes 98312 | tf_op jit(solution)/shard_map/ppermute | solution.py:480
  30.4 0.0 collective-permute-start.7
  30.4 2.4 %collective-permute-start.8 = (f32[4,8,256]{2,1,0:T(8,128)S(1)}, f32[4,8,256]{2,1,0:T(8,128)S(1)}, u32[]{:S(2)}, u32[]{:S(2)}) collective-permute-start(f32[4,8,256]{2,1,0:T(8,128)S(1)} %get-tuple-element.40), channel_id=1, source_target_pairs={{0,3},{1,2},{2,1},{3,0},{4,7},{5,6},{6,5},{7,4},{8,11},{9,10},{10,... | collective-permute-start | bytes 98312 | tf_op jit(solution)/shard_map/ppermute | solution.py:480
  32.9 0.0 collective-permute-done.6
  32.9 2.4 %collective-permute-done.7 = f32[4,8,256]{2,1,0:T(8,128)S(1)} collective-permute-done((f32[4,8,256]{2,1,0:T(8,128)S(1)}, f32[4,8,256]{2,1,0:T(8,128)S(1)}, u32[]{:S(2)}, u32[]{:S(2)}) %collective-permute-start.7) | collective-permute-done | bytes 32800 | tf_op jit(solution)/shard_map/ppermute | solution.py:480
  35.3 0.9 %collective-permute-done.8 = f32[4,8,256]{2,1,0:T(8,128)S(1)} collective-permute-done((f32[4,8,256]{2,1,0:T(8,128)S(1)}, f32[4,8,256]{2,1,0:T(8,128)S(1)}, u32[]{:S(2)}, u32[]{:S(2)}) %collective-permute-start.8) | collective-permute-done | bytes 32800 | tf_op jit(solution)/shard_map/ppermute | solution.py:480
  36.3 0.6 %pad_maximum_fusion.1 = f32[4,8,256]{2,1,0:T(8,128)} fusion(f32[1,8,256]{2,1,0:T(8,128)S(1)} %fusion.6, f32[3,8,256]{2,1,0:T(8,128)S(1)} %fusion.1), kind=kLoop, calls=%fused_computation.1 | loop fusion | flops 8192 | bytes 65536 | tf_op jit(solution)/shard_map/concatenate | solution.py:492
  (5 shorter events, 0.1 us)
Async XLA Ops:
  2.7 10.7 %collective-permute-start = (f32[8,8,1024]{2,1,0:T(8,128)S(1)}, f32[8,8,1024]{2,1,0:T(8,128)S(1)}, u32[]{:S(2)}, u32[]{:S(2)}) collective-permute-start(f32[8,8,1024]{2,1,0:T(8,128)S(1)} %get-tuple-element.21), channel_id=1, source_target_pairs={{0,1},{2,3},{1,0},{3,2},{4,5},{6,7},{5,4},{7,6},{8,9},{10,11},{9,8... | collective-permute-start | bytes 786440 | tf_op jit(solution)/shard_map/ppermute | solution.py:22
  4.3 9.1 %collective-permute-start.1 = (f32[8,8,1024]{2,1,0:T(8,128)S(1)}, f32[8,8,1024]{2,1,0:T(8,128)S(1)}, u32[]{:S(2)}, u32[]{:S(2)}) collective-permute-start(f32[8,8,1024]{2,1,0:T(8,128)S(1)} %get-tuple-element.22), channel_id=1, source_target_pairs={{1,2},{2,1},{5,6},{6,5},{9,10},{10,9},{13,14},{14,13},{17,18},{18,... | collective-permute-start | bytes 786440 | tf_op jit(solution)/shard_map/ppermute | solution.py:22
  5.0 3.5 %collective-permute-start.2 = (f32[2,16,1024]{2,1,0:T(8,128)S(1)}, f32[2,16,1024]{2,1,0:T(8,128)S(1)}, u32[]{:S(2)}, u32[]{:S(2)}) collective-permute-start(f32[2,16,1024]{2,1,0:T(8,128)S(1)} %get-tuple-element.23), channel_id=1, source_target_pairs={{0,4},{8,12},{16,20},{24,28},{4,0},{12,8},{20,16},{28,24},{1,5},{9... | collective-permute-start | bytes 393224 | tf_op jit(solution)/shard_map/ppermute | solution.py:22
  5.1 8.3 %collective-permute-start.3 = (f32[2,16,1024]{2,1,0:T(8,128)S(1)}, f32[2,16,1024]{2,1,0:T(8,128)S(1)}, u32[]{:S(2)}, u32[]{:S(2)}) collective-permute-start(f32[2,16,1024]{2,1,0:T(8,128)S(1)} %get-tuple-element.24), channel_id=1, source_target_pairs={{4,8},{12,16},{20,24},{8,4},{16,12},{24,20},{5,9},{13,17},{21,25},... | collective-permute-start | bytes 393224 | tf_op jit(solution)/shard_map/ppermute | solution.py:22
  14.0 4.7 %collective-permute-start.4 = (f32[48,1024]{1,0:T(8,128)S(1)}, f32[48,1024]{1,0:T(8,128)S(1)}, u32[]{:S(2)}, u32[]{:S(2)}) collective-permute-start(f32[48,1024]{1,0:T(8,128)S(1)} %get-tuple-element.26), channel_id=1, source_target_pairs={{0,4},{8,12},{16,20},{24,28},{4,0},{12,8},{20,16},{28,24},{1,5},{9... | collective-permute-start | bytes 589832 | tf_op jit(solution)/shard_map/ppermute | solution.py:22
  14.1 9.2 %collective-permute-start.5 = (f32[48,1024]{1,0:T(8,128)S(1)}, f32[48,1024]{1,0:T(8,128)S(1)}, u32[]{:S(2)}, u32[]{:S(2)}) collective-permute-start(f32[48,1024]{1,0:T(8,128)S(1)} %get-tuple-element.27), channel_id=1, source_target_pairs={{4,8},{12,16},{20,24},{8,4},{16,12},{24,20},{5,9},{13,17},{21,25},... | collective-permute-start | bytes 589832 | tf_op jit(solution)/shard_map/ppermute | solution.py:22
  26.0 6.9 %collective-permute-start.6 = (f32[4,8,256]{2,1,0:T(8,128)S(1)}, f32[4,8,256]{2,1,0:T(8,128)S(1)}, u32[]{:S(2)}, u32[]{:S(2)}) collective-permute-start(f32[4,8,256]{2,1,0:T(8,128)S(1)} %get-tuple-element.42), channel_id=1, source_target_pairs={{0,1},{1,0},{2,3},{3,2},{4,5},{5,4},{6,7},{7,6},{8,9},{9,8},{10,11... | collective-permute-start | bytes 98312 | tf_op jit(solution)/shard_map/ppermute | solution.py:480
  30.4 4.8 %collective-permute-start.7 = (f32[4,8,256]{2,1,0:T(8,128)S(1)}, f32[4,8,256]{2,1,0:T(8,128)S(1)}, u32[]{:S(2)}, u32[]{:S(2)}) collective-permute-start(f32[4,8,256]{2,1,0:T(8,128)S(1)} %get-tuple-element.41), channel_id=1, source_target_pairs={{0,2},{1,3},{2,0},{3,1},{4,6},{5,7},{6,4},{7,5},{8,10},{9,11},{10,... | collective-permute-start | bytes 98312 | tf_op jit(solution)/shard_map/ppermute | solution.py:480
  30.4 5.7 %collective-permute-start.8 = (f32[4,8,256]{2,1,0:T(8,128)S(1)}, f32[4,8,256]{2,1,0:T(8,128)S(1)}, u32[]{:S(2)}, u32[]{:S(2)}) collective-permute-start(f32[4,8,256]{2,1,0:T(8,128)S(1)} %get-tuple-element.40), channel_id=1, source_target_pairs={{0,3},{1,2},{2,1},{3,0},{4,7},{5,6},{6,5},{7,4},{8,11},{9,10},{10,... | collective-permute-start | bytes 98312 | tf_op jit(solution)/shard_map/ppermute | solution.py:480

commit v3 on v2

--- a/solution.py
+++ b/solution.py
@@ -64,7 +64,7 @@
 
 
 def pack_kernel(
-    field_far, diff_far, vel_far, field, diff, vel, even_d, odd_d, even_r, odd_r, flat, coefs, sems
+    field_far, diff_far, vel_far, field, diff, vel, even_d, odd_d, odd_r, even_r, flat, coefs, sems
 ):
     loads = [
         pltpu.make_async_copy(source, target, sems.at[i])
@@ -77,13 +77,14 @@
     for load in loads:
         load.wait()
     rows, depth, width = field.shape
+    pitch = depth + 4
     count = width // lanes
     depth_odd = lax.axis_index("depth") % 2 == 1
     rows_odd = lax.axis_index("rows") % 2 == 1
 
     for c in range(count):
         for r in range(rows):
-            place = pl.ds(r * depth, depth)
+            place = pl.ds(r * pitch, depth)
             coef = coef_of(diff, vel, r, c)
             flat[c, place, :] = field[r, :, cols(c)]
             for i in range(4):
@@ -101,7 +102,7 @@
     for near, step in ((0, 1), (depth - 1, -1)):
 
         def slab(ref, d):
-            return [ref[c, pl.ds(d, rows, stride=depth), :] for c in range(count)]
+            return [ref[c, pl.ds(d, rows, stride=pitch), :] for c in range(count)]
 
         u0, u1, u2 = (slab(flat, near + step * j) for j in range(3))
         near_coef = [slab(coefs.at[i], near) for i in range(4)]
@@ -134,7 +135,7 @@
 
 
 def edge_kernel(
-    field, diff, vel, even_d, odd_d, even_r, odd_r, even_2, odd_2, middles, ext, edge
+    field, diff, vel, even_d, odd_d, odd_r, even_r, odd_2, even_2, middles, ext, edge
 ):
     rows, depth, width = field.shape
     every = range(width // lanes)
@@ -215,7 +216,7 @@
 class Block:
     def __init__(self, rows, depth, width):
         self.rows, self.depth, self.every = rows, depth, range(width // lanes)
-        self.pitch = depth + 2 * margin
+        self.pitch = depth + 2 * margin + 1
 
     def at(self, r, d):
         return (r + 2) * self.pitch + margin + d
@@ -256,7 +257,7 @@
 
 
 def inner_kernel(
-    field, diff, vel, even_d, odd_d, even_r, odd_r, middles, first, second, third, slabs, front
+    field, diff, vel, even_d, odd_d, odd_r, even_r, middles, first, second, third, slabs, front
 ):
     rows, depth, width = field.shape
     block = Block(rows, depth, width)
@@ -302,7 +303,7 @@
 
 
 def rim_kernel(
-    opacity, diff, vel, even_d, odd_d, even_r, odd_r, even_2, odd_2, *refs
+    opacity, diff, vel, even_d, odd_d, odd_r, even_r, odd_2, even_2, *refs
 ):
     first, second, third, slabs, front, front_far, partial, sem = refs[5:]
     rows, depth, width = front.shape
@@ -366,10 +367,9 @@
         block.put(third, block.across(0, d, rows), values)
 
     def shine(d, carry):
-        center = block.slab(third, 0, d, rows)
+        shallow, center, deep = planes[d], planes[d + 1], planes[d + 2]
         before, after = beside(center)
         above, below = block.slab(third, -1, d, rows), block.slab(third, 1, d, rows)
-        shallow, deep = block.slab(third, 0, d - 1, rows), block.slab(third, 0, d + 1, rows)
         result = []
         for c in every:
             through, total, red, green = carry[c]
@@ -388,7 +388,9 @@
 
     zero, one = jnp.zeros((rows, lanes), jnp.float32), jnp.ones((rows, lanes), jnp.float32)
     carry = tuple((one, zero, zero, zero) for _ in every)
+    planes = [block.slab(third, 0, -1, rows), block.slab(third, 0, 0, rows)]
     for d in range(depth):
+        planes.append(block.slab(third, 0, d + 1, rows))
         carry = shine(d, carry)
     for c, (through, total, red, green) in enumerate(carry):
         partial[0, :, cols(c)] = red
@@ -419,13 +421,13 @@
     in_hbm = pl.BlockSpec(memory_space=pltpu.HBM)
 
     own_types = [pltpu.VMEM(x.shape, x.dtype) for x in (field, diffusivity, velocity)]
-    *own, even_d, odd_d, even_r, odd_r = pl.pallas_call(
+    *own, even_d, odd_d, odd_r, even_r = pl.pallas_call(
         pack_kernel,
         in_specs=[in_hbm] * 3,
         out_shape=own_types + [vmem((8, rows, width))] * 2 + [vmem((2, depth, width))] * 2,
         scratch_shapes=[
-            vmem((count, rows * depth, lanes)),
-            vmem((4, count, rows * depth, lanes)),
+            vmem((count, rows * (depth + 4), lanes)),
+            vmem((4, count, rows * (depth + 4), lanes)),
             pltpu.SemaphoreType.DMA((3,)),
         ],
         compiler_params=params,
@@ -436,19 +438,19 @@
     odd_d = here(swap_pairs(odd_d, "depth", 1))
     even_r = here(swap_pairs(even_r, "rows", 0))
     own = [here(x) for x in own]
-    even_2, odd_2, middles = pl.pallas_call(
+    odd_2, even_2, middles = pl.pallas_call(
         edge_kernel,
         out_shape=[vmem((2 * depth + 16, width))] * 2 + [vmem((4, depth, width))],
         scratch_shapes=[
-            vmem((4, count, block.pitch, lanes)),
-            vmem((2, count, block.pitch, lanes)),
+            vmem((4, count, depth + 2 * margin, lanes)),
+            vmem((2, count, depth + 2 * margin, lanes)),
         ],
         compiler_params=params,
         name="edge",
-    )(*own, even_d, odd_d, even_r, odd_r)
+    )(*own, even_d, odd_d, odd_r, even_r)
+    odd_2 = here(swap_pairs(odd_2, "rows", 1))
     even_2 = here(swap_pairs(even_2, "rows", 0))
-    odd_2 = here(swap_pairs(odd_2, "rows", 1))
-    held = [vmem((count, (rows + 4) * block.pitch, lanes))] * 3
+    held = [vmem((count, (rows + 4) * block.pitch + margin, lanes))] * 3
     held += [vmem((2, 4, count, rows + 8, lanes)), vmem(field.shape)]
     state = pl.pallas_call(
         inner_kernel,
@@ -458,7 +460,7 @@
             flops=80 * field.size, bytes_accessed=8 * field.size, transcendentals=0
         ),
         name="inner",
-    )(*own, even_d, odd_d, even_r, odd_r, here(middles))
+    )(*own, even_d, odd_d, odd_r, even_r, here(middles))
     opacity = opacity_total / (depth * groups)
     *_, front, partial = pl.pallas_call(
         lambda *refs: rim_kernel(opacity, *refs),
@@ -469,20 +471,21 @@
         input_output_aliases={8 + i: i for i in range(5)},
         compiler_params=params,
         name="rim",
-    )(*own[1:], even_d, odd_d, even_r, odd_r, even_2, odd_2, *[here(x) for x in state])
+    )(*own[1:], even_d, odd_d, odd_r, even_r, odd_2, even_2, *[here(x) for x in state])
 
     position = lax.axis_index("depth")
     split = partial.reshape(4, rows, groups, width // groups)
-    parts = []
+    parts = {}
     for apart in range(groups):
         part = lax.dynamic_index_in_dim(split, position ^ apart, 2, keepdims=False)
         if apart:
             part = lax.ppermute(part, "depth", [(i, i ^ apart) for i in range(groups)])
-        parts.append(part)
-    parts = jnp.stack(parts)
+        parts[apart] = part
+    parts = jnp.stack([parts[-apart % groups] for apart in range(groups)])
     picture = None
     for s in range(groups):
-        segment = lax.dynamic_index_in_dim(parts, position ^ s, 0, keepdims=False)
+        apart = position ^ s
+        segment = lax.dynamic_index_in_dim(parts, -apart % groups, 0, keepdims=False)
         if picture is None:
             colors, through = segment[:3], segment[3:]
             picture = (colors, through)

time: 37 us -> 33.4 us (0.903)
  Pallas kernels: 6.79 us -> 5.09 us
  waiting for transfers between devices: 12.7 us -> 11.6 us
  starting transfers between devices: 15.9 us -> 15.1 us
    ppermute x6, waiting for transfers between devices: 9.44 us -> 7.72 us  [swap_pairs(): return lax.ppermute(value, axis, pairs(lax.axis_size(axis), first))]
    pallas_call x1, Pallas kernels: 2.59 us -> 1.32 us  [shards(): pl.pallas_call(lambda *refs: rim_kernel(opacity, *refs), out_shape=held +...]
    ppermute x3, starting transfers between devices: 6.89 us -> 5.91 us  [shards(): part = lax.ppermute(part, 'depth', [(i, i ^ apart) for i in range(groups)])]
    ppermute x3, waiting for transfers between devices: 3.27 us -> 3.91 us  [shards(): part = lax.ppermute(part, 'depth', [(i, i ^ apart) for i in range(groups)])]
where the time goes in v3:
time: 33.4 us; the launch traced here: 33.2 us
  starting transfers between devices  15.1 us (45%)
  waiting for transfers between devices  11.6 us (35%)
  Pallas kernels  5.09 us (15%)
  between operations  0.73 us (2%)
  other arithmetic  0.68 us (2%)
    ppermute x6, starting transfers between devices, swap_pairs(): return lax.ppermute(value, axis, pairs(lax.axis_size(axis), first))  9.15 us
    ppermute x6, waiting for transfers between devices, swap_pairs(): return lax.ppermute(value, axis, pairs(lax.axis_size(axis), first))  7.72 us
    ppermute x3, starting transfers between devices, shards(): part = lax.ppermute(part, 'depth', [(i, i ^ apart) for i in range(groups)])  5.91 us
    ppermute x3, waiting for transfers between devices, shards(): part = lax.ppermute(part, 'depth', [(i, i ^ apart) for i in range(groups)])  3.91 us
    pallas_call x1, Pallas kernels, shards(): pl.pallas_call(pack_kernel, in_specs=[in_hbm] * 3, out_shape=own_types +...  1.78 us
    pallas_call x1, Pallas kernels, shards(): pl.pallas_call(lambda *refs: rim_kernel(opacity, *refs), out_shape=held +...  1.32 us
    pallas_call x1, Pallas kernels, shards(): pl.pallas_call(inner_kernel, out_shape=held, compiler_params=params, cost...  1.32 us
    pallas_call x1, Pallas kernels, shards(): pl.pallas_call(edge_kernel, out_shape=[vmem((2 * depth + 16, width))] * 2...  0.68 us
  transfers between devices with their start and end apart: 9, of which 4 were waited for; matrix products, arithmetic and copies ran while one was open for 0% of the time, Pallas kernels for 4%

profile of v3, /device:TPU:4, one launch (start us, length us, event | category | flops | bytes accessed | tf_op | source)
XLA Modules:
  0.0 33.2 jit_solution(12582671995283470519)
XLA Ops:
  0.6 1.8 %pack.1 = (f32[8,16,1024]{2,1,0:T(8,128)S(1)}, bf16[8,16,1024]{2,1,0:T(8,128)(2,1)S(1)}, bf16[3,8,16,1024]{3,2,1,0:T(8,128)(2,1)S(1)}, f32[8,8,1024]{2,1,0:T(8,1...) custom-call(f32[8,16,1024]{2,1,0:T(8,128)} %field_far.1, ...), custom_call_target="tpu_custom_call" | custom-call | tf_op jit(solution)/shard_map/pack/pallas_call | solution.py:424
  2.4 1.6 %collective-permute-start = (f32[8,8,1024]{2,1,0:T(8,128)S(1)}, f32[8,8,1024]{2,1,0:T(8,128)S(1)}, u32[]{:S(2)}, u32[]{:S(2)}) collective-permute-start(f32[8,8,1024]{2,1,0:T(8,128)S(1)} %get-tuple-element.21), channel_id=1, source_target_pairs={{0,1},{2,3},{1,0},{3,2},{4,5},{6,7},{5,4},{7,6},{8,9},{10,11},{9,8... | collective-permute-start | bytes 786440 | tf_op jit(solution)/shard_map/ppermute | solution.py:22
  4.1 0.7 %collective-permute-start.1 = (f32[8,8,1024]{2,1,0:T(8,128)S(1)}, f32[8,8,1024]{2,1,0:T(8,128)S(1)}, u32[]{:S(2)}, u32[]{:S(2)}) collective-permute-start(f32[8,8,1024]{2,1,0:T(8,128)S(1)} %get-tuple-element.22), channel_id=1, source_target_pairs={{1,2},{2,1},{5,6},{6,5},{9,10},{10,9},{13,14},{14,13},{17,18},{18,... | collective-permute-start | bytes 786440 | tf_op jit(solution)/shard_map/ppermute | solution.py:22
  4.7 2.5 %collective-permute-start.2 = (f32[2,16,1024]{2,1,0:T(8,128)S(1)}, f32[2,16,1024]{2,1,0:T(8,128)S(1)}, u32[]{:S(2)}, u32[]{:S(2)}) collective-permute-start(f32[2,16,1024]{2,1,0:T(8,128)S(1)} %get-tuple-element.23), channel_id=1, source_target_pairs={{4,8},{12,16},{20,24},{8,4},{16,12},{24,20},{5,9},{13,17},{21,25},... | collective-permute-start | bytes 393224 | tf_op jit(solution)/shard_map/ppermute | solution.py:22
  7.2 1.1 %collective-permute-start.3 = (f32[2,16,1024]{2,1,0:T(8,128)S(1)}, f32[2,16,1024]{2,1,0:T(8,128)S(1)}, u32[]{:S(2)}, u32[]{:S(2)}) collective-permute-start(f32[2,16,1024]{2,1,0:T(8,128)S(1)} %get-tuple-element.24), channel_id=1, source_target_pairs={{0,4},{8,12},{16,20},{24,28},{4,0},{12,8},{20,16},{28,24},{1,5},{9... | collective-permute-start | bytes 393224 | tf_op jit(solution)/shard_map/ppermute | solution.py:22
  8.3 4.1 %collective-permute-done.2.odd_r.refs_4_ = f32[2,16,1024]{2,1,0:T(8,128)S(1)} collective-permute-done((f32[2,16,1024]{2,1,0:T(8,128)S(1)}, f32[2,16,1024]{2,1,0:T(8,128)S(1)}, u32[]{:S(2)}, u32[]{:S(2)}) %collective-permute-start.2) | collective-permute-done | bytes 131104 | tf_op jit(solution)/shard_map/ppermute | solution.py:22
  12.4 0.0 collective-permute-done.3.even_r.refs_5_
  12.4 0.0 collective-permute-done.even_d.refs_2_
  12.4 0.0 collective-permute-done.1.odd_d.refs_3_
  12.4 0.7 %edge.1 = (f32[48,1024]{1,0:T(8,128)S(1)}, f32[48,1024]{1,0:T(8,128)S(1)}, f32[4,16,1024]{2,1,0:T(8,128)S(1)}) custom-call(f32[8,16,1024]{2,1,0:T(8,128)S(1)} %get-tuple-element.25.field, bf16[8,16,1024]{2,1,0:T(8,128)(2,1)S(1)} %get-tuple-element.19.diff.refs_0_, bf16[3,8,16,1024]{3,2,1,0:T(8,128)(2,1)S(1)} %get-tuple-element.20.vel.refs_1_, ...), custom_call_target="tpu_custom_call" | custom-call | tf_op jit(solution)/shard_map/edge/pallas_call | solution.py:441
  13.1 3.1 %collective-permute-start.4 = (f32[48,1024]{1,0:T(8,128)S(1)}, f32[48,1024]{1,0:T(8,128)S(1)}, u32[]{:S(2)}, u32[]{:S(2)}) collective-permute-start(f32[48,1024]{1,0:T(8,128)S(1)} %get-tuple-element.26), channel_id=1, source_target_pairs={{4,8},{12,16},{20,24},{8,4},{16,12},{24,20},{5,9},{13,17},{21,25},... | collective-permute-start | bytes 589832 | tf_op jit(solution)/shard_map/ppermute | solution.py:22
  16.2 0.2 collective-permute-start.5
  16.4 1.3 %inner.1 = (f32[8,404,128]{2,1,0:T(8,128)S(1)}, f32[8,404,128]{2,1,0:T(8,128)S(1)}, f32[8,404,128]{2,1,0:T(8,128)S(1)}, f32[2,4,8,16,128]{4,3,2,1,0:T(8,128)S(1)}, f32[8,16,1024]{2,1,0:T(8,128)S(1)}) custom-call(f32[8,16,1024]{2,1,0:T(8,128)S(1)} %get-tuple-element.25.field, bf16[8,16,1024]{2,1,0:T(8,128)(2,1)S(1)} %get-tuple-element.19.diff.refs_0_, ...), custom_call_target="tpu_custom_call" | custom-call | flops 10485760 | bytes 1048576 | tf_op jit(solution)/shard_map/inner/pallas_call | solution.py:455
  17.7 3.6 %collective-permute-done.4.refs_6_ = f32[48,1024]{1,0:T(8,128)S(1)} collective-permute-done((f32[48,1024]{1,0:T(8,128)S(1)}, f32[48,1024]{1,0:T(8,128)S(1)}, u32[]{:S(2)}, u32[]{:S(2)}) %collective-permute-start.4) | collective-permute-done | bytes 196640 | tf_op jit(solution)/shard_map/ppermute | solution.py:22
  21.3 0.0 collective-permute-done.5.refs_7_
  21.3 1.3 %rim.1 = (f32[8,404,128]{2,1,0:T(8,128)S(1)}, f32[8,404,128]{2,1,0:T(8,128)S(1)}, f32[8,404,128]{2,1,0:T(8,128)S(1)}, f32[2,4,8,16,128]{4,3,2,1,0:T(8,128)S(1)},...) custom-call(bf16[8,16,1024]{2,1,0:T(8,128)(2,1)S(1)} %get-tuple-elem, ...), custom_call_target="tpu_custom_call", output_to_operand_aliasing={{0}: (8, {}), {1}: (9, {}), {2}: (10, {}), {3}: (11, {}), {... | custom-call | tf_op jit(solution)/shard_map/rim/pallas_call | solution.py:465
  22.7 2.8 %collective-permute-start.6 = (f32[4,8,256]{2,1,0:T(8,128)S(1)}, f32[4,8,256]{2,1,0:T(8,128)S(1)}, u32[]{:S(2)}, u32[]{:S(2)}) collective-permute-start(f32[4,8,256]{2,1,0:T(8,128)S(1)} %get-tuple-element.42), channel_id=1, source_target_pairs={{0,3},{1,2},{2,1},{3,0},{4,7},{5,6},{6,5},{7,4},{8,11},{9,10},{10,... | collective-permute-start | bytes 98312 | tf_op jit(solution)/shard_map/ppermute | solution.py:482
  25.5 3.1 %collective-permute-start.7 = (f32[4,8,256]{2,1,0:T(8,128)S(1)}, f32[4,8,256]{2,1,0:T(8,128)S(1)}, u32[]{:S(2)}, u32[]{:S(2)}) collective-permute-start(f32[4,8,256]{2,1,0:T(8,128)S(1)} %get-tuple-element.41), channel_id=1, source_target_pairs={{0,2},{1,3},{2,0},{3,1},{4,6},{5,7},{6,4},{7,5},{8,10},{9,11},{10,... | collective-permute-start | bytes 98312 | tf_op jit(solution)/shard_map/ppermute | solution.py:482
  28.6 0.0 collective-permute-start.8
  28.6 0.0 collective-permute-done.6
  28.6 2.2 %collective-permute-done.7 = f32[4,8,256]{2,1,0:T(8,128)S(1)} collective-permute-done((f32[4,8,256]{2,1,0:T(8,128)S(1)}, f32[4,8,256]{2,1,0:T(8,128)S(1)}, u32[]{:S(2)}, u32[]{:S(2)}) %collective-permute-start.7) | collective-permute-done | bytes 32800 | tf_op jit(solution)/shard_map/ppermute | solution.py:482
  30.8 1.7 %collective-permute-done.8 = f32[4,8,256]{2,1,0:T(8,128)S(1)} collective-permute-done((f32[4,8,256]{2,1,0:T(8,128)S(1)}, f32[4,8,256]{2,1,0:T(8,128)S(1)}, u32[]{:S(2)}, u32[]{:S(2)}) %collective-permute-start.8) | collective-permute-done | bytes 32800 | tf_op jit(solution)/shard_map/ppermute | solution.py:482
  32.6 0.6 %pad_maximum_fusion.1 = f32[4,8,256]{2,1,0:T(8,128)} fusion(f32[1,8,256]{2,1,0:T(8,128)S(1)} %fusion.6, f32[3,8,256]{2,1,0:T(8,128)S(1)} %fusion.1), kind=kLoop, calls=%fused_computation.1 | loop fusion | flops 8192 | bytes 65536 | tf_op jit(solution)/shard_map/concatenate | solution.py:495
  (5 shorter events, 0.1 us)
Async XLA Ops:
  2.4 10.0 %collective-permute-start = (f32[8,8,1024]{2,1,0:T(8,128)S(1)}, f32[8,8,1024]{2,1,0:T(8,128)S(1)}, u32[]{:S(2)}, u32[]{:S(2)}) collective-permute-start(f32[8,8,1024]{2,1,0:T(8,128)S(1)} %get-tuple-element.21), channel_id=1, source_target_pairs={{0,1},{2,3},{1,0},{3,2},{4,5},{6,7},{5,4},{7,6},{8,9},{10,11},{9,8... | collective-permute-start | bytes 786440 | tf_op jit(solution)/shard_map/ppermute | solution.py:22
  4.1 8.4 %collective-permute-start.1 = (f32[8,8,1024]{2,1,0:T(8,128)S(1)}, f32[8,8,1024]{2,1,0:T(8,128)S(1)}, u32[]{:S(2)}, u32[]{:S(2)}) collective-permute-start(f32[8,8,1024]{2,1,0:T(8,128)S(1)} %get-tuple-element.22), channel_id=1, source_target_pairs={{1,2},{2,1},{5,6},{6,5},{9,10},{10,9},{13,14},{14,13},{17,18},{18,... | collective-permute-start | bytes 786440 | tf_op jit(solution)/shard_map/ppermute | solution.py:22
  4.7 7.7 %collective-permute-start.2 = (f32[2,16,1024]{2,1,0:T(8,128)S(1)}, f32[2,16,1024]{2,1,0:T(8,128)S(1)}, u32[]{:S(2)}, u32[]{:S(2)}) collective-permute-start(f32[2,16,1024]{2,1,0:T(8,128)S(1)} %get-tuple-element.23), channel_id=1, source_target_pairs={{4,8},{12,16},{20,24},{8,4},{16,12},{24,20},{5,9},{13,17},{21,25},... | collective-permute-start | bytes 393224 | tf_op jit(solution)/shard_map/ppermute | solution.py:22
  7.2 5.2 %collective-permute-start.3 = (f32[2,16,1024]{2,1,0:T(8,128)S(1)}, f32[2,16,1024]{2,1,0:T(8,128)S(1)}, u32[]{:S(2)}, u32[]{:S(2)}) collective-permute-start(f32[2,16,1024]{2,1,0:T(8,128)S(1)} %get-tuple-element.24), channel_id=1, source_target_pairs={{0,4},{8,12},{16,20},{24,28},{4,0},{12,8},{20,16},{28,24},{1,5},{9... | collective-permute-start | bytes 393224 | tf_op jit(solution)/shard_map/ppermute | solution.py:22
  13.1 8.2 %collective-permute-start.4 = (f32[48,1024]{1,0:T(8,128)S(1)}, f32[48,1024]{1,0:T(8,128)S(1)}, u32[]{:S(2)}, u32[]{:S(2)}) collective-permute-start(f32[48,1024]{1,0:T(8,128)S(1)} %get-tuple-element.26), channel_id=1, source_target_pairs={{4,8},{12,16},{20,24},{8,4},{16,12},{24,20},{5,9},{13,17},{21,25},... | collective-permute-start | bytes 589832 | tf_op jit(solution)/shard_map/ppermute | solution.py:22
  16.2 5.1 %collective-permute-start.5 = (f32[48,1024]{1,0:T(8,128)S(1)}, f32[48,1024]{1,0:T(8,128)S(1)}, u32[]{:S(2)}, u32[]{:S(2)}) collective-permute-start(f32[48,1024]{1,0:T(8,128)S(1)} %get-tuple-element.27), channel_id=1, source_target_pairs={{0,4},{8,12},{16,20},{24,28},{4,0},{12,8},{20,16},{28,24},{1,5},{9... | collective-permute-start | bytes 589832 | tf_op jit(solution)/shard_map/ppermute | solution.py:22
  22.7 5.9 %collective-permute-start.6 = (f32[4,8,256]{2,1,0:T(8,128)S(1)}, f32[4,8,256]{2,1,0:T(8,128)S(1)}, u32[]{:S(2)}, u32[]{:S(2)}) collective-permute-start(f32[4,8,256]{2,1,0:T(8,128)S(1)} %get-tuple-element.42), channel_id=1, source_target_pairs={{0,3},{1,2},{2,1},{3,0},{4,7},{5,6},{6,5},{7,4},{8,11},{9,10},{10,... | collective-permute-start | bytes 98312 | tf_op jit(solution)/shard_map/ppermute | solution.py:482
  25.5 5.3 %collective-permute-start.7 = (f32[4,8,256]{2,1,0:T(8,128)S(1)}, f32[4,8,256]{2,1,0:T(8,128)S(1)}, u32[]{:S(2)}, u32[]{:S(2)}) collective-permute-start(f32[4,8,256]{2,1,0:T(8,128)S(1)} %get-tuple-element.41), channel_id=1, source_target_pairs={{0,2},{1,3},{2,0},{3,1},{4,6},{5,7},{6,4},{7,5},{8,10},{9,11},{10,... | collective-permute-start | bytes 98312 | tf_op jit(solution)/shard_map/ppermute | solution.py:482
  28.6 3.9 %collective-permute-start.8 = (f32[4,8,256]{2,1,0:T(8,128)S(1)}, f32[4,8,256]{2,1,0:T(8,128)S(1)}, u32[]{:S(2)}, u32[]{:S(2)}) collective-permute-start(f32[4,8,256]{2,1,0:T(8,128)S(1)} %get-tuple-element.40), channel_id=1, source_target_pairs={{0,1},{1,0},{2,3},{3,2},{4,5},{5,4},{6,7},{7,6},{8,9},{9,8},{10,11... | collective-permute-start | bytes 98312 | tf_op jit(solution)/shard_map/ppermute | solution.py:482

commit v4 on v3

v4 whole, which is shorter than its diff:
```python
import jax
import jax.numpy as jnp
from jax import lax
from jax.experimental import pallas as pl
from jax.experimental.pallas import tpu as pltpu
from jax.sharding import PartitionSpec as P

time_step = 0.2
growth_rate = 1.0
opacity_total = 3.0

lanes = 128
margin = 8
pack_gap = 4


def pairs(count, first):
    forward = [(i, i + 1) for i in range(first, count - 1, 2)]
    return forward + [(target, source) for source, target in forward]


def swap_pairs(value, axis, first):
    return lax.ppermute(value, axis, pairs(lax.axis_size(axis), first))


def stencil(u, low, high, coef):
    diff = coef[0]
    change = growth_rate * u * (1.0 - u)
    for before, after, speed in zip(low, high, coef[1:]):
        change = change + (diff + jnp.maximum(speed, 0.0)) * (before - u)
        change = change + (diff - jnp.minimum(speed, 0.0)) * (after - u)
    return u + time_step * change


def beside(chunks):
    lane = lax.broadcasted_iota(jnp.int32, chunks[0].shape, 1)
    right = [pltpu.roll(x, 1, 1) for x in chunks]
    left = [pltpu.roll(x, lanes - 1, 1) for x in chunks]
    zero = jnp.zeros_like(chunks[0])
    count = len(chunks)
    before = [jnp.where(lane == 0, right[c - 1] if c else zero, right[c]) for c in range(count)]
    after = [
        jnp.where(lane == lanes - 1, left[c + 1] if c + 1 < count else zero, left[c])
        for c in range(count)
    ]
    return before, after


def cols(c):
    return slice(c * lanes, (c + 1) * lanes)


def coef_of(diff, vel, r, c):
    return [diff[r, :, cols(c)].astype(jnp.float32)] + [
        vel[i, r, :, cols(c)].astype(jnp.float32) for i in range(3)
    ]


def weight_low(diff, speed):
    return time_step * (diff + jnp.maximum(speed, 0.0))


def weight_high(diff, speed):
    return time_step * (diff - jnp.minimum(speed, 0.0))


def pack_kernel(
    field_far, diff_far, vel_far, field, diff, vel, even_d, odd_d, odd_f, near, flat, coefs, sems
):
    loads = [
        pltpu.make_async_copy(source, target, sems.at[i])
        for i, (source, target) in enumerate(
            ((field_far, field), (diff_far, diff), (vel_far, vel))
        )
    ]
    for load in loads:
        load.start()
    for load in loads:
        load.wait()
    rows, depth, width = field.shape
    count = width // lanes
    pitch = depth + pack_gap
    depth_odd = lax.axis_index("depth") % 2 == 1
    rows_odd = lax.axis_index("rows") % 2 == 1

    for c in range(count):
        for r in range(rows):
            place = pl.ds(r * pitch, depth)
            coef = coef_of(diff, vel, r, c)
            flat[c, place, :] = field[r, :, cols(c)]
            for i in range(4):
                coefs[i, c, place, :] = coef[i]
        first, last = field[0, :, cols(c)], field[rows - 1, :, cols(c)]
        odd_f[:, cols(c)] = jnp.where(rows_odd, last, first)

    row = lax.broadcasted_iota(jnp.int32, (rows, lanes), 0)
    sides = []
    for k, start, step in ((0, 0, 1), (1, depth - 1, -1)):

        def slab(ref, d):
            return [ref[c, pl.ds(d, rows, stride=pitch), :] for c in range(count)]

        u0, u1, u2 = (slab(flat, start + step * j) for j in range(3))
        near_coef = [slab(coefs.at[i], start) for i in range(4)]
        next_coef = [slab(coefs.at[i], start + step) for i in range(4)]
        before, after = beside(u1)
        side = []
        for c in range(count):
            near[k, :, cols(c)] = u0[c]
            above, below = past_rows(u1[c], row)
            deep = (u0[c], u2[c]) if step > 0 else (u2[c], u0[c])
            coef = [next_coef[i][c] for i in range(4)]
            middle = stencil(
                u1[c], (above, deep[0], before[c]), (below, deep[1], after[c]), coef
            )
            weight = row_weight(row, coef)
            side.append([u0[c], u1[c]] + [near_coef[i][c] for i in range(4)] + [middle, weight])
        sides.append(side)
    low, high = sides
    for c in range(count):
        for i in range(8):
            even_d[i, :, cols(c)] = jnp.where(depth_odd, low[c][i], high[c][i])
            odd_d[i, :, cols(c)] = jnp.where(depth_odd, high[c][i], low[c][i])


def spare_kernel(field, diff, vel, odd_x, even_x, partial, own_w, own_d, ext):
    rows, depth, width = field.shape
    every = range(width // lanes)
    rows_odd = lax.axis_index("rows") % 2 == 1
    own = pl.ds(margin, depth)
    shallow, deep = pl.ds(margin - 1, depth), pl.ds(margin + 1, depth)
    none = jnp.zeros((depth, lanes), jnp.float32)
    zero = jnp.zeros((1, lanes), jnp.float32)
    for j, r in enumerate((0, 1, rows - 2, rows - 1)):
        u = [field[r, :, cols(c)] for c in every]
        before, after = beside(u)
        for c in every:
            ext[j, c, margin - 1 : margin, :] = zero
            ext[j, c, own, :] = u[c]
            ext[j, c, margin + depth : margin + depth + 1, :] = zero
        for c in every:
            above = field[r - 1, :, cols(c)] if r > 0 else none
            below = field[r + 1, :, cols(c)] if r < rows - 1 else none
            coef = coef_of(diff, vel, r, c)
            partial[j, :, cols(c)] = stencil(
                u[c],
                (above, ext[j, c, shallow, :], before[c]),
                (below, ext[j, c, deep, :], after[c]),
                coef,
            )
            low = weight_low(coef[0], coef[2])[0:1]
            high = weight_high(coef[0], coef[2])[depth - 1 : depth]
            own_d[2 * j : 2 * j + 1, cols(c)] = low
            own_d[2 * j + 1 : 2 * j + 2, cols(c)] = high
            if r == 0:
                own_w[0, :, cols(c)] = weight_low(coef[0], coef[1])
            if r == rows - 1:
                own_w[1, :, cols(c)] = weight_high(coef[0], coef[1])
    for c in every:
        first, last = field[0, :, cols(c)], field[rows - 1, :, cols(c)]
        even_x[:depth, cols(c)] = jnp.where(rows_odd, first, last)
        for start, length, low, high in (
            (0, depth, own_w[0, :, cols(c)], own_w[1, :, cols(c)]),
            (depth, depth, partial[0, :, cols(c)], partial[3, :, cols(c)]),
            (2 * depth, 2, own_d[0:2, cols(c)], own_d[6:8, cols(c)]),
        ):
            even_x[pl.ds(depth + start, length), cols(c)] = jnp.where(rows_odd, low, high)
            odd_x[pl.ds(start, length), cols(c)] = jnp.where(rows_odd, high, low)


def arrived(even, odd, is_odd, index, even_index=None):
    a, b = even[index if even_index is None else even_index], odd[index]
    return jnp.where(is_odd, a, b), jnp.where(is_odd, b, a)


def past_rows(u, row):
    rows = u.shape[0]
    above = jnp.where(row == 0, 0.0, pltpu.roll(u, 1, 0))
    below = jnp.where(row == rows - 1, 0.0, pltpu.roll(u, rows - 1, 0))
    return above, below


def row_weight(row, coef):
    return jnp.where(row == 0, weight_low(coef[0], coef[1]), weight_high(coef[0], coef[1]))


def at_ends(first, last, shape):
    place = lax.broadcasted_iota(jnp.int32, shape, 0)
    return jnp.where(place == 0, first, jnp.where(place == shape[0] - 1, last, 0.0))


def edge_kernel(
    diff, vel, even_d, odd_d, odd_f, even_x, near, partial, own_w, own_d,
    odd_2, even_2, middles, partly, sides, ext, stack,
):
    _, rows, width = even_d.shape
    depth = diff.shape[1]
    every = range(width // lanes)
    depth_odd = lax.axis_index("depth") % 2 == 1
    rows_odd = lax.axis_index("rows") % 2 == 1
    own = pl.ds(margin, depth)
    shallow, deep = pl.ds(margin - 1, depth), pl.ds(margin + 1, depth)
    row = lax.broadcasted_iota(jnp.int32, (rows, lanes), 0)
    none = jnp.zeros((depth, lanes), jnp.float32)
    zero = jnp.zeros((1, lanes), jnp.float32)
    lines = {j: [] for j in range(4)}
    for c in every:
        beyond = arrived(even_x, odd_f, rows_odd, (pl.ds(0, depth), cols(c)))
        for j, r in enumerate((0, 1, rows - 2, rows - 1)):
            value = partial[j, :, cols(c)]
            if j in (0, 3):
                value = value + own_w[j // 3, :, cols(c)] * beyond[j // 3]
            both = arrived(even_d, odd_d, depth_odd, (0, pl.ds(r, 1), cols(c)))
            weights = [own_d[2 * j + k : 2 * j + k + 1, cols(c)] for k in range(2)]
            value = value + at_ends(weights[0] * both[0], weights[1] * both[1], value.shape)
            lines[j].append(value)
            middles[j, :, cols(c)] = value
            if j in (0, 3):
                ext[j // 3, c, margin - 1 : margin, :] = zero
                ext[j // 3, c, own, :] = value
                ext[j // 3, c, margin + depth : margin + depth + 1, :] = zero
    for j, inner, r in ((0, 1, 0), (3, 2, rows - 1)):
        u = lines[j]
        before, after = beside(u)
        for c in every:
            next_row = lines[inner][c]
            above, below = (none, next_row) if r == 0 else (next_row, none)
            partly[j // 3, :, cols(c)] = stencil(
                u[c],
                (above, ext[j // 3, c, shallow, :], before[c]),
                (below, ext[j // 3, c, deep, :], after[c]),
                coef_of(diff, vel, r, c),
            )
    for c in every:
        first, last = partly[0, :, cols(c)], partly[1, :, cols(c)]
        even_2[:depth, cols(c)] = jnp.where(rows_odd, first, last)
        odd_2[:depth, cols(c)] = jnp.where(rows_odd, last, first)

    def came(item, c, k):
        return arrived(even_d, odd_d, depth_odd, (item, slice(None), cols(c)))[k]

    for k in range(2):
        u = [came(0, c, k) for c in every]
        before, after = beside(u)
        for c in every:
            above, below = past_rows(u[c], row)
            here_d, beyond_d = near[k, :, cols(c)], came(1, c, k)
            low_d, high_d = (beyond_d, here_d) if k == 0 else (here_d, beyond_d)
            coef = [came(2 + i, c, k) for i in range(4)]
            sides[k, 0, :, cols(c)] = stencil(
                u[c], (above, low_d, before[c]), (below, high_d, after[c]), coef
            )
            sides[k, 1, :, cols(c)] = row_weight(row, coef)
            values = (u[c], beyond_d, sides[k, 0, :, cols(c)], sides[k, 1, :, cols(c)])
            for j, value in enumerate(values):
                stack[c, pl.ds((4 * k + j) * (rows + 1), rows), :] = value
    for c in every:
        first = stack[c, pl.ds(0, 8, stride=rows + 1), :]
        last = stack[c, pl.ds(rows - 1, 8, stride=rows + 1), :]
        even_2[depth : depth + 8, cols(c)] = jnp.where(rows_odd, first, last)
        odd_2[depth : depth + 8, cols(c)] = jnp.where(rows_odd, last, first)


class Block:
    def __init__(self, rows, depth, width):
        self.rows, self.depth, self.every = rows, depth, range(width // lanes)
        self.pitch = depth + 2 * margin + 1

    def at(self, r, d):
        return (r + 2) * self.pitch + margin + d

    def along(self, r, d=0):
        return pl.ds(self.at(r, d), self.depth)

    def across(self, r, d, length):
        return pl.ds(self.at(r, d), length, stride=self.pitch)

    def line(self, ref, r, d=0):
        return [ref[c, self.along(r, d), :] for c in self.every]

    def slab(self, ref, r, d, length):
        return [ref[c, self.across(r, d, length), :] for c in self.every]

    def put(self, ref, place, values):
        for c in self.every:
            ref[c, place, :] = values[c]

    def section_line(self, ref, r, coef):
        u = self.line(ref, r)
        before, after = beside(u)
        low = (self.line(ref, r - 1), self.line(ref, r, -1), before)
        high = (self.line(ref, r + 1), self.line(ref, r, 1), after)
        return [
            stencil(u[c], [x[c] for x in low], [x[c] for x in high], coef(c)) for c in self.every
        ]

    def section_slab(self, ref, r, d, length, coef):
        u = self.slab(ref, r, d, length)
        before, after = beside(u)
        low = (self.slab(ref, r - 1, d, length), self.slab(ref, r, d - 1, length), before)
        high = (self.slab(ref, r + 1, d, length), self.slab(ref, r, d + 1, length), after)
        return [
            stencil(u[c], [x[c] for x in low], [x[c] for x in high], coef(c)) for c in self.every
        ]


def inner_kernel(
    field, diff, vel, even_d, odd_d, middles, sides,
    second, third, front_far, first, front, sem,
):
    rows, depth, width = field.shape
    block = Block(rows, depth, width)
    depth_odd = lax.axis_index("depth") % 2 == 1
    for c in block.every:
        for r in range(1, rows - 1):
            first[c, block.along(r), :] = field[r, :, cols(c)]
        low, high = arrived(even_d, odd_d, depth_odd, (0, slice(None), cols(c)))
        first[c, block.across(0, -1, rows), :] = low
        first[c, block.across(0, depth, rows), :] = high
        low, high = arrived(even_d, odd_d, depth_odd, (6, slice(None), cols(c)))
        second[c, block.across(0, -2, rows), :] = low
        second[c, block.across(0, depth + 1, rows), :] = high
        second[c, block.across(0, -1, rows), :] = sides[0, 0, :, cols(c)]
        second[c, block.across(0, depth, rows), :] = sides[1, 0, :, cols(c)]
        for j, r in enumerate((0, 1, rows - 2, rows - 1)):
            second[c, block.along(r), :] = middles[j, :, cols(c)]

    def own_middle(r, carry):
        values = block.section_line(first, r, lambda c: coef_of(diff, vel, r, c))
        block.put(second, block.along(r), values)
        return carry

    lax.fori_loop(2, rows - 2, own_middle, 0)

    def own_front(r, carry):
        values = block.section_line(second, r, lambda c: coef_of(diff, vel, r, c))
        block.put(third, block.along(r), values)
        for c in block.every:
            front[r, :, cols(c)] = values[c]
        return carry

    lax.fori_loop(1, rows - 1, own_front, 0)
    within = pl.ds(1, rows - 2)
    save = pltpu.make_async_copy(front.at[within], front_far.at[within], sem)
    save.start()
    save.wait()


def rim_kernel(
    opacity, field, even_d, odd_d, odd_x, even_x, odd_2, even_2, own_w, own_d, middles, partly, sides,
    *refs
):
    second, third, front_far, partial, front, sems = refs[3:]
    rows, depth, width = field.shape
    block = Block(rows, depth, width)
    every = block.every
    depth_odd = lax.axis_index("depth") % 2 == 1
    rows_odd = lax.axis_index("rows") % 2 == 1
    line = (depth, lanes)

    def spare(start, length, c):
        index = (slice(start, start + length), cols(c))
        shifted = (slice(depth + start, depth + start + length), cols(c))
        return arrived(even_x, odd_x, rows_odd, index, shifted)

    def corner(k, j, c):
        place = depth + 4 * k + j
        return arrived(even_2, odd_2, rows_odd, (slice(place, place + 1), cols(c)))

    def cell(ref, c, r, d, value):
        ref[c, pl.ds(block.at(r, d), 1), :] = value

    ends = ((0, 0, -1), (1, depth - 1, depth))
    rims = ((0, 0, -1), (1, rows - 1, rows))

    for c in every:
        weights, parts = spare(0, depth, c), spare(depth, depth, c)
        fronts = arrived(even_2, odd_2, rows_odd, (slice(0, depth), cols(c)))
        along = [spare(2 * depth + k, 1, c) for k in range(2)]
        corners = [[corner(k, j, c) for j in range(4)] for k in range(2)]
        for e, r, past in rims:
            near = [corners[k][0][e] for k in range(2)]
            middle = parts[e] + weights[e] * field[r, :, cols(c)]
            middle = middle + at_ends(along[0][e] * near[0], along[1][e] * near[1], line)
            second[c, block.along(past), :] = middle
            own_ends, past_ends = [], []
            for k, d, beyond in ends:
                index = (slice(r, r + 1), cols(c))
                outside = arrived(even_d, odd_d, depth_odd, (0, *index))[k]
                next_cell = arrived(even_d, odd_d, depth_odd, (6, *index))[k]
                next_weight = arrived(even_d, odd_d, depth_odd, (7, *index))[k]
                _, far_cell, part, weight = (x[e] for x in corners[k])
                past_ends.append(part + weight * outside)
                own_ends.append(sides[k, 0, *index] + sides[k, 1, *index] * near[k])
                cell(second, c, past, beyond, past_ends[k])
                cell(second, c, r, beyond, own_ends[k])
                cell(second, c, r, 2 * beyond - d, next_cell + next_weight * far_cell)
            own_along = [own_d[6 * e + k : 6 * e + k + 1, cols(c)] for k in range(2)]
            value = partly[e, :, cols(c)] + own_w[e, :, cols(c)] * middle
            value = value + at_ends(
                own_along[0] * own_ends[0], own_along[1] * own_ends[1], line
            )
            third[c, block.along(r), :] = value
            front[e, :, cols(c)] = value
            value = fronts[e] + weights[e] * middles[3 * e, :, cols(c)]
            third[c, block.along(past), :] = value + at_ends(
                along[0][e] * past_ends[0], along[1][e] * past_ends[1], line
            )
    saves = [
        pltpu.make_async_copy(front.at[e], front_far.at[r], sems.at[e]) for e, r, past in rims
    ]
    for save in saves:
        save.start()
    for k, d, beyond in ends:
        items = [
            [
                arrived(even_d, odd_d, depth_odd, (2 + i, slice(None), cols(c)))[k]
                for i in range(4)
            ]
            for c in every
        ]
        values = block.section_slab(second, 0, beyond, rows, lambda c: items[c])
        block.put(third, block.across(0, beyond, rows), values)

    def shine(d, carry):
        shallow, center, deep = planes[d], planes[d + 1], planes[d + 2]
        before, after = beside(center)
        above, below = block.slab(third, -1, d, rows), block.slab(third, 1, d, rows)
        result = []
        for c in every:
            through, total, red, green = carry[c]
            u = center[c]
            grad_row = below[c] - above[c]
            grad_deep = deep[c] - shallow[c]
            grad_col = after[c] - before[c]
            lighting = 0.48 * grad_row + 0.64 * grad_deep + 0.6 * grad_col
            magnitude = grad_row * grad_row + grad_deep * grad_deep + grad_col * grad_col + 0.4
            shade = 0.35 + 0.65 * lighting * lighting / magnitude
            passed = jnp.exp(-opacity * u)
            weight = through * (1.0 - passed) * shade
            colored = weight * u
            result.append((through * passed, total + weight, red + colored, green + colored * u))
        return tuple(result)

    zero, one = jnp.zeros((rows, lanes), jnp.float32), jnp.ones((rows, lanes), jnp.float32)
    carry = tuple((one, zero, zero, zero) for _ in every)
    planes = [block.slab(third, 0, -1, rows), block.slab(third, 0, 0, rows)]
    for d in range(depth):
        planes.append(block.slab(third, 0, d + 1, rows))
        carry = shine(d, carry)
    for c, (through, total, red, green) in enumerate(carry):
        partial[0, :, cols(c)] = red
        partial[1, :, cols(c)] = green
        partial[2, :, cols(c)] = total - red
        partial[3, :, cols(c)] = through
    for save in saves:
        save.wait()


def vmem(shape):
    return pltpu.VMEM(shape, jnp.float32)


def here(value):
    return pltpu.with_memory_space_constraint(value, pltpu.VMEM)


def far(value):
    return pltpu.with_memory_space_constraint(value, pltpu.HBM)


def shards(field, diffusivity, velocity):
    rows, depth, width = field.shape
    count = width // lanes
    block = Block(rows, depth, width)
    groups = lax.axis_size("depth")
    params = pltpu.CompilerParams(vmem_limit_bytes=24 * 2**20)
    in_hbm = pl.BlockSpec(memory_space=pltpu.HBM)

    own_types = [pltpu.VMEM(x.shape, x.dtype) for x in (field, diffusivity, velocity)]
    *own, even_d, odd_d, odd_f, near = pl.pallas_call(
        pack_kernel,
        in_specs=[in_hbm] * 3,
        out_shape=own_types
        + [vmem((8, rows, width))] * 2
        + [vmem((depth, width)), vmem((2, rows, width))],
        scratch_shapes=[
            vmem((count, rows * (depth + pack_gap), lanes)),
            vmem((4, count, rows * (depth + pack_gap), lanes)),
            pltpu.SemaphoreType.DMA((3,)),
        ],
        compiler_params=params,
        name="pack",
    )(far(field), far(diffusivity), far(velocity))
    odd_f = here(swap_pairs(odd_f, "rows", 1))
    even_d = here(swap_pairs(even_d, "depth", 0))
    odd_d = here(swap_pairs(odd_d, "depth", 1))
    own = [here(x) for x in own]
    spare_rows = (2 * depth + 2 + 7) // 8 * 8
    odd_x, even_x, *kept = pl.pallas_call(
        spare_kernel,
        out_shape=[vmem((spare_rows, width)), vmem((depth + spare_rows, width))]
        + [vmem((4, depth, width)), vmem((2, depth, width)), vmem((8, width))],
        scratch_shapes=[vmem((4, count, depth + 2 * margin, lanes))],
        compiler_params=params,
        cost_estimate=pl.CostEstimate(
            flops=40 * field.size, bytes_accessed=4 * field.size, transcendentals=0
        ),
        name="spare",
    )(*own)
    odd_x = here(swap_pairs(odd_x, "rows", 1))
    even_x = here(swap_pairs(even_x, "rows", 0))
    kept = [here(x) for x in kept]
    odd_2, even_2, middles, partly, sides = pl.pallas_call(
        edge_kernel,
        out_shape=[
            vmem((depth + 8, width)),
            vmem((depth + 8, width)),
            vmem((4, depth, width)),
            vmem((2, depth, width)),
            vmem((2, 2, rows, width)),
        ],
        scratch_shapes=[
            vmem((2, count, depth + 2 * margin, lanes)),
            vmem((count, 8 * (rows + 1), lanes)),
        ],
        compiler_params=params,
        name="edge",
    )(*own[1:], even_d, odd_d, odd_f, even_x, here(near), *kept)
    odd_2 = here(swap_pairs(odd_2, "rows", 1))
    even_2 = here(swap_pairs(even_2, "rows", 0))
    middles, partly, sides = here(middles), here(partly), here(sides)
    held = [vmem((count, (rows + 4) * block.pitch + margin, lanes))] * 2
    held += [pltpu.HBM(field.shape, field.dtype)]
    in_vmem = pl.BlockSpec(memory_space=pltpu.VMEM)
    second, third, front = pl.pallas_call(
        inner_kernel,
        out_shape=held,
        out_specs=[in_vmem] * 2 + [in_hbm],
        scratch_shapes=[
            vmem((count, (rows + 4) * block.pitch + margin, lanes)),
            vmem(field.shape),
            pltpu.SemaphoreType.DMA,
        ],
        compiler_params=params,
        cost_estimate=pl.CostEstimate(
            flops=80 * field.size, bytes_accessed=8 * field.size, transcendentals=0
        ),
        name="inner",
    )(*own, even_d, odd_d, middles, sides)
    opacity = opacity_total / (depth * groups)
    _, _, front, partial = pl.pallas_call(
        lambda *refs: rim_kernel(opacity, *refs),
        in_specs=[in_vmem] * 14 + [in_hbm],
        out_shape=held + [vmem((4, rows, width))],
        out_specs=[in_vmem] * 2 + [in_hbm, in_vmem],
        scratch_shapes=[vmem((2, depth, width)), pltpu.SemaphoreType.DMA((2,))],
        input_output_aliases={12 + i: i for i in range(3)},
        compiler_params=params,
        name="rim",
    )(
        own[0], even_d, odd_d, odd_x, even_x, odd_2, even_2, *kept[1:], middles, partly, sides,
        here(second), here(third), far(front),
    )

    position = lax.axis_index("depth")
    split = partial.reshape(4, rows, groups, width // groups)
    parts = {}
    for apart in range(groups):
        part = lax.dynamic_index_in_dim(split, position ^ apart, 2, keepdims=False)
        if apart:
            part = lax.ppermute(part, "depth", [(i, i ^ apart) for i in range(groups)])
        parts[apart] = part
    parts = jnp.stack([parts[-apart % groups] for apart in range(groups)])
    picture = None
    for s in range(groups):
        apart = position ^ s
        segment = lax.dynamic_index_in_dim(parts, -apart % groups, 0, keepdims=False)
        if picture is None:
            colors, through = segment[:3], segment[3:]
            picture = (colors, through)
        else:
            colors = colors + through * segment[:3]
            through = through * segment[3:]
    return front, jnp.concatenate([colors, through], axis=0)


def solution(mesh):
    return jax.shard_map(
        shards,
        mesh=mesh,
        in_specs=(
            P("rows", "depth", None),
            P("rows", "depth", None),
            P(None, "rows", "depth", None),
        ),
        out_specs=(P("rows", "depth", None), P(None, "rows", "depth")),
        check_vma=False,
    )
```

time: 33.4 us -> 32.3 us (0.967)
  waiting for transfers between devices: 11.6 us -> 6.22 us
  starting transfers between devices: 15.1 us -> 17.9 us
  Pallas kernels: 5.09 us -> 6.46 us
    ppermute x6 -> x7, waiting for transfers between devices: 7.72 us -> 2.31 us  [swap_pairs(): return lax.ppermute(value, axis, pairs(lax.axis_size(axis), first))]
    ppermute x6 -> x7, starting transfers between devices: 9.15 us -> 12 us  [swap_pairs(): return lax.ppermute(value, axis, pairs(lax.axis_size(axis), first))]
    pallas_call x3 -> x4, Pallas kernels: 3.32 us -> 4.71 us  [the longest x1 1.92 us: shards(): pl.pallas_call(inner_kernel, out_shape=held, out_specs=[in_vmem] * 2 + [i...]
  transfers between devices with their start and end apart: 9 -> 10, of which waited for: 4 -> 4; matrix products, arithmetic and copies ran while one was open for 0% -> 0% of each run, Pallas kernels for 4% -> 11%
where the time goes in v4:
time: 32.3 us; the launch traced here: 32.1 us
  starting transfers between devices  17.9 us (55%)
  Pallas kernels  6.46 us (20%)
  waiting for transfers between devices  6.22 us (19%)
  between operations  0.79 us (2%)
  other arithmetic  0.68 us (2%)
    ppermute x7, starting transfers between devices, swap_pairs(): return lax.ppermute(value, axis, pairs(lax.axis_size(axis), first))  12 us
    ppermute x3, starting transfers between devices, shards(): part = lax.ppermute(part, 'depth', [(i, i ^ apart) for i in range(groups)])  5.91 us
    ppermute x3, waiting for transfers between devices, shards(): part = lax.ppermute(part, 'depth', [(i, i ^ apart) for i in range(groups)])  3.91 us
    ppermute x7, waiting for transfers between devices, swap_pairs(): return lax.ppermute(value, axis, pairs(lax.axis_size(axis), first))  2.31 us
    pallas_call x1, Pallas kernels, shards(): pl.pallas_call(inner_kernel, out_shape=held, out_specs=[in_vmem] * 2 + [i...  1.92 us
    pallas_call x1, Pallas kernels, shards(): pl.pallas_call(pack_kernel, in_specs=[in_hbm] * 3, out_shape=own_types +...  1.76 us
    pallas_call x1, Pallas kernels, shards(): pl.pallas_call(lambda *refs: rim_kernel(opacity, *refs), in_specs=[in_vme...  1.3 us
    pallas_call x1, Pallas kernels, shards(): pl.pallas_call(edge_kernel, out_shape=[vmem((depth + 8, width)), vmem((de...  1.05 us
  transfers between devices with their start and end apart: 10, of which 4 were waited for; matrix products, arithmetic and copies ran while one was open for 0% of the time, Pallas kernels for 11%

profile of v4, /device:TPU:4, one launch (start us, length us, event | category | flops | bytes accessed | tf_op | source)
XLA Modules:
  0.0 32.1 jit_solution(7277771218803217979)
XLA Ops:
  0.6 1.8 %pack.1 = (f32[8,16,1024]{2,1,0:T(8,128)S(1)}, bf16[8,16,1024]{2,1,0:T(8,128)(2,1)S(1)}, bf16[3,8,16,1024]{3,2,1,0:T(8,128)(2,1)S(1)}, f32[8,8,1024]{2,1,0:T(8,1...) custom-call(f32[8,16,1024]{2,1,0:T(8,128)} %field_far.1, ...), custom_call_target="tpu_custom_call" | custom-call | tf_op jit(solution)/shard_map/pack/pallas_call | solution.py:481
  2.4 1.6 %collective-permute-start = (f32[8,8,1024]{2,1,0:T(8,128)S(1)}, f32[8,8,1024]{2,1,0:T(8,128)S(1)}, u32[]{:S(2)}, u32[]{:S(2)}) collective-permute-start(f32[8,8,1024]{2,1,0:T(8,128)S(1)} %get-tuple-element.25), channel_id=1, source_target_pairs={{0,1},{2,3},{1,0},{3,2},{4,5},{6,7},{5,4},{7,6},{8,9},{10,11},{9,8... | collective-permute-start | bytes 786440 | tf_op jit(solution)/shard_map/ppermute | solution.py:23
  4.0 0.7 %collective-permute-start.1 = (f32[8,8,1024]{2,1,0:T(8,128)S(1)}, f32[8,8,1024]{2,1,0:T(8,128)S(1)}, u32[]{:S(2)}, u32[]{:S(2)}) collective-permute-start(f32[8,8,1024]{2,1,0:T(8,128)S(1)} %get-tuple-element.26), channel_id=1, source_target_pairs={{1,2},{2,1},{5,6},{6,5},{9,10},{10,9},{13,14},{14,13},{17,18},{18,... | collective-permute-start | bytes 786440 | tf_op jit(solution)/shard_map/ppermute | solution.py:23
  4.7 0.4 %spare.1 = (f32[40,1024]{1,0:T(8,128)S(1)}, f32[56,1024]{1,0:T(8,128)S(1)}, f32[4,16,1024]{2,1,0:T(8,128)S(1)}, f32[2,16,1024]{2,1,0:T(8,128)S(1)}, f32[8,1024]{1,0:T(8,128)S(1)}) custom-call(f32[8,16,1024]{2,1,0:T(8,128)S(1)} %get-tuple-element.24.field.refs_0_, bf16[8,16,1024]{2,1,0:T(8,128)(2,1)S(1)} %get-tuple-element.27.diff, ...), custom_call_target="tpu_custom_call" | custom-call | flops 5242880 | bytes 524288 | tf_op jit(solution)/shard_map/spare/pallas_call | solution.py:500
  5.2 0.1 collective-permute-start.3
  5.2 3.4 %collective-permute-start.4 = (f32[16,1024]{1,0:T(8,128)S(1)}, f32[16,1024]{1,0:T(8,128)S(1)}, u32[]{:S(2)}, u32[]{:S(2)}) collective-permute-start(f32[16,1024]{1,0:T(8,128)S(1)} %get-tuple-element.31), channel_id=1, source_target_pairs={{4,8},{12,16},{20,24},{8,4},{16,12},{24,20},{5,9},{13,17},{21,25},... | collective-permute-start | bytes 196616 | tf_op jit(solution)/shard_map/ppermute | solution.py:23
  8.7 3.0 %collective-permute-start.2 = (f32[40,1024]{1,0:T(8,128)S(1)}, f32[40,1024]{1,0:T(8,128)S(1)}, u32[]{:S(2)}, u32[]{:S(2)}) collective-permute-start(f32[40,1024]{1,0:T(8,128)S(1)} %get-tuple-element.29), channel_id=1, source_target_pairs={{4,8},{12,16},{20,24},{8,4},{16,12},{24,20},{5,9},{13,17},{21,25},... | collective-permute-start | bytes 491528 | tf_op jit(solution)/shard_map/ppermute | solution.py:23
  11.7 0.4 %collective-permute-done.4.odd_f = f32[16,1024]{1,0:T(8,128)S(1)} collective-permute-done((f32[16,1024]{1,0:T(8,128)S(1)}, f32[16,1024]{1,0:T(8,128)S(1)}, u32[]{:S(2)}, u32[]{:S(2)}) %collective-permute-start.4) | collective-permute-done | bytes 65568 | tf_op jit(solution)/shard_map/ppermute | solution.py:23
  12.1 0.0 collective-permute-done.3.even_x.refs_4_
  12.1 0.0 collective-permute-done.even_d.refs_1_
  12.1 0.0 collective-permute-done.1.odd_d.refs_2_
  12.1 1.1 %edge.1 = (f32[24,1024]{1,0:T(8,128)}, f32[24,1024]{1,0:T(8,128)}, f32[4,16,1024]{2,1,0:T(8,128)S(1)}, f32[2,16,1024]{2,1,0:T(8,128)S(1)}, f32[2,2,8,1024]{3,2,1,0:T(8,128)S(1)}) custom-call(bf16[8,16,1024]{2,1,0:T(8,128)(2,1)S(1)} %get-tuple-element.27.diff, bf16[3,8,16,1024]{3,2,1,0:T(8,128)(2,1)S(1)} %get-tuple-element.28.vel, ...), custom_call_target="tpu_custom_call" | custom-call | tf_op jit(solution)/shard_map/edge/pallas_call | solution.py:514
  13.2 3.1 %collective-permute-start.5 = (f32[24,1024]{1,0:T(8,128)}, f32[24,1024]{1,0:T(8,128)S(1)}, u32[]{:S(2)}, u32[]{:S(2)}) collective-permute-start(f32[24,1024]{1,0:T(8,128)} %get-tuple-element.36), channel_id=1, source_target_pairs={{4,8},{12,16},{20,24},{8,4},{16,12},{24,20},{5,9},{13,17},{21,25},... | collective-permute-start | bytes 294920 | tf_op jit(solution)/shard_map/ppermute | solution.py:23
  16.3 0.1 collective-permute-start.6
  16.4 1.9 %inner.1 = (f32[8,404,128]{2,1,0:T(8,128)S(1)}, f32[8,404,128]{2,1,0:T(8,128)S(1)}, f32[8,16,1024]{2,1,0:T(8,128)}) custom-call(f32[8,16,1024]{2,1,0:T(8,128)S(1)} %get-tuple-element.24.field.refs_0_, bf16[8,16,1024]{2,1,0:T(8,128)(2,1)S(1)} %get-tuple-element.27.diff, bf16[3,8,16,1024]{3,2,1,0:T(8,128)(2,1)S(1)} %get-tuple-element.28.vel, ...), custom_call_target="tpu_custom_call" | custom-call | flops 10485760 | bytes 1048576 | tf_op jit(solution)/shard_map/inner/pallas_call | solution.py:536
  18.3 0.0 collective-permute-done.2.refs_3_
  18.3 1.9 %collective-permute-done.5.refs_5_ = f32[24,1024]{1,0:T(8,128)S(1)} collective-permute-done((f32[24,1024]{1,0:T(8,128)}, f32[24,1024]{1,0:T(8,128)S(1)}, u32[]{:S(2)}, u32[]{:S(2)}) %collective-permute-start.5) | collective-permute-done | bytes 98336 | tf_op jit(solution)/shard_map/ppermute | solution.py:23
  20.2 0.0 collective-permute-done.6.refs_6_
  20.2 1.3 %rim.1 = (f32[8,404,128]{2,1,0:T(8,128)S(1)}, f32[8,404,128]{2,1,0:T(8,128)S(1)}, f32[8,16,1024]{2,1,0:T(8,128)}, f32[4,8,1024]{2,1,0:T(8,128)S(1)}) custom-call(f32[8,16,1024]{2,1,0:T(8,128)S(1)} %get-tuple-element.24.field.refs_0_, ...), custom_call_target="tpu_custom_call", output_to_operand_aliasing={{0}: (12, {}), {1}: (13, {}), {2}: (14, {})} | custom-call | tf_op jit(solution)/shard_map/rim/pallas_call | solution.py:552
  21.6 2.5 %collective-permute-start.7 = (f32[4,8,256]{2,1,0:T(8,128)S(1)}, f32[4,8,256]{2,1,0:T(8,128)S(1)}, u32[]{:S(2)}, u32[]{:S(2)}) collective-permute-start(f32[4,8,256]{2,1,0:T(8,128)S(1)} %get-tuple-element.52), channel_id=1, source_target_pairs={{0,3},{1,2},{2,1},{3,0},{4,7},{5,6},{6,5},{7,4},{8,11},{9,10},{10,... | collective-permute-start | bytes 98312 | tf_op jit(solution)/shard_map/ppermute | solution.py:572
  24.1 3.4 %collective-permute-start.8 = (f32[4,8,256]{2,1,0:T(8,128)S(1)}, f32[4,8,256]{2,1,0:T(8,128)S(1)}, u32[]{:S(2)}, u32[]{:S(2)}) collective-permute-start(f32[4,8,256]{2,1,0:T(8,128)S(1)} %get-tuple-element.51), channel_id=1, source_target_pairs={{0,2},{1,3},{2,0},{3,1},{4,6},{5,7},{6,4},{7,5},{8,10},{9,11},{10,... | collective-permute-start | bytes 98312 | tf_op jit(solution)/shard_map/ppermute | solution.py:572
  27.5 2.2 %collective-permute-done.8 = f32[4,8,256]{2,1,0:T(8,128)S(1)} collective-permute-done((f32[4,8,256]{2,1,0:T(8,128)S(1)}, f32[4,8,256]{2,1,0:T(8,128)S(1)}, u32[]{:S(2)}, u32[]{:S(2)}) %collective-permute-start.8) | collective-permute-done | bytes 32800 | tf_op jit(solution)/shard_map/ppermute | solution.py:572
  29.7 1.7 %collective-permute-done.9 = f32[4,8,256]{2,1,0:T(8,128)S(1)} collective-permute-done((f32[4,8,256]{2,1,0:T(8,128)S(1)}, f32[4,8,256]{2,1,0:T(8,128)S(1)}, u32[]{:S(2)}, u32[]{:S(2)}) %collective-permute-start.9) | collective-permute-done | bytes 32800 | tf_op jit(solution)/shard_map/ppermute | solution.py:572
  31.5 0.6 %pad_maximum_fusion.1 = f32[4,8,256]{2,1,0:T(8,128)} fusion(f32[1,8,256]{2,1,0:T(8,128)S(1)} %fusion.6, f32[3,8,256]{2,1,0:T(8,128)S(1)} %fusion.1), kind=kLoop, calls=%fused_computation.1 | loop fusion | flops 8192 | bytes 65536 | tf_op jit(solution)/shard_map/concatenate | solution.py:585
  (7 shorter events, 0.1 us)
Async XLA Ops:
  2.4 9.7 %collective-permute-start = (f32[8,8,1024]{2,1,0:T(8,128)S(1)}, f32[8,8,1024]{2,1,0:T(8,128)S(1)}, u32[]{:S(2)}, u32[]{:S(2)}) collective-permute-start(f32[8,8,1024]{2,1,0:T(8,128)S(1)} %get-tuple-element.25), channel_id=1, source_target_pairs={{0,1},{2,3},{1,0},{3,2},{4,5},{6,7},{5,4},{7,6},{8,9},{10,11},{9,8... | collective-permute-start | bytes 786440 | tf_op jit(solution)/shard_map/ppermute | solution.py:23
  4.0 8.1 %collective-permute-start.1 = (f32[8,8,1024]{2,1,0:T(8,128)S(1)}, f32[8,8,1024]{2,1,0:T(8,128)S(1)}, u32[]{:S(2)}, u32[]{:S(2)}) collective-permute-start(f32[8,8,1024]{2,1,0:T(8,128)S(1)} %get-tuple-element.26), channel_id=1, source_target_pairs={{1,2},{2,1},{5,6},{6,5},{9,10},{10,9},{13,14},{14,13},{17,18},{18,... | collective-permute-start | bytes 786440 | tf_op jit(solution)/shard_map/ppermute | solution.py:23
  5.2 7.0 %collective-permute-start.3 = (f32[56,1024]{1,0:T(8,128)S(1)}, f32[56,1024]{1,0:T(8,128)S(1)}, u32[]{:S(2)}, u32[]{:S(2)}) collective-permute-start(f32[56,1024]{1,0:T(8,128)S(1)} %get-tuple-element.30), channel_id=1, source_target_pairs={{0,4},{8,12},{16,20},{24,28},{4,0},{12,8},{20,16},{28,24},{1,5},{9... | collective-permute-start | bytes 688136 | tf_op jit(solution)/shard_map/ppermute | solution.py:23
  5.2 6.9 %collective-permute-start.4 = (f32[16,1024]{1,0:T(8,128)S(1)}, f32[16,1024]{1,0:T(8,128)S(1)}, u32[]{:S(2)}, u32[]{:S(2)}) collective-permute-start(f32[16,1024]{1,0:T(8,128)S(1)} %get-tuple-element.31), channel_id=1, source_target_pairs={{4,8},{12,16},{20,24},{8,4},{16,12},{24,20},{5,9},{13,17},{21,25},... | collective-permute-start | bytes 196616 | tf_op jit(solution)/shard_map/ppermute | solution.py:23
  8.7 9.7 %collective-permute-start.2 = (f32[40,1024]{1,0:T(8,128)S(1)}, f32[40,1024]{1,0:T(8,128)S(1)}, u32[]{:S(2)}, u32[]{:S(2)}) collective-permute-start(f32[40,1024]{1,0:T(8,128)S(1)} %get-tuple-element.29), channel_id=1, source_target_pairs={{4,8},{12,16},{20,24},{8,4},{16,12},{24,20},{5,9},{13,17},{21,25},... | collective-permute-start | bytes 491528 | tf_op jit(solution)/shard_map/ppermute | solution.py:23
  13.2 7.0 %collective-permute-start.5 = (f32[24,1024]{1,0:T(8,128)}, f32[24,1024]{1,0:T(8,128)S(1)}, u32[]{:S(2)}, u32[]{:S(2)}) collective-permute-start(f32[24,1024]{1,0:T(8,128)} %get-tuple-element.36), channel_id=1, source_target_pairs={{4,8},{12,16},{20,24},{8,4},{16,12},{24,20},{5,9},{13,17},{21,25},... | collective-permute-start | bytes 294920 | tf_op jit(solution)/shard_map/ppermute | solution.py:23
  16.3 3.9 %collective-permute-start.6 = (f32[24,1024]{1,0:T(8,128)}, f32[24,1024]{1,0:T(8,128)S(1)}, u32[]{:S(2)}, u32[]{:S(2)}) collective-permute-start(f32[24,1024]{1,0:T(8,128)} %get-tuple-element.37), channel_id=1, source_target_pairs={{0,4},{8,12},{16,20},{24,28},{4,0},{12,8},{20,16},{28,24},{1,5},{9... | collective-permute-start | bytes 294920 | tf_op jit(solution)/shard_map/ppermute | solution.py:23
  21.6 5.9 %collective-permute-start.7 = (f32[4,8,256]{2,1,0:T(8,128)S(1)}, f32[4,8,256]{2,1,0:T(8,128)S(1)}, u32[]{:S(2)}, u32[]{:S(2)}) collective-permute-start(f32[4,8,256]{2,1,0:T(8,128)S(1)} %get-tuple-element.52), channel_id=1, source_target_pairs={{0,3},{1,2},{2,1},{3,0},{4,7},{5,6},{6,5},{7,4},{8,11},{9,10},{10,... | collective-permute-start | bytes 98312 | tf_op jit(solution)/shard_map/ppermute | solution.py:572
  24.1 5.6 %collective-permute-start.8 = (f32[4,8,256]{2,1,0:T(8,128)S(1)}, f32[4,8,256]{2,1,0:T(8,128)S(1)}, u32[]{:S(2)}, u32[]{:S(2)}) collective-permute-start(f32[4,8,256]{2,1,0:T(8,128)S(1)} %get-tuple-element.51), channel_id=1, source_target_pairs={{0,2},{1,3},{2,0},{3,1},{4,6},{5,7},{6,4},{7,5},{8,10},{9,11},{10,... | collective-permute-start | bytes 98312 | tf_op jit(solution)/shard_map/ppermute | solution.py:572
  27.5 3.9 %collective-permute-start.9 = (f32[4,8,256]{2,1,0:T(8,128)S(1)}, f32[4,8,256]{2,1,0:T(8,128)S(1)}, u32[]{:S(2)}, u32[]{:S(2)}) collective-permute-start(f32[4,8,256]{2,1,0:T(8,128)S(1)} %get-tuple-element.50), channel_id=1, source_target_pairs={{0,1},{1,0},{2,3},{3,2},{4,5},{5,4},{6,7},{7,6},{8,9},{9,8},{10,11... | collective-permute-start | bytes 98312 | tf_op jit(solution)/shard_map/ppermute | solution.py:572

commit v5 on v4

--- a/solution.py
+++ b/solution.py
@@ -11,6 +11,7 @@
 
 lanes = 128
 margin = 8
+halves = 1
 pack_gap = 4
 
 
@@ -47,7 +48,16 @@
 
 
 def cols(c):
-    return slice(c * lanes, (c + 1) * lanes)
+    start = c * lanes
+    return pl.ds(start if isinstance(c, int) else pl.multiple_of(start, lanes), lanes)
+
+
+def over(count, body, unroll):
+    def step(i, carry):
+        body(i)
+        return carry
+
+    lax.fori_loop(0, count, step, 0, unroll=unroll)
 
 
 def coef_of(diff, vel, r, c):
@@ -67,29 +77,37 @@
 def pack_kernel(
     field_far, diff_far, vel_far, field, diff, vel, even_d, odd_d, odd_f, near, flat, coefs, sems
 ):
-    loads = [
-        pltpu.make_async_copy(source, target, sems.at[i])
-        for i, (source, target) in enumerate(
-            ((field_far, field), (diff_far, diff), (vel_far, vel))
-        )
-    ]
-    for load in loads:
-        load.start()
-    for load in loads:
-        load.wait()
     rows, depth, width = field.shape
     count = width // lanes
     pitch = depth + pack_gap
     depth_odd = lax.axis_index("depth") % 2 == 1
     rows_odd = lax.axis_index("rows") % 2 == 1
-
+    parts = [(field_far, field), (diff_far, diff)]
+    parts += [(vel_far.at[i], vel.at[i]) for i in range(3)]
+    step = rows // halves
+    loads = [
+        [
+            pltpu.make_async_copy(
+                source.at[pl.ds(h * step, step)], target.at[pl.ds(h * step, step)], sems.at[h, i]
+            )
+            for i, (source, target) in enumerate(parts)
+        ]
+        for h in range(halves)
+    ]
+    for half in loads:
+        for load in half:
+            load.start()
+    for h, half in enumerate(loads):
+        for load in half:
+            load.wait()
+        for c in range(count):
+            for r in range(h * step, (h + 1) * step):
+                place = pl.ds(r * pitch, depth)
+                coef = coef_of(diff, vel, r, c)
+                flat[c, place, :] = field[r, :, cols(c)]
+                for i in range(4):
+                    coefs[i, c, place, :] = coef[i]
     for c in range(count):
-        for r in range(rows):
-            place = pl.ds(r * pitch, depth)
-            coef = coef_of(diff, vel, r, c)
-            flat[c, place, :] = field[r, :, cols(c)]
-            for i in range(4):
-                coefs[i, c, place, :] = coef[i]
         first, last = field[0, :, cols(c)], field[rows - 1, :, cols(c)]
         odd_f[:, cols(c)] = jnp.where(rows_odd, last, first)
 
@@ -373,7 +391,7 @@
     ends = ((0, 0, -1), (1, depth - 1, depth))
     rims = ((0, 0, -1), (1, rows - 1, rows))
 
-    for c in every:
+    def around(c):
         weights, parts = spare(0, depth, c), spare(depth, depth, c)
         fronts = arrived(even_2, odd_2, rows_odd, (slice(0, depth), cols(c)))
         along = [spare(2 * depth + k, 1, c) for k in range(2)]
@@ -406,6 +424,8 @@
             third[c, block.along(past), :] = value + at_ends(
                 along[0][e] * past_ends[0], along[1][e] * past_ends[1], line
             )
+
+    over(len(every), around, 2)
     saves = [
         pltpu.make_async_copy(front.at[e], front_far.at[r], sems.at[e]) for e, r, past in rims
     ]
@@ -423,7 +443,7 @@
         block.put(third, block.across(0, beyond, rows), values)
 
     def shine(d, carry):
-        shallow, center, deep = planes[d], planes[d + 1], planes[d + 2]
+        shallow, center, deep = (block.slab(third, 0, d + i, rows) for i in (-1, 0, 1))
         before, after = beside(center)
         above, below = block.slab(third, -1, d, rows), block.slab(third, 1, d, rows)
         result = []
@@ -444,10 +464,7 @@
 
     zero, one = jnp.zeros((rows, lanes), jnp.float32), jnp.ones((rows, lanes), jnp.float32)
     carry = tuple((one, zero, zero, zero) for _ in every)
-    planes = [block.slab(third, 0, -1, rows), block.slab(third, 0, 0, rows)]
-    for d in range(depth):
-        planes.append(block.slab(third, 0, d + 1, rows))
-        carry = shine(d, carry)
+    carry = lax.fori_loop(0, depth, shine, carry, unroll=8)
     for c, (through, total, red, green) in enumerate(carry):
         partial[0, :, cols(c)] = red
         partial[1, :, cols(c)] = green
@@ -487,7 +504,7 @@
         scratch_shapes=[
             vmem((count, rows * (depth + pack_gap), lanes)),
             vmem((4, count, rows * (depth + pack_gap), lanes)),
-            pltpu.SemaphoreType.DMA((3,)),
+            pltpu.SemaphoreType.DMA((halves, 5)),
         ],
         compiler_params=params,
         name="pack",

time: 32.3 us -> 32 us (level)
  no operation moved by 1% of the time
where the time goes in v5:
time: 32 us; the launch traced here: 31.8 us
  starting transfers between devices  17.9 us (56%)
  waiting for transfers between devices  6.22 us (19%)
  Pallas kernels  6.14 us (19%)
  between operations  0.79 us (2%)
  other arithmetic  0.68 us (2%)
    ppermute x7, starting transfers between devices, swap_pairs(): return lax.ppermute(value, axis, pairs(lax.axis_size(axis), first))  12 us
    ppermute x3, starting transfers between devices, shards(): part = lax.ppermute(part, 'depth', [(i, i ^ apart) for i in range(groups)])  5.91 us
    ppermute x3, waiting for transfers between devices, shards(): part = lax.ppermute(part, 'depth', [(i, i ^ apart) for i in range(groups)])  3.91 us
    ppermute x7, waiting for transfers between devices, swap_pairs(): return lax.ppermute(value, axis, pairs(lax.axis_size(axis), first))  2.31 us
    pallas_call x1, Pallas kernels, shards(): pl.pallas_call(inner_kernel, out_shape=held, out_specs=[in_vmem] * 2 + [i...  1.92 us
    pallas_call x1, Pallas kernels, shards(): pl.pallas_call(pack_kernel, in_specs=[in_hbm] * 3, out_shape=own_types +...  1.73 us
    pallas_call x1, Pallas kernels, shards(): pl.pallas_call(edge_kernel, out_shape=[vmem((depth + 8, width)), vmem((de...  1.05 us
    pallas_call x1, Pallas kernels, shards(): pl.pallas_call(lambda *refs: rim_kernel(opacity, *refs), in_specs=[in_vme...  1.01 us
  transfers between devices with their start and end apart: 10, of which 4 were waited for; matrix products, arithmetic and copies ran while one was open for 0% of the time, Pallas kernels for 11%

profile of v5, /device:TPU:4, one launch (start us, length us, event | category | flops | bytes accessed | tf_op | source)
XLA Modules:
  0.0 31.8 jit_solution(18105895487972033986)
XLA Ops:
  0.6 1.7 %pack.1 = (f32[8,16,1024]{2,1,0:T(8,128)S(1)}, bf16[8,16,1024]{2,1,0:T(8,128)(2,1)S(1)}, bf16[3,8,16,1024]{3,2,1,0:T(8,128)(2,1)S(1)}, f32[8,8,1024]{2,1,0:T(8,1...) custom-call(f32[8,16,1024]{2,1,0:T(8,128)} %field_far.1, ...), custom_call_target="tpu_custom_call" | custom-call | tf_op jit(solution)/shard_map/pack/pallas_call | solution.py:498
  2.4 1.6 %collective-permute-start = (f32[8,8,1024]{2,1,0:T(8,128)S(1)}, f32[8,8,1024]{2,1,0:T(8,128)S(1)}, u32[]{:S(2)}, u32[]{:S(2)}) collective-permute-start(f32[8,8,1024]{2,1,0:T(8,128)S(1)} %get-tuple-element.25), channel_id=1, source_target_pairs={{0,1},{2,3},{1,0},{3,2},{4,5},{6,7},{5,4},{7,6},{8,9},{10,11},{9,8... | collective-permute-start | bytes 786440 | tf_op jit(solution)/shard_map/ppermute | solution.py:24
  4.0 0.7 %collective-permute-start.1 = (f32[8,8,1024]{2,1,0:T(8,128)S(1)}, f32[8,8,1024]{2,1,0:T(8,128)S(1)}, u32[]{:S(2)}, u32[]{:S(2)}) collective-permute-start(f32[8,8,1024]{2,1,0:T(8,128)S(1)} %get-tuple-element.26), channel_id=1, source_target_pairs={{1,2},{2,1},{5,6},{6,5},{9,10},{10,9},{13,14},{14,13},{17,18},{18,... | collective-permute-start | bytes 786440 | tf_op jit(solution)/shard_map/ppermute | solution.py:24
  4.7 0.4 %spare.1 = (f32[40,1024]{1,0:T(8,128)S(1)}, f32[56,1024]{1,0:T(8,128)S(1)}, f32[4,16,1024]{2,1,0:T(8,128)S(1)}, f32[2,16,1024]{2,1,0:T(8,128)S(1)}, f32[8,1024]{1,0:T(8,128)S(1)}) custom-call(f32[8,16,1024]{2,1,0:T(8,128)S(1)} %get-tuple-element.24.field.refs_0_, bf16[8,16,1024]{2,1,0:T(8,128)(2,1)S(1)} %get-tuple-element.27.diff, ...), custom_call_target="tpu_custom_call" | custom-call | flops 5242880 | bytes 524288 | tf_op jit(solution)/shard_map/spare/pallas_call | solution.py:517
  5.1 0.1 collective-permute-start.3
  5.2 3.4 %collective-permute-start.4 = (f32[16,1024]{1,0:T(8,128)S(1)}, f32[16,1024]{1,0:T(8,128)S(1)}, u32[]{:S(2)}, u32[]{:S(2)}) collective-permute-start(f32[16,1024]{1,0:T(8,128)S(1)} %get-tuple-element.31), channel_id=1, source_target_pairs={{4,8},{12,16},{20,24},{8,4},{16,12},{24,20},{5,9},{13,17},{21,25},... | collective-permute-start | bytes 196616 | tf_op jit(solution)/shard_map/ppermute | solution.py:24
  8.6 3.0 %collective-permute-start.2 = (f32[40,1024]{1,0:T(8,128)S(1)}, f32[40,1024]{1,0:T(8,128)S(1)}, u32[]{:S(2)}, u32[]{:S(2)}) collective-permute-start(f32[40,1024]{1,0:T(8,128)S(1)} %get-tuple-element.29), channel_id=1, source_target_pairs={{4,8},{12,16},{20,24},{8,4},{16,12},{24,20},{5,9},{13,17},{21,25},... | collective-permute-start | bytes 491528 | tf_op jit(solution)/shard_map/ppermute | solution.py:24
  11.7 0.4 %collective-permute-done.4.odd_f = f32[16,1024]{1,0:T(8,128)S(1)} collective-permute-done((f32[16,1024]{1,0:T(8,128)S(1)}, f32[16,1024]{1,0:T(8,128)S(1)}, u32[]{:S(2)}, u32[]{:S(2)}) %collective-permute-start.4) | collective-permute-done | bytes 65568 | tf_op jit(solution)/shard_map/ppermute | solution.py:24
  12.1 0.0 collective-permute-done.3.even_x.refs_4_
  12.1 0.0 collective-permute-done.even_d.refs_1_
  12.1 0.0 collective-permute-done.1.odd_d.refs_2_
  12.1 1.1 %edge.1 = (f32[24,1024]{1,0:T(8,128)}, f32[24,1024]{1,0:T(8,128)}, f32[4,16,1024]{2,1,0:T(8,128)S(1)}, f32[2,16,1024]{2,1,0:T(8,128)S(1)}, f32[2,2,8,1024]{3,2,1,0:T(8,128)S(1)}) custom-call(bf16[8,16,1024]{2,1,0:T(8,128)(2,1)S(1)} %get-tuple-element.27.diff, bf16[3,8,16,1024]{3,2,1,0:T(8,128)(2,1)S(1)} %get-tuple-element.28.vel, ...), custom_call_target="tpu_custom_call" | custom-call | tf_op jit(solution)/shard_map/edge/pallas_call | solution.py:531
  13.2 3.1 %collective-permute-start.5 = (f32[24,1024]{1,0:T(8,128)}, f32[24,1024]{1,0:T(8,128)S(1)}, u32[]{:S(2)}, u32[]{:S(2)}) collective-permute-start(f32[24,1024]{1,0:T(8,128)} %get-tuple-element.36), channel_id=1, source_target_pairs={{4,8},{12,16},{20,24},{8,4},{16,12},{24,20},{5,9},{13,17},{21,25},... | collective-permute-start | bytes 294920 | tf_op jit(solution)/shard_map/ppermute | solution.py:24
  16.3 0.1 collective-permute-start.6
  16.4 1.9 %inner.1 = (f32[8,404,128]{2,1,0:T(8,128)S(1)}, f32[8,404,128]{2,1,0:T(8,128)S(1)}, f32[8,16,1024]{2,1,0:T(8,128)}) custom-call(f32[8,16,1024]{2,1,0:T(8,128)S(1)} %get-tuple-element.24.field.refs_0_, bf16[8,16,1024]{2,1,0:T(8,128)(2,1)S(1)} %get-tuple-element.27.diff, bf16[3,8,16,1024]{3,2,1,0:T(8,128)(2,1)S(1)} %get-tuple-element.28.vel, ...), custom_call_target="tpu_custom_call" | custom-call | flops 10485760 | bytes 1048576 | tf_op jit(solution)/shard_map/inner/pallas_call | solution.py:553
  18.3 1.9 %collective-permute-done.5.refs_5_ = f32[24,1024]{1,0:T(8,128)S(1)} collective-permute-done((f32[24,1024]{1,0:T(8,128)}, f32[24,1024]{1,0:T(8,128)S(1)}, u32[]{:S(2)}, u32[]{:S(2)}) %collective-permute-start.5) | collective-permute-done | bytes 98336 | tf_op jit(solution)/shard_map/ppermute | solution.py:24
  20.2 1.0 %rim.1 = (f32[8,404,128]{2,1,0:T(8,128)S(1)}, f32[8,404,128]{2,1,0:T(8,128)S(1)}, f32[8,16,1024]{2,1,0:T(8,128)}, f32[4,8,1024]{2,1,0:T(8,128)S(1)}) custom-call(f32[8,16,1024]{2,1,0:T(8,128)S(1)} %get-tuple-element.24.field.refs_0_, ...), custom_call_target="tpu_custom_call", output_to_operand_aliasing={{0}: (12, {}), {1}: (13, {}), {2}: (14, {})} | custom-call | tf_op jit(solution)/shard_map/rim/pallas_call | solution.py:569
  21.2 2.5 %collective-permute-start.7 = (f32[4,8,256]{2,1,0:T(8,128)S(1)}, f32[4,8,256]{2,1,0:T(8,128)S(1)}, u32[]{:S(2)}, u32[]{:S(2)}) collective-permute-start(f32[4,8,256]{2,1,0:T(8,128)S(1)} %get-tuple-element.52), channel_id=1, source_target_pairs={{0,3},{1,2},{2,1},{3,0},{4,7},{5,6},{6,5},{7,4},{8,11},{9,10},{10,... | collective-permute-start | bytes 98312 | tf_op jit(solution)/shard_map/ppermute | solution.py:589
  23.8 3.4 %collective-permute-start.8 = (f32[4,8,256]{2,1,0:T(8,128)S(1)}, f32[4,8,256]{2,1,0:T(8,128)S(1)}, u32[]{:S(2)}, u32[]{:S(2)}) collective-permute-start(f32[4,8,256]{2,1,0:T(8,128)S(1)} %get-tuple-element.51), channel_id=1, source_target_pairs={{0,2},{1,3},{2,0},{3,1},{4,6},{5,7},{6,4},{7,5},{8,10},{9,11},{10,... | collective-permute-start | bytes 98312 | tf_op jit(solution)/shard_map/ppermute | solution.py:589
  27.2 0.0 collective-permute-start.9
  27.2 0.0 collective-permute-done.7
  27.2 2.2 %collective-permute-done.8 = f32[4,8,256]{2,1,0:T(8,128)S(1)} collective-permute-done((f32[4,8,256]{2,1,0:T(8,128)S(1)}, f32[4,8,256]{2,1,0:T(8,128)S(1)}, u32[]{:S(2)}, u32[]{:S(2)}) %collective-permute-start.8) | collective-permute-done | bytes 32800 | tf_op jit(solution)/shard_map/ppermute | solution.py:589
  29.4 1.7 %collective-permute-done.9 = f32[4,8,256]{2,1,0:T(8,128)S(1)} collective-permute-done((f32[4,8,256]{2,1,0:T(8,128)S(1)}, f32[4,8,256]{2,1,0:T(8,128)S(1)}, u32[]{:S(2)}, u32[]{:S(2)}) %collective-permute-start.9) | collective-permute-done | bytes 32800 | tf_op jit(solution)/shard_map/ppermute | solution.py:589
  31.2 0.6 %pad_maximum_fusion.1 = f32[4,8,256]{2,1,0:T(8,128)} fusion(f32[1,8,256]{2,1,0:T(8,128)S(1)} %fusion.6, f32[3,8,256]{2,1,0:T(8,128)S(1)} %fusion.1), kind=kLoop, calls=%fused_computation.1 | loop fusion | flops 8192 | bytes 65536 | tf_op jit(solution)/shard_map/concatenate | solution.py:602
  (7 shorter events, 0.1 us)
Async XLA Ops:
  2.4 9.7 %collective-permute-start = (f32[8,8,1024]{2,1,0:T(8,128)S(1)}, f32[8,8,1024]{2,1,0:T(8,128)S(1)}, u32[]{:S(2)}, u32[]{:S(2)}) collective-permute-start(f32[8,8,1024]{2,1,0:T(8,128)S(1)} %get-tuple-element.25), channel_id=1, source_target_pairs={{0,1},{2,3},{1,0},{3,2},{4,5},{6,7},{5,4},{7,6},{8,9},{10,11},{9,8... | collective-permute-start | bytes 786440 | tf_op jit(solution)/shard_map/ppermute | solution.py:24
  4.0 8.1 %collective-permute-start.1 = (f32[8,8,1024]{2,1,0:T(8,128)S(1)}, f32[8,8,1024]{2,1,0:T(8,128)S(1)}, u32[]{:S(2)}, u32[]{:S(2)}) collective-permute-start(f32[8,8,1024]{2,1,0:T(8,128)S(1)} %get-tuple-element.26), channel_id=1, source_target_pairs={{1,2},{2,1},{5,6},{6,5},{9,10},{10,9},{13,14},{14,13},{17,18},{18,... | collective-permute-start | bytes 786440 | tf_op jit(solution)/shard_map/ppermute | solution.py:24
  5.1 7.0 %collective-permute-start.3 = (f32[56,1024]{1,0:T(8,128)S(1)}, f32[56,1024]{1,0:T(8,128)S(1)}, u32[]{:S(2)}, u32[]{:S(2)}) collective-permute-start(f32[56,1024]{1,0:T(8,128)S(1)} %get-tuple-element.30), channel_id=1, source_target_pairs={{0,4},{8,12},{16,20},{24,28},{4,0},{12,8},{20,16},{28,24},{1,5},{9... | collective-permute-start | bytes 688136 | tf_op jit(solution)/shard_map/ppermute | solution.py:24
  5.2 6.9 %collective-permute-start.4 = (f32[16,1024]{1,0:T(8,128)S(1)}, f32[16,1024]{1,0:T(8,128)S(1)}, u32[]{:S(2)}, u32[]{:S(2)}) collective-permute-start(f32[16,1024]{1,0:T(8,128)S(1)} %get-tuple-element.31), channel_id=1, source_target_pairs={{4,8},{12,16},{20,24},{8,4},{16,12},{24,20},{5,9},{13,17},{21,25},... | collective-permute-start | bytes 196616 | tf_op jit(solution)/shard_map/ppermute | solution.py:24
  8.6 9.7 %collective-permute-start.2 = (f32[40,1024]{1,0:T(8,128)S(1)}, f32[40,1024]{1,0:T(8,128)S(1)}, u32[]{:S(2)}, u32[]{:S(2)}) collective-permute-start(f32[40,1024]{1,0:T(8,128)S(1)} %get-tuple-element.29), channel_id=1, source_target_pairs={{4,8},{12,16},{20,24},{8,4},{16,12},{24,20},{5,9},{13,17},{21,25},... | collective-permute-start | bytes 491528 | tf_op jit(solution)/shard_map/ppermute | solution.py:24
  13.2 7.0 %collective-permute-start.5 = (f32[24,1024]{1,0:T(8,128)}, f32[24,1024]{1,0:T(8,128)S(1)}, u32[]{:S(2)}, u32[]{:S(2)}) collective-permute-start(f32[24,1024]{1,0:T(8,128)} %get-tuple-element.36), channel_id=1, source_target_pairs={{4,8},{12,16},{20,24},{8,4},{16,12},{24,20},{5,9},{13,17},{21,25},... | collective-permute-start | bytes 294920 | tf_op jit(solution)/shard_map/ppermute | solution.py:24
  16.3 3.9 %collective-permute-start.6 = (f32[24,1024]{1,0:T(8,128)}, f32[24,1024]{1,0:T(8,128)S(1)}, u32[]{:S(2)}, u32[]{:S(2)}) collective-permute-start(f32[24,1024]{1,0:T(8,128)} %get-tuple-element.37), channel_id=1, source_target_pairs={{0,4},{8,12},{16,20},{24,28},{4,0},{12,8},{20,16},{28,24},{1,5},{9... | collective-permute-start | bytes 294920 | tf_op jit(solution)/shard_map/ppermute | solution.py:24
  21.2 5.9 %collective-permute-start.7 = (f32[4,8,256]{2,1,0:T(8,128)S(1)}, f32[4,8,256]{2,1,0:T(8,128)S(1)}, u32[]{:S(2)}, u32[]{:S(2)}) collective-permute-start(f32[4,8,256]{2,1,0:T(8,128)S(1)} %get-tuple-element.52), channel_id=1, source_target_pairs={{0,3},{1,2},{2,1},{3,0},{4,7},{5,6},{6,5},{7,4},{8,11},{9,10},{10,... | collective-permute-start | bytes 98312 | tf_op jit(solution)/shard_map/ppermute | solution.py:589
  23.8 5.6 %collective-permute-start.8 = (f32[4,8,256]{2,1,0:T(8,128)S(1)}, f32[4,8,256]{2,1,0:T(8,128)S(1)}, u32[]{:S(2)}, u32[]{:S(2)}) collective-permute-start(f32[4,8,256]{2,1,0:T(8,128)S(1)} %get-tuple-element.51), channel_id=1, source_target_pairs={{0,2},{1,3},{2,0},{3,1},{4,6},{5,7},{6,4},{7,5},{8,10},{9,11},{10,... | collective-permute-start | bytes 98312 | tf_op jit(solution)/shard_map/ppermute | solution.py:589
  27.2 3.9 %collective-permute-start.9 = (f32[4,8,256]{2,1,0:T(8,128)S(1)}, f32[4,8,256]{2,1,0:T(8,128)S(1)}, u32[]{:S(2)}, u32[]{:S(2)}) collective-permute-start(f32[4,8,256]{2,1,0:T(8,128)S(1)} %get-tuple-element.50), channel_id=1, source_target_pairs={{0,1},{1,0},{2,3},{3,2},{4,5},{5,4},{6,7},{7,6},{8,9},{9,8},{10,11... | collective-permute-start | bytes 98312 | tf_op jit(solution)/shard_map/ppermute | solution.py:589

commit v6 on v5

--- a/solution.py
+++ b/solution.py
@@ -136,9 +136,13 @@
         sides.append(side)
     low, high = sides
     for c in range(count):
-        for i in range(8):
-            even_d[i, :, cols(c)] = jnp.where(depth_odd, low[c][i], high[c][i])
-            odd_d[i, :, cols(c)] = jnp.where(depth_odd, high[c][i], low[c][i])
+        for i in range(7):
+            even_d[of_deep(rows, c, i)] = jnp.where(depth_odd, low[c][i], high[c][i])
+            odd_d[of_deep(rows, c, i)] = jnp.where(depth_odd, high[c][i], low[c][i])
+        for i, r in enumerate((0, rows - 1)):
+            f_val, l_val = low[c][7][r : r + 1], high[c][7][r : r + 1]
+            even_d[of_deep(rows, c, 7, i, 1)] = jnp.where(depth_odd, f_val, l_val)
+            odd_d[of_deep(rows, c, 7, i, 1)] = jnp.where(depth_odd, l_val, f_val)
 
 
 def spare_kernel(field, diff, vel, odd_x, even_x, partial, own_w, own_d, ext):
@@ -191,6 +195,15 @@
     return jnp.where(is_odd, a, b), jnp.where(is_odd, b, a)
 
 
+def deep_rows(rows):
+    return 7 * rows + 2
+
+
+def of_deep(rows, c, item, start=0, length=None):
+    place = c * deep_rows(rows) + item * rows + start
+    return pl.ds(place, rows if length is None else length), slice(None)
+
+
 def past_rows(u, row):
     rows = u.shape[0]
     above = jnp.where(row == 0, 0.0, pltpu.roll(u, 1, 0))
@@ -211,7 +224,7 @@
     diff, vel, even_d, odd_d, odd_f, even_x, near, partial, own_w, own_d,
     odd_2, even_2, middles, partly, sides, ext, stack,
 ):
-    _, rows, width = even_d.shape
+    _, rows, width = near.shape
     depth = diff.shape[1]
     every = range(width // lanes)
     depth_odd = lax.axis_index("depth") % 2 == 1
@@ -228,7 +241,7 @@
             value = partial[j, :, cols(c)]
             if j in (0, 3):
                 value = value + own_w[j // 3, :, cols(c)] * beyond[j // 3]
-            both = arrived(even_d, odd_d, depth_odd, (0, pl.ds(r, 1), cols(c)))
+            both = arrived(even_d, odd_d, depth_odd, of_deep(rows, c, 0, r, 1))
             weights = [own_d[2 * j + k : 2 * j + k + 1, cols(c)] for k in range(2)]
             value = value + at_ends(weights[0] * both[0], weights[1] * both[1], value.shape)
             lines[j].append(value)
@@ -255,7 +268,7 @@
         odd_2[:depth, cols(c)] = jnp.where(rows_odd, last, first)
 
     def came(item, c, k):
-        return arrived(even_d, odd_d, depth_odd, (item, slice(None), cols(c)))[k]
+        return arrived(even_d, odd_d, depth_odd, of_deep(rows, c, item))[k]
 
     for k in range(2):
         u = [came(0, c, k) for c in every]
@@ -282,10 +295,10 @@
 class Block:
     def __init__(self, rows, depth, width):
         self.rows, self.depth, self.every = rows, depth, range(width // lanes)
-        self.pitch = depth + 2 * margin + 1
+        self.pitch = depth + margin + 1
 
     def at(self, r, d):
-        return (r + 2) * self.pitch + margin + d
+        return (r + 1) * self.pitch + margin + d
 
     def along(self, r, d=0):
         return pl.ds(self.at(r, d), self.depth)
@@ -332,10 +345,10 @@
     for c in block.every:
         for r in range(1, rows - 1):
             first[c, block.along(r), :] = field[r, :, cols(c)]
-        low, high = arrived(even_d, odd_d, depth_odd, (0, slice(None), cols(c)))
+        low, high = arrived(even_d, odd_d, depth_odd, of_deep(rows, c, 0))
         first[c, block.across(0, -1, rows), :] = low
         first[c, block.across(0, depth, rows), :] = high
-        low, high = arrived(even_d, odd_d, depth_odd, (6, slice(None), cols(c)))
+        low, high = arrived(even_d, odd_d, depth_odd, of_deep(rows, c, 6))
         second[c, block.across(0, -2, rows), :] = low
         second[c, block.across(0, depth + 1, rows), :] = high
         second[c, block.across(0, -1, rows), :] = sides[0, 0, :, cols(c)]
@@ -404,9 +417,9 @@
             own_ends, past_ends = [], []
             for k, d, beyond in ends:
                 index = (slice(r, r + 1), cols(c))
-                outside = arrived(even_d, odd_d, depth_odd, (0, *index))[k]
-                next_cell = arrived(even_d, odd_d, depth_odd, (6, *index))[k]
-                next_weight = arrived(even_d, odd_d, depth_odd, (7, *index))[k]
+                outside = arrived(even_d, odd_d, depth_odd, of_deep(rows, c, 0, r, 1))[k]
+                next_cell = arrived(even_d, odd_d, depth_odd, of_deep(rows, c, 6, r, 1))[k]
+                next_weight = arrived(even_d, odd_d, depth_odd, of_deep(rows, c, 7, e, 1))[k]
                 _, far_cell, part, weight = (x[e] for x in corners[k])
                 past_ends.append(part + weight * outside)
                 own_ends.append(sides[k, 0, *index] + sides[k, 1, *index] * near[k])
@@ -434,7 +447,7 @@
     for k, d, beyond in ends:
         items = [
             [
-                arrived(even_d, odd_d, depth_odd, (2 + i, slice(None), cols(c)))[k]
+                arrived(even_d, odd_d, depth_odd, of_deep(rows, c, 2 + i))[k]
                 for i in range(4)
             ]
             for c in every
@@ -499,7 +512,7 @@
         pack_kernel,
         in_specs=[in_hbm] * 3,
         out_shape=own_types
-        + [vmem((8, rows, width))] * 2
+        + [vmem((count * deep_rows(rows), lanes))] * 2
         + [vmem((depth, width)), vmem((2, rows, width))],
         scratch_shapes=[
             vmem((count, rows * (depth + pack_gap), lanes)),
@@ -516,7 +529,7 @@
     spare_rows = (2 * depth + 2 + 7) // 8 * 8
     odd_x, even_x, *kept = pl.pallas_call(
         spare_kernel,
-        out_shape=[vmem((spare_rows, width)), vmem((depth + spare_rows, width))]
+        out_shape=[vmem((spare_rows, width)), vmem((depth + spare_rows + 8, width))]
         + [vmem((4, depth, width)), vmem((2, depth, width)), vmem((8, width))],
         scratch_shapes=[vmem((4, count, depth + 2 * margin, lanes))],
         compiler_params=params,
@@ -547,7 +560,7 @@
     odd_2 = here(swap_pairs(odd_2, "rows", 1))
     even_2 = here(swap_pairs(even_2, "rows", 0))
     middles, partly, sides = here(middles), here(partly), here(sides)
-    held = [vmem((count, (rows + 4) * block.pitch + margin, lanes))] * 2
+    held = [vmem((count, (rows + 2) * block.pitch + margin, lanes))] * 2
     held += [pltpu.HBM(field.shape, field.dtype)]
     in_vmem = pl.BlockSpec(memory_space=pltpu.VMEM)
     second, third, front = pl.pallas_call(
@@ -555,7 +568,7 @@
         out_shape=held,
         out_specs=[in_vmem] * 2 + [in_hbm],
         scratch_shapes=[
-            vmem((count, (rows + 4) * block.pitch + margin, lanes)),
+            vmem((count, (rows + 2) * block.pitch + margin, lanes)),
             vmem(field.shape),
             pltpu.SemaphoreType.DMA,
         ],

time: 32 us -> 31.6 us (0.988)
  waiting for transfers between devices: 6.22 us -> 5.55 us
    ppermute x7, waiting for transfers between devices: 2.31 us -> 1.64 us  [swap_pairs(): return lax.ppermute(value, axis, pairs(lax.axis_size(axis), first))]
  transfers between devices with their start and end apart: 10 -> 10, of which waited for: 4 -> 4; matrix products, arithmetic and copies ran while one was open for 0% -> 0% of each run, Pallas kernels for 11% -> 10%
where the time goes in v6:
time: 31.6 us; the launch traced here: 31.4 us
  starting transfers between devices  18.2 us (58%)
  Pallas kernels  6.15 us (19%)
  waiting for transfers between devices  5.55 us (18%)
  between operations  0.79 us (2%)
  other arithmetic  0.68 us (2%)
    ppermute x7, starting transfers between devices, swap_pairs(): return lax.ppermute(value, axis, pairs(lax.axis_size(axis), first))  12.3 us
    ppermute x3, starting transfers between devices, shards(): part = lax.ppermute(part, 'depth', [(i, i ^ apart) for i in range(groups)])  5.85 us
    ppermute x3, waiting for transfers between devices, shards(): part = lax.ppermute(part, 'depth', [(i, i ^ apart) for i in range(groups)])  3.91 us
    pallas_call x1, Pallas kernels, shards(): pl.pallas_call(inner_kernel, out_shape=held, out_specs=[in_vmem] * 2 + [i...  1.95 us
    pallas_call x1, Pallas kernels, shards(): pl.pallas_call(pack_kernel, in_specs=[in_hbm] * 3, out_shape=own_types +...  1.72 us
    ppermute x7, waiting for transfers between devices, swap_pairs(): return lax.ppermute(value, axis, pairs(lax.axis_size(axis), first))  1.64 us
    pallas_call x1, Pallas kernels, shards(): pl.pallas_call(edge_kernel, out_shape=[vmem((depth + 8, width)), vmem((de...  1.07 us
    pallas_call x1, Pallas kernels, shards(): pl.pallas_call(lambda *refs: rim_kernel(opacity, *refs), in_specs=[in_vme...  0.97 us
  transfers between devices with their start and end apart: 10, of which 4 were waited for; matrix products, arithmetic and copies ran while one was open for 0% of the time, Pallas kernels for 10%

profile of v6, /device:TPU:4, one launch (start us, length us, event | category | flops | bytes accessed | tf_op | source)
XLA Modules:
  0.0 31.4 jit_solution(7379629572953754014)
XLA Ops:
  0.6 1.7 %pack.1 = (f32[8,16,1024]{2,1,0:T(8,128)S(1)}, bf16[8,16,1024]{2,1,0:T(8,128)(2,1)S(1)}, bf16[3,8,16,1024]{3,2,1,0:T(8,128)(2,1)S(1)}, f32[464,128]{1,0:T(8,128)...) custom-call(f32[8,16,1024]{2,1,0:T(8,128)} %field_far.1, ...), custom_call_target="tpu_custom_call" | custom-call | tf_op jit(solution)/shard_map/pack/pallas_call | solution.py:511
  2.4 0.4 %spare.1 = (f32[40,1024]{1,0:T(8,128)S(1)}, f32[64,1024]{1,0:T(8,128)S(1)}, f32[4,16,1024]{2,1,0:T(8,128)S(1)}, f32[2,16,1024]{2,1,0:T(8,128)S(1)}, f32[8,1024]{1,0:T(8,128)S(1)}) custom-call(f32[8,16,1024]{2,1,0:T(8,128)S(1)} %get-tuple-element.24.field.refs_0_, bf16[8,16,1024]{2,1,0:T(8,128)(2,1)S(1)} %get-tuple-element.27.diff, ...), custom_call_target="tpu_custom_call" | custom-call | flops 5242880 | bytes 524288 | tf_op jit(solution)/shard_map/spare/pallas_call | solution.py:530
  2.8 0.1 collective-permute-start.3
  2.9 1.6 %collective-permute-start = (f32[464,128]{1,0:T(8,128)S(1)}, f32[464,128]{1,0:T(8,128)S(1)}, u32[]{:S(2)}, u32[]{:S(2)}) collective-permute-start(f32[464,128]{1,0:T(8,128)S(1)} %get-tuple-element.25), channel_id=1, source_target_pairs={{0,1},{2,3},{1,0},{3,2},{4,5},{6,7},{5,4},{7,6},{8,9},{10,11},{9,8... | collective-permute-start | bytes 712712 | tf_op jit(solution)/shard_map/ppermute | solution.py:24
  4.5 0.7 %collective-permute-start.1 = (f32[464,128]{1,0:T(8,128)S(1)}, f32[464,128]{1,0:T(8,128)S(1)}, u32[]{:S(2)}, u32[]{:S(2)}) collective-permute-start(f32[464,128]{1,0:T(8,128)S(1)} %get-tuple-element.26), channel_id=1, source_target_pairs={{1,2},{2,1},{5,6},{6,5},{9,10},{10,9},{13,14},{14,13},{17,18},{18,... | collective-permute-start | bytes 712712 | tf_op jit(solution)/shard_map/ppermute | solution.py:24
  5.2 3.1 %collective-permute-start.4 = (f32[16,1024]{1,0:T(8,128)S(1)}, f32[16,1024]{1,0:T(8,128)S(1)}, u32[]{:S(2)}, u32[]{:S(2)}) collective-permute-start(f32[16,1024]{1,0:T(8,128)S(1)} %get-tuple-element.31), channel_id=1, source_target_pairs={{4,8},{12,16},{20,24},{8,4},{16,12},{24,20},{5,9},{13,17},{21,25},... | collective-permute-start | bytes 196616 | tf_op jit(solution)/shard_map/ppermute | solution.py:24
  8.3 3.3 %collective-permute-start.2 = (f32[40,1024]{1,0:T(8,128)S(1)}, f32[40,1024]{1,0:T(8,128)S(1)}, u32[]{:S(2)}, u32[]{:S(2)}) collective-permute-start(f32[40,1024]{1,0:T(8,128)S(1)} %get-tuple-element.29), channel_id=1, source_target_pairs={{4,8},{12,16},{20,24},{8,4},{16,12},{24,20},{5,9},{13,17},{21,25},... | collective-permute-start | bytes 491528 | tf_op jit(solution)/shard_map/ppermute | solution.py:24
  11.7 0.1 collective-permute-done.4.odd_f
  11.8 0.0 collective-permute-done.even_d.refs_1_
  11.8 0.0 collective-permute-done.1.odd_d.refs_2_
  11.8 0.0 collective-permute-done.3.even_x.refs_4_
  11.8 1.1 %edge.1 = (f32[24,1024]{1,0:T(8,128)}, f32[24,1024]{1,0:T(8,128)}, f32[4,16,1024]{2,1,0:T(8,128)S(1)}, f32[2,16,1024]{2,1,0:T(8,128)S(1)}, f32[2,2,8,1024]{3,2,1,0:T(8,128)S(1)}) custom-call(bf16[8,16,1024]{2,1,0:T(8,128)(2,1)S(1)} %get-tuple-element.27.diff, bf16[3,8,16,1024]{3,2,1,0:T(8,128)(2,1)S(1)} %get-tuple-element.28.vel, ...), custom_call_target="tpu_custom_call" | custom-call | tf_op jit(solution)/shard_map/edge/pallas_call | solution.py:544
  12.8 3.4 %collective-permute-start.5 = (f32[24,1024]{1,0:T(8,128)}, f32[24,1024]{1,0:T(8,128)S(1)}, u32[]{:S(2)}, u32[]{:S(2)}) collective-permute-start(f32[24,1024]{1,0:T(8,128)} %get-tuple-element.36), channel_id=1, source_target_pairs={{4,8},{12,16},{20,24},{8,4},{16,12},{24,20},{5,9},{13,17},{21,25},... | collective-permute-start | bytes 294920 | tf_op jit(solution)/shard_map/ppermute | solution.py:24
  16.3 0.1 collective-permute-start.6
  16.4 2.0 %inner.1 = (f32[8,258,128]{2,1,0:T(8,128)S(1)}, f32[8,258,128]{2,1,0:T(8,128)S(1)}, f32[8,16,1024]{2,1,0:T(8,128)}) custom-call(f32[8,16,1024]{2,1,0:T(8,128)S(1)} %get-tuple-element.24.field.refs_0_, bf16[8,16,1024]{2,1,0:T(8,128)(2,1)S(1)} %get-tuple-element.27.diff, bf16[3,8,16,1024]{3,2,1,0:T(8,128)(2,1)S(1)} %get-tuple-element.28.vel, ...), custom_call_target="tpu_custom_call" | custom-call | flops 10485760 | bytes 1048576 | tf_op jit(solution)/shard_map/inner/pallas_call | solution.py:566
  18.4 1.5 %collective-permute-done.5.refs_5_ = f32[24,1024]{1,0:T(8,128)S(1)} collective-permute-done((f32[24,1024]{1,0:T(8,128)}, f32[24,1024]{1,0:T(8,128)S(1)}, u32[]{:S(2)}, u32[]{:S(2)}) %collective-permute-start.5) | collective-permute-done | bytes 98336 | tf_op jit(solution)/shard_map/ppermute | solution.py:24
  19.9 0.0 collective-permute-done.6.refs_6_
  19.9 1.0 %rim.1 = (f32[8,258,128]{2,1,0:T(8,128)S(1)}, f32[8,258,128]{2,1,0:T(8,128)S(1)}, f32[8,16,1024]{2,1,0:T(8,128)}, f32[4,8,1024]{2,1,0:T(8,128)S(1)}) custom-call(f32[8,16,1024]{2,1,0:T(8,128)S(1)} %get-tuple-element.24.field.refs_0_, ...), custom_call_target="tpu_custom_call", output_to_operand_aliasing={{0}: (12, {}), {1}: (13, {}), {2}: (14, {})} | custom-call | tf_op jit(solution)/shard_map/rim/pallas_call | solution.py:582
  20.9 3.1 %collective-permute-start.7 = (f32[4,8,256]{2,1,0:T(8,128)S(1)}, f32[4,8,256]{2,1,0:T(8,128)S(1)}, u32[]{:S(2)}, u32[]{:S(2)}) collective-permute-start(f32[4,8,256]{2,1,0:T(8,128)S(1)} %get-tuple-element.52), channel_id=1, source_target_pairs={{0,3},{1,2},{2,1},{3,0},{4,7},{5,6},{6,5},{7,4},{8,11},{9,10},{10,... | collective-permute-start | bytes 98312 | tf_op jit(solution)/shard_map/ppermute | solution.py:602
  24.0 2.7 %collective-permute-start.8 = (f32[4,8,256]{2,1,0:T(8,128)S(1)}, f32[4,8,256]{2,1,0:T(8,128)S(1)}, u32[]{:S(2)}, u32[]{:S(2)}) collective-permute-start(f32[4,8,256]{2,1,0:T(8,128)S(1)} %get-tuple-element.51), channel_id=1, source_target_pairs={{0,2},{1,3},{2,0},{3,1},{4,6},{5,7},{6,4},{7,5},{8,10},{9,11},{10,... | collective-permute-start | bytes 98312 | tf_op jit(solution)/shard_map/ppermute | solution.py:602
  26.7 0.0 collective-permute-start.9
  26.7 2.6 %collective-permute-done.8 = f32[4,8,256]{2,1,0:T(8,128)S(1)} collective-permute-done((f32[4,8,256]{2,1,0:T(8,128)S(1)}, f32[4,8,256]{2,1,0:T(8,128)S(1)}, u32[]{:S(2)}, u32[]{:S(2)}) %collective-permute-start.8) | collective-permute-done | bytes 32800 | tf_op jit(solution)/shard_map/ppermute | solution.py:602
  29.3 1.3 %collective-permute-done.9 = f32[4,8,256]{2,1,0:T(8,128)S(1)} collective-permute-done((f32[4,8,256]{2,1,0:T(8,128)S(1)}, f32[4,8,256]{2,1,0:T(8,128)S(1)}, u32[]{:S(2)}, u32[]{:S(2)}) %collective-permute-start.9) | collective-permute-done | bytes 32800 | tf_op jit(solution)/shard_map/ppermute | solution.py:602
  30.7 0.6 %pad_maximum_fusion.1 = f32[4,8,256]{2,1,0:T(8,128)} fusion(f32[1,8,256]{2,1,0:T(8,128)S(1)} %fusion.6, f32[3,8,256]{2,1,0:T(8,128)S(1)} %fusion.1), kind=kLoop, calls=%fused_computation.1 | loop fusion | flops 8192 | bytes 65536 | tf_op jit(solution)/shard_map/concatenate | solution.py:615
  (7 shorter events, 0.1 us)
Async XLA Ops:
  2.8 9.0 %collective-permute-start.3 = (f32[64,1024]{1,0:T(8,128)S(1)}, f32[64,1024]{1,0:T(8,128)S(1)}, u32[]{:S(2)}, u32[]{:S(2)}) collective-permute-start(f32[64,1024]{1,0:T(8,128)S(1)} %get-tuple-element.30), channel_id=1, source_target_pairs={{0,4},{8,12},{16,20},{24,28},{4,0},{12,8},{20,16},{28,24},{1,5},{9... | collective-permute-start | bytes 786440 | tf_op jit(solution)/shard_map/ppermute | solution.py:24
  2.9 8.9 %collective-permute-start = (f32[464,128]{1,0:T(8,128)S(1)}, f32[464,128]{1,0:T(8,128)S(1)}, u32[]{:S(2)}, u32[]{:S(2)}) collective-permute-start(f32[464,128]{1,0:T(8,128)S(1)} %get-tuple-element.25), channel_id=1, source_target_pairs={{0,1},{2,3},{1,0},{3,2},{4,5},{6,7},{5,4},{7,6},{8,9},{10,11},{9,8... | collective-permute-start | bytes 712712 | tf_op jit(solution)/shard_map/ppermute | solution.py:24
  4.5 7.3 %collective-permute-start.1 = (f32[464,128]{1,0:T(8,128)S(1)}, f32[464,128]{1,0:T(8,128)S(1)}, u32[]{:S(2)}, u32[]{:S(2)}) collective-permute-start(f32[464,128]{1,0:T(8,128)S(1)} %get-tuple-element.26), channel_id=1, source_target_pairs={{1,2},{2,1},{5,6},{6,5},{9,10},{10,9},{13,14},{14,13},{17,18},{18,... | collective-permute-start | bytes 712712 | tf_op jit(solution)/shard_map/ppermute | solution.py:24
  5.2 6.6 %collective-permute-start.4 = (f32[16,1024]{1,0:T(8,128)S(1)}, f32[16,1024]{1,0:T(8,128)S(1)}, u32[]{:S(2)}, u32[]{:S(2)}) collective-permute-start(f32[16,1024]{1,0:T(8,128)S(1)} %get-tuple-element.31), channel_id=1, source_target_pairs={{4,8},{12,16},{20,24},{8,4},{16,12},{24,20},{5,9},{13,17},{21,25},... | collective-permute-start | bytes 196616 | tf_op jit(solution)/shard_map/ppermute | solution.py:24
  8.3 10.0 %collective-permute-start.2 = (f32[40,1024]{1,0:T(8,128)S(1)}, f32[40,1024]{1,0:T(8,128)S(1)}, u32[]{:S(2)}, u32[]{:S(2)}) collective-permute-start(f32[40,1024]{1,0:T(8,128)S(1)} %get-tuple-element.29), channel_id=1, source_target_pairs={{4,8},{12,16},{20,24},{8,4},{16,12},{24,20},{5,9},{13,17},{21,25},... | collective-permute-start | bytes 491528 | tf_op jit(solution)/shard_map/ppermute | solution.py:24
  12.8 7.0 %collective-permute-start.5 = (f32[24,1024]{1,0:T(8,128)}, f32[24,1024]{1,0:T(8,128)S(1)}, u32[]{:S(2)}, u32[]{:S(2)}) collective-permute-start(f32[24,1024]{1,0:T(8,128)} %get-tuple-element.36), channel_id=1, source_target_pairs={{4,8},{12,16},{20,24},{8,4},{16,12},{24,20},{5,9},{13,17},{21,25},... | collective-permute-start | bytes 294920 | tf_op jit(solution)/shard_map/ppermute | solution.py:24
  16.3 3.6 %collective-permute-start.6 = (f32[24,1024]{1,0:T(8,128)}, f32[24,1024]{1,0:T(8,128)S(1)}, u32[]{:S(2)}, u32[]{:S(2)}) collective-permute-start(f32[24,1024]{1,0:T(8,128)} %get-tuple-element.37), channel_id=1, source_target_pairs={{0,4},{8,12},{16,20},{24,28},{4,0},{12,8},{20,16},{28,24},{1,5},{9... | collective-permute-start | bytes 294920 | tf_op jit(solution)/shard_map/ppermute | solution.py:24
  20.9 5.9 %collective-permute-start.7 = (f32[4,8,256]{2,1,0:T(8,128)S(1)}, f32[4,8,256]{2,1,0:T(8,128)S(1)}, u32[]{:S(2)}, u32[]{:S(2)}) collective-permute-start(f32[4,8,256]{2,1,0:T(8,128)S(1)} %get-tuple-element.52), channel_id=1, source_target_pairs={{0,3},{1,2},{2,1},{3,0},{4,7},{5,6},{6,5},{7,4},{8,11},{9,10},{10,... | collective-permute-start | bytes 98312 | tf_op jit(solution)/shard_map/ppermute | solution.py:602
  24.0 5.3 %collective-permute-start.8 = (f32[4,8,256]{2,1,0:T(8,128)S(1)}, f32[4,8,256]{2,1,0:T(8,128)S(1)}, u32[]{:S(2)}, u32[]{:S(2)}) collective-permute-start(f32[4,8,256]{2,1,0:T(8,128)S(1)} %get-tuple-element.51), channel_id=1, source_target_pairs={{0,2},{1,3},{2,0},{3,1},{4,6},{5,7},{6,4},{7,5},{8,10},{9,11},{10,... | collective-permute-start | bytes 98312 | tf_op jit(solution)/shard_map/ppermute | solution.py:602
  26.7 3.9 %collective-permute-start.9 = (f32[4,8,256]{2,1,0:T(8,128)S(1)}, f32[4,8,256]{2,1,0:T(8,128)S(1)}, u32[]{:S(2)}, u32[]{:S(2)}) collective-permute-start(f32[4,8,256]{2,1,0:T(8,128)S(1)} %get-tuple-element.50), channel_id=1, source_target_pairs={{0,1},{1,0},{2,3},{3,2},{4,5},{5,4},{6,7},{7,6},{8,9},{9,8},{10,11... | collective-permute-start | bytes 98312 | tf_op jit(solution)/shard_map/ppermute | solution.py:602
